TPU v7x, 32 devices: a whole 2x2x4 slice. The times are simulated.
32 devices in a mesh: dcp: 8 (over z, y), rep: 4 (over x, core).
Axes of the slice: x: 2, y: 2, z: 4, core: 2. Of those that a mesh axis runs over, the one named last changes fastest.
Arguments:
- query: bfloat16 [4096, 1024], P(('rep', 'dcp')), parts along dimension 0, may hold values from -6 to 6
- key: bfloat16 [4096, 128], P(('rep', 'dcp')), parts along dimension 0, may hold values from -6 to 6
- value: bfloat16 [4096, 128], P(('rep', 'dcp')), parts along dimension 0, may hold values from -6 to 6
- grad_out: bfloat16 [4096, 1024], P(('rep', 'dcp')), parts along dimension 0, may hold values from -6 to 6
- loader_pos: int32 [4096], P('rep'), parts along dimension 0, may hold values from 0 to 1023, as said below
- doc_lengths: int32 [12], P('rep'), parts along dimension 0, may hold values from 1 to 640, 1024 in all
Outputs:
- attn_out: bfloat16 [4096, 1024], P(('rep', 'dcp')), parts along dimension 0
- dquery: bfloat16 [4096, 1024], P(('rep', 'dcp')), parts along dimension 0
- dkey: bfloat16 [4096, 128], P(('rep', 'dcp')), parts along dimension 0
- dvalue: bfloat16 [4096, 128], P(('rep', 'dcp')), parts along dimension 0
There are 4 independent parts, one for each index of `rep`. A program takes and returns all parts, laid end to end along the dimension named above; each array names one. Nothing has to cross between parts.
Inputs may be any that keep to these rules, and one draw needn't show every extreme that they name: `loader_pos`: a permutation of the 1024 context positions; each aligned block of 128 loader rows holds exactly 128 // 8 positions of every aligned block of 128 context positions.
All inputs are finite; a program needn't handle non-finite values.
Results may differ from a plain program's by a relative error of at most 0.023.
Values may be sent and summed in bfloat16 or wider, within the bound.
No kernel may reach another device: no remote copies, remote signals or barrier semaphores. Data moves between devices by JAX's collectives and lax.ppermute only.
A program may use at most 64 MiB of HBM per device.

v0:
```python
import math

import jax
import jax.numpy as jnp
from jax import lax
from jax.sharding import PartitionSpec as P

SPAN = 5


def passed_along(value, axis, steps):
    count = lax.axis_size(axis)
    initial, last = (max(0, -steps), min(count, count - steps))
    return lax.ppermute(value, axis, [(source, source + steps) for source in range(initial, last)])


def document_of(positions, doc_ends):
    return jnp.sum((positions[:, None] >= doc_ends[None, :]).astype(jnp.int32), axis=1)


def tile_scores(queries, tile_pairs, head_width):
    return jnp.einsum(
        "qhd,kd->hqk", queries, tile_pairs[:, :head_width], preferred_element_type=jnp.float32
    ) * (1.0 / math.sqrt(head_width))


def per_device(query, key, value, grad_out, loader_pos, doc_lengths):
    tok_rows = query.shape[0]
    head_width = key.shape[1]
    head_count = query.shape[1] // head_width
    score_scale = 1.0 / math.sqrt(head_width)
    devices = lax.axis_size("dcp")
    own_index = lax.axis_index("dcp")
    slot_ids = jnp.arange(tok_rows, dtype=jnp.int32)
    total_rows = tok_rows * devices
    own_positions = lax.dynamic_slice_in_dim(loader_pos, own_index * tok_rows, tok_rows, 0)
    send_order = jnp.argsort(own_positions)
    inverse = (
        jnp.zeros((total_rows,), jnp.int32)
        .at[loader_pos]
        .set(jnp.arange(total_rows, dtype=jnp.int32))
    )
    sources = lax.dynamic_slice_in_dim(inverse, own_index * tok_rows, tok_rows, 0) // tok_rows
    arrival = jnp.argsort(sources * tok_rows + slot_ids)
    placing = jnp.argsort(arrival)
    key_pairs = jnp.concatenate([key, value], axis=1)
    grad_in = None
    query_in, pairs_in, grad_in = (
        lax.all_to_all(query[send_order], "dcp", split_axis=0, concat_axis=0, tiled=True),
        lax.all_to_all(key_pairs[send_order], "dcp", split_axis=0, concat_axis=0, tiled=True),
        lax.all_to_all(grad_out[send_order], "dcp", split_axis=0, concat_axis=0, tiled=True),
    )
    queries = query_in[placing].reshape(tok_rows, head_count, head_width)
    own_pairs = pairs_in[placing]
    doc_ends = jnp.cumsum(doc_lengths)
    query_pos = own_index * tok_rows + slot_ids
    query_doc = document_of(query_pos, doc_ends)
    tile_masks = []
    for offset in range(SPAN + 1):
        key_pos = (own_index - offset) * tok_rows + slot_ids
        allowed = (key_pos[None, :] >= 0) & (key_pos[None, :] <= query_pos[:, None])
        tile_masks.append(allowed & (query_doc[:, None] == document_of(key_pos, doc_ends)[None, :]))

    def stats_step(running, tile_pairs, tile_mask):
        row_top, row_total = running
        scores = tile_scores(queries, tile_pairs, head_width)
        new_top = jnp.maximum(
            row_top, jnp.max(jnp.where(tile_mask[None], scores, -jnp.inf), axis=2)
        )
        row_total = row_total * jnp.exp(row_top - new_top) + jnp.sum(
            jnp.where(tile_mask[None], jnp.exp(scores - new_top[:, :, None]), 0.0), axis=2
        )
        return (new_top, row_total)

    start_stats = (
        jnp.full((head_count, tok_rows), -jnp.inf, jnp.float32),
        jnp.zeros((head_count, tok_rows), jnp.float32),
    )
    running = stats_step(start_stats, own_pairs, tile_masks[0])
    tile_list = [own_pairs]
    for offset in range(1, SPAN + 1):
        arrived = passed_along(own_pairs, "dcp", offset)
        tile_list.append(arrived)
        running = stats_step(running, arrived, tile_masks[offset])
    log_total = running[0] + jnp.log(running[1])

    def output_step(out_accum, tile_pairs, tile_mask):
        prob_full = jnp.where(
            tile_mask[None],
            jnp.exp(tile_scores(queries, tile_pairs, head_width) - log_total[:, :, None]),
            0.0,
        )
        return out_accum + jnp.einsum(
            "hqk,kd->qhd",
            prob_full.astype(jnp.bfloat16),
            tile_pairs[:, head_width:],
            preferred_element_type=jnp.float32,
        )

    out_accum = jnp.zeros((tok_rows, head_count, head_width), jnp.float32)
    out_accum = output_step(out_accum, own_pairs, tile_masks[0])
    for offset in range(1, SPAN + 1):
        out_accum = output_step(out_accum, tile_list[offset], tile_masks[offset])
    attended = out_accum.astype(jnp.bfloat16)
    grad_rows = grad_in[placing].reshape(tok_rows, head_count, head_width)
    row_delta = jnp.einsum("qhd,qhd->hq", grad_rows, attended, preferred_element_type=jnp.float32)

    def backward_step(running, tile_pairs, tile_mask):
        scores = tile_scores(queries, tile_pairs, head_width)
        prob_full = jnp.where(tile_mask[None], jnp.exp(scores - log_total[:, :, None]), 0.0)
        prob_low = prob_full.astype(jnp.bfloat16)
        grad_prob = jnp.einsum(
            "qhd,kd->hqk", grad_rows, tile_pairs[:, head_width:], preferred_element_type=jnp.float32
        )
        grad_score = (prob_full * (grad_prob - row_delta[:, :, None])).astype(jnp.bfloat16)
        dq_accum = running[0] + jnp.einsum(
            "hqk,kd->qhd",
            grad_score,
            tile_pairs[:, :head_width],
            preferred_element_type=jnp.float32,
        )
        grad_key = (
            jnp.einsum("hqk,qhd->kd", grad_score, queries, preferred_element_type=jnp.float32)
            * score_scale
        )
        grad_value = jnp.einsum(
            "hqk,qhd->kd", prob_low, grad_rows, preferred_element_type=jnp.float32
        )
        return (dq_accum, jnp.concatenate([grad_key, grad_value], axis=1))

    zero_part = jnp.zeros((tok_rows, 2 * head_width), jnp.float32)
    dq_accum, own_part = backward_step(
        (jnp.zeros((tok_rows, head_count, head_width), jnp.float32), zero_part),
        own_pairs,
        tile_masks[0],
    )
    partials = [own_part]
    for offset in range(1, SPAN + 1):
        dq_accum, tile_part = backward_step(
            (dq_accum, zero_part), tile_list[offset], tile_masks[offset]
        )
        partials.append(tile_part)
    summed = partials[0]
    for offset in range(1, SPAN + 1):
        summed = summed + passed_along(
            partials[offset].astype(jnp.bfloat16), "dcp", -offset
        ).astype(jnp.float32)
    attn_out = attended.reshape(tok_rows, head_count * head_width)
    dquery = (
        (dq_accum * score_scale).astype(jnp.bfloat16).reshape(tok_rows, head_count * head_width)
    )
    return (
        attn_out,
        dquery,
        summed[:, :head_width].astype(jnp.bfloat16),
        summed[:, head_width:].astype(jnp.bfloat16),
    )


def solution(mesh):
    in_specs = (
        P(("rep", "dcp"), None),
        P(("rep", "dcp"), None),
        P(("rep", "dcp"), None),
        P(("rep", "dcp"), None),
        P("rep"),
        P("rep"),
    )
    out_specs = (
        P(("rep", "dcp"), None),
        P(("rep", "dcp"), None),
        P(("rep", "dcp"), None),
        P(("rep", "dcp"), None),
    )
    return jax.shard_map(
        per_device, mesh=mesh, in_specs=in_specs, out_specs=out_specs, check_vma=False
    )
```

profile of v0, /device:TPU:4, one launch (start us, length us, event | category | flops | bytes accessed | tf_op | source)
XLA Modules:
  0.0 101.9 jit_solution(13136290292841170032)
XLA Ops:
  1.5 2.5 %sort.45 = (s32[128]{0:T(128)}, s32[128]{0:T(128)S(1)}) sort(s32[128]{0:T(128)S(1)} %dynamic_slice.6, s32[128]{0:T(128)S(1)} %iota.64), dimensions={0}, to_apply=%region_0.0 | sort | flops 896 | bytes 2048 | tf_op jit(solution)/shard_map/jit(argsort)/sort | solution.py:37
  4.8 1.5 %gather_fusion = bf16[128,256]{1,0:T(8,128)(2,1)} fusion(bf16[128,256]{1,0:T(8,128)(2,1)S(1)} %pad_maximum_fusion, s32[1024]{0:T(1024)S(1)} %pad_clamp_fusion.1), kind=kCustom, calls=%fused_computation | custom fusion | bytes 131584 | tf_op jit(solution)/shard_map/gather | solution.py:50
  6.3 6.3 %all-to-all-start = ((bf16[8,16,256]{2,1,0:T(8,128)(2,1)}), bf16[8,16,256]{2,1,0:T(8,128)(2,1)S(1)}, u32[]{:S(2)}, u32[]{:S(2)}) async-start(bf16[8,16,256]{2,1,0:T(8,128)(2,1)} %bitcast.2), calls=%async_computation | async-start | bytes 131072 | tf_op jit(solution)/shard_map/all_to_all | solution.py:50
  12.6 4.3 %scatter_custom_fusion = s32[1024]{0:T(1024)S(1)} fusion(s32[1024]{0:T(1024)S(1)} %compare_select_fusion, s32[1024]{0:T(1024)S(1)} %iota.65, s32[]{:T(128)} %constant.20.clone.1), kind=kCustom, calls=%fused_computation.160 | custom fusion | bytes 4100 | tf_op jit(solution)/shard_map/scatter | solution.py:41
  17.1 2.5 %sort.46 = (s32[128]{0:T(128)}, s32[128]{0:T(128)S(1)}) sort(s32[128]{0:T(128)S(1)} %iota_add_fusion.6, s32[128]{0:T(128)S(1)} %iota.67), dimensions={0}, to_apply=%region_2.3 | sort | flops 896 | bytes 2048 | tf_op jit(solution)/shard_map/jit(argsort)/sort | solution.py:44
  19.6 2.5 %sort.47 = (s32[128]{0:T(128)}, s32[128]{0:T(128)S(1)}) sort(s32[128]{0:T(128)S(1)} %get-tuple-element.8, s32[128]{0:T(128)S(1)} %iota.68), dimensions={0}, to_apply=%region_3.4 | sort | flops 896 | bytes 2048 | tf_op jit(solution)/shard_map/jit(argsort)/sort | solution.py:45
  22.1 1.6 %gather_fusion.2 = bf16[128,1024]{1,0:T(8,128)(2,1)} fusion(bf16[128,1024]{1,0:T(8,128)(2,1)S(1)} %copy-done, s32[1024]{0:T(1024)S(1)} %pad_clamp_fusion.1), kind=kCustom, calls=%fused_computation.2 | custom fusion | bytes 524800 | tf_op jit(solution)/shard_map/gather | solution.py:49
  23.7 6.1 %all-to-all-start.1 = ((bf16[8,16,1024]{2,1,0:T(8,128)(2,1)}), bf16[8,16,1024]{2,1,0:T(8,128)(2,1)S(1)}, u32[]{:S(2)}, u32[]{:S(2)}) async-start(bf16[8,16,1024]{2,1,0:T(8,128)(2,1)} %bitcast.8), calls=%async_computation.1 | async-start | bytes 524288 | tf_op jit(solution)/shard_map/all_to_all | solution.py:49
  30.7 1.6 %gather_fusion.4 = bf16[128,1024]{1,0:T(8,128)(2,1)} fusion(bf16[128,1024]{1,0:T(8,128)(2,1)S(1)} %copy-done.1, s32[1024]{0:T(1024)S(1)} %pad_clamp_fusion.1), kind=kCustom, calls=%fused_computation.4 | custom fusion | bytes 524800 | tf_op jit(solution)/shard_map/gather | solution.py:51
  33.6 4.3 %collective-permute-start.3 = (bf16[128,256]{1,0:T(8,128)(2,1)S(1)}, bf16[128,256]{1,0:T(8,128)(2,1)S(1)}, u32[]{:S(2)}, u32[]{:S(2)}) collective-permute-start(bf16[128,256]{1,0:T(8,128)(2,1)S(1)} %gather_fusion.1), channel_id=1, source_target_pairs={{0,16},{4,20},{8,24},{12,28},{1,17},{5,21},{9,25},{13,29},{2,18},{... | collective-permute-start | bytes 196616 | tf_op jit(solution)/shard_map/ppermute | solution.py:14
  37.9 1.3 %collective-permute-start.2 = (bf16[128,256]{1,0:T(8,128)(2,1)S(1)}, bf16[128,256]{1,0:T(8,128)(2,1)S(1)}, u32[]{:S(2)}, u32[]{:S(2)}) collective-permute-start(bf16[128,256]{1,0:T(8,128)(2,1)S(1)} %gather_fusion.1), channel_id=1, source_target_pairs={{0,12},{4,16},{8,20},{12,24},{16,28},{1,13},{5,17},{9,21},{13,25},... | collective-permute-start | bytes 196616 | tf_op jit(solution)/shard_map/ppermute | solution.py:14
  39.2 4.0 %collective-permute-start.1 = (bf16[128,256]{1,0:T(8,128)(2,1)S(1)}, bf16[128,256]{1,0:T(8,128)(2,1)S(1)}, u32[]{:S(2)}, u32[]{:S(2)}) collective-permute-start(bf16[128,256]{1,0:T(8,128)(2,1)S(1)} %gather_fusion.1), channel_id=1, source_target_pairs={{0,8},{4,12},{8,16},{12,20},{16,24},{20,28},{1,9},{5,13},{9,17},{1... | collective-permute-start | bytes 196616 | tf_op jit(solution)/shard_map/ppermute | solution.py:14
  43.2 2.7 %collective-permute-start = (bf16[128,256]{1,0:T(8,128)(2,1)S(1)}, bf16[128,256]{1,0:T(8,128)(2,1)S(1)}, u32[]{:S(2)}, u32[]{:S(2)}) collective-permute-start(bf16[128,256]{1,0:T(8,128)(2,1)S(1)} %gather_fusion.1), channel_id=1, source_target_pairs={{0,4},{4,8},{8,12},{12,16},{16,20},{20,24},{24,28},{1,5},{5,9},{9,... | collective-permute-start | bytes 196616 | tf_op jit(solution)/shard_map/ppermute | solution.py:14
  46.0 1.3 %collective-permute-start.4 = (bf16[128,256]{1,0:T(8,128)(2,1)S(1)}, bf16[128,256]{1,0:T(8,128)(2,1)S(1)}, u32[]{:S(2)}, u32[]{:S(2)}) collective-permute-start(bf16[128,256]{1,0:T(8,128)(2,1)S(1)} %gather_fusion.1), channel_id=1, source_target_pairs={{0,20},{4,24},{8,28},{1,21},{5,25},{9,29},{2,22},{6,26},{10,30},{3... | collective-permute-start | bytes 196616 | tf_op jit(solution)/shard_map/ppermute | solution.py:14
  47.3 4.5 %all-to-all-start.2 = ((bf16[8,16,1024]{2,1,0:T(8,128)(2,1)}), bf16[8,16,1024]{2,1,0:T(8,128)(2,1)S(1)}, u32[]{:S(2)}, u32[]{:S(2)}) async-start(bf16[8,16,1024]{2,1,0:T(8,128)(2,1)} %bitcast.30), calls=%async_computation.2 | async-start | bytes 524288 | tf_op jit(solution)/shard_map/all_to_all | solution.py:51
  54.3 3.7 %all-to-all-done.2 = bf16[8,16,1024]{2,1,0:T(8,128)(2,1)S(1)} async-done(((bf16[8,16,1024]{2,1,0:T(8,128)(2,1)}), bf16[8,16,1024]{2,1,0:T(8,128)(2,1)S(1)}, u32[]{:S(2)}, u32[]{:S(2)}) %all-to-all-start.2) | async-done | bytes 262176 | tf_op jit(solution)/shard_map/all_to_all | solution.py:51
  69.1 1.1 %fusion.74 = f32[128,8,128]{2,0,1:T(8,128)} fusion(f32[8,128,128]{1,2,0:T(8,128)S(1)} %get-tuple-element.46, f32[8,128]{1,0:T(8,128)S(1)} %log_add_fusion, pred[128,128]{0,1:T(8,128)(4,1)S(1)} %get-tuple-element.36, bf16[128,256]{1,0:T(8,128)(2,1)S(1)} %copy-done.8), kind=kOutput, calls=%fused_computation.143 | convolution fusion | flops 33947648 | bytes 1101824 | tf_op jit(solution)/shard_map/hqk,kd->qhd/dot_general | solution.py:93
  70.2 2.1 %copy.157 = f32[8,128,128]{1,2,0:T(8,128)} copy(f32[8,128,128]{2,0,1:T(8,128)} %bitcast_convert_fusion) | data formatting | bytes 1048576
  82.3 4.1 %collective-permute-start.5 = (bf16[128,256]{0,1:T(8,128)(2,1)S(1)}, bf16[128,256]{0,1:T(8,128)(2,1)S(1)}, u32[]{:S(2)}, u32[]{:S(2)}) collective-permute-start(bf16[128,256]{0,1:T(8,128)(2,1)S(1)} %pad_maximum_fusion.1), channel_id=1, source_target_pairs={{4,0},{8,4},{12,8},{16,12},{20,16},{24,20},{28,24},{5,1},{9,5},{13... | collective-permute-start | bytes 196616 | tf_op jit(solution)/shard_map/ppermute | solution.py:14
  86.4 1.3 %collective-permute-start.6 = (bf16[128,256]{0,1:T(8,128)(2,1)S(1)}, bf16[128,256]{0,1:T(8,128)(2,1)S(1)}, u32[]{:S(2)}, u32[]{:S(2)}) collective-permute-start(bf16[128,256]{0,1:T(8,128)(2,1)S(1)} %pad_maximum_fusion.2), channel_id=1, source_target_pairs={{8,0},{12,4},{16,8},{20,12},{24,16},{28,20},{9,1},{13,5},{17,9},{2... | collective-permute-start | bytes 196616 | tf_op jit(solution)/shard_map/ppermute | solution.py:14
  87.7 1.3 %collective-permute-start.7 = (bf16[128,256]{0,1:T(8,128)(2,1)S(1)}, bf16[128,256]{0,1:T(8,128)(2,1)S(1)}, u32[]{:S(2)}, u32[]{:S(2)}) collective-permute-start(bf16[128,256]{0,1:T(8,128)(2,1)S(1)} %pad_maximum_fusion.3), channel_id=1, source_target_pairs={{12,0},{16,4},{20,8},{24,12},{28,16},{13,1},{17,5},{21,9},{25,13},... | collective-permute-start | bytes 196616 | tf_op jit(solution)/shard_map/ppermute | solution.py:14
  89.0 1.3 %collective-permute-start.8 = (bf16[128,256]{0,1:T(8,128)(2,1)S(1)}, bf16[128,256]{0,1:T(8,128)(2,1)S(1)}, u32[]{:S(2)}, u32[]{:S(2)}) collective-permute-start(bf16[128,256]{0,1:T(8,128)(2,1)S(1)} %pad_maximum_fusion.4), channel_id=1, source_target_pairs={{16,0},{20,4},{24,8},{28,12},{17,1},{21,5},{25,9},{29,13},{18,2},{... | collective-permute-start | bytes 196616 | tf_op jit(solution)/shard_map/ppermute | solution.py:14
  90.4 1.3 %collective-permute-start.9 = (bf16[128,256]{0,1:T(8,128)(2,1)S(1)}, bf16[128,256]{0,1:T(8,128)(2,1)S(1)}, u32[]{:S(2)}, u32[]{:S(2)}) collective-permute-start(bf16[128,256]{0,1:T(8,128)(2,1)S(1)} %pad_maximum_fusion.5), channel_id=1, source_target_pairs={{20,0},{24,4},{28,8},{21,1},{25,5},{29,9},{22,2},{26,6},{30,10},{2... | collective-permute-start | bytes 196616 | tf_op jit(solution)/shard_map/ppermute | solution.py:14
  96.4 4.0 %collective-permute-done.9 = bf16[128,256]{0,1:T(8,128)(2,1)S(1)} collective-permute-done((bf16[128,256]{0,1:T(8,128)(2,1)S(1)}, bf16[128,256]{0,1:T(8,128)(2,1)S(1)}, u32[]{:S(2)}, u32[]{:S(2)}) %collective-permute-start.9) | collective-permute-done | bytes 65568 | tf_op jit(solution)/shard_map/ppermute | solution.py:14
  (147 shorter events, 33.4 us)
Async XLA Ops:
  0.6 21.5 %copy-start = (bf16[128,1024]{1,0:T(8,128)(2,1)S(1)}, bf16[128,1024]{1,0:T(8,128)(2,1)}, u32[]{:S(2)}) copy-start(bf16[128,1024]{1,0:T(8,128)(2,1)} %param.6) | copy-start | bytes 786436
  6.3 17.5 %all-to-all-start = ((bf16[8,16,256]{2,1,0:T(8,128)(2,1)}), bf16[8,16,256]{2,1,0:T(8,128)(2,1)S(1)}, u32[]{:S(2)}, u32[]{:S(2)}) async-start(bf16[8,16,256]{2,1,0:T(8,128)(2,1)} %bitcast.2), calls=%async_computation | async-start | bytes 131072 | tf_op jit(solution)/shard_map/all_to_all | solution.py:50
  23.7 7.0 %copy-start.1 = (bf16[128,1024]{1,0:T(8,128)(2,1)S(1)}, bf16[128,1024]{1,0:T(8,128)(2,1)}, u32[]{:S(2)}) copy-start(bf16[128,1024]{1,0:T(8,128)(2,1)} %param.9) | copy-start | bytes 786436
  23.7 23.5 %all-to-all-start.1 = ((bf16[8,16,1024]{2,1,0:T(8,128)(2,1)}), bf16[8,16,1024]{2,1,0:T(8,128)(2,1)S(1)}, u32[]{:S(2)}, u32[]{:S(2)}) async-start(bf16[8,16,1024]{2,1,0:T(8,128)(2,1)} %bitcast.8), calls=%async_computation.1 | async-start | bytes 524288 | tf_op jit(solution)/shard_map/all_to_all | solution.py:49
  33.6 19.2 %copy-start.7 = (bf16[128,256]{1,0:T(8,128)(2,1)}, bf16[128,256]{1,0:T(8,128)(2,1)S(1)}, u32[]{:S(2)}) copy-start(bf16[128,256]{1,0:T(8,128)(2,1)S(1)} %gather_fusion.1) | copy-start | bytes 196612
  33.6 20.1 %collective-permute-start.3 = (bf16[128,256]{1,0:T(8,128)(2,1)S(1)}, bf16[128,256]{1,0:T(8,128)(2,1)S(1)}, u32[]{:S(2)}, u32[]{:S(2)}) collective-permute-start(bf16[128,256]{1,0:T(8,128)(2,1)S(1)} %gather_fusion.1), channel_id=1, source_target_pairs={{0,16},{4,20},{8,24},{12,28},{1,17},{5,21},{9,25},{13,29},{2,18},{... | collective-permute-start | bytes 196616 | tf_op jit(solution)/shard_map/ppermute | solution.py:14
  37.9 21.0 %collective-permute-start.2 = (bf16[128,256]{1,0:T(8,128)(2,1)S(1)}, bf16[128,256]{1,0:T(8,128)(2,1)S(1)}, u32[]{:S(2)}, u32[]{:S(2)}) collective-permute-start(bf16[128,256]{1,0:T(8,128)(2,1)S(1)} %gather_fusion.1), channel_id=1, source_target_pairs={{0,12},{4,16},{8,20},{12,24},{16,28},{1,13},{5,17},{9,21},{13,25},... | collective-permute-start | bytes 196616 | tf_op jit(solution)/shard_map/ppermute | solution.py:14
  39.2 21.2 %collective-permute-start.1 = (bf16[128,256]{1,0:T(8,128)(2,1)S(1)}, bf16[128,256]{1,0:T(8,128)(2,1)S(1)}, u32[]{:S(2)}, u32[]{:S(2)}) collective-permute-start(bf16[128,256]{1,0:T(8,128)(2,1)S(1)} %gather_fusion.1), channel_id=1, source_target_pairs={{0,8},{4,12},{8,16},{12,20},{16,24},{20,28},{1,9},{5,13},{9,17},{1... | collective-permute-start | bytes 196616 | tf_op jit(solution)/shard_map/ppermute | solution.py:14
  43.2 18.6 %collective-permute-start = (bf16[128,256]{1,0:T(8,128)(2,1)S(1)}, bf16[128,256]{1,0:T(8,128)(2,1)S(1)}, u32[]{:S(2)}, u32[]{:S(2)}) collective-permute-start(bf16[128,256]{1,0:T(8,128)(2,1)S(1)} %gather_fusion.1), channel_id=1, source_target_pairs={{0,4},{4,8},{8,12},{12,16},{16,20},{20,24},{24,28},{1,5},{5,9},{9,... | collective-permute-start | bytes 196616 | tf_op jit(solution)/shard_map/ppermute | solution.py:14
  46.0 7.1 %collective-permute-start.4 = (bf16[128,256]{1,0:T(8,128)(2,1)S(1)}, bf16[128,256]{1,0:T(8,128)(2,1)S(1)}, u32[]{:S(2)}, u32[]{:S(2)}) collective-permute-start(bf16[128,256]{1,0:T(8,128)(2,1)S(1)} %gather_fusion.1), channel_id=1, source_target_pairs={{0,20},{4,24},{8,28},{1,21},{5,25},{9,29},{2,22},{6,26},{10,30},{3... | collective-permute-start | bytes 196616 | tf_op jit(solution)/shard_map/ppermute | solution.py:14
  47.3 10.8 %all-to-all-start.2 = ((bf16[8,16,1024]{2,1,0:T(8,128)(2,1)}), bf16[8,16,1024]{2,1,0:T(8,128)(2,1)S(1)}, u32[]{:S(2)}, u32[]{:S(2)}) async-start(bf16[8,16,1024]{2,1,0:T(8,128)(2,1)} %bitcast.30), calls=%async_computation.2 | async-start | bytes 524288 | tf_op jit(solution)/shard_map/all_to_all | solution.py:51
  63.5 1.0 %copy-start.2 = (f32[8,128,128]{1,2,0:T(8,128)S(1)}, f32[8,128,128]{1,2,0:T(8,128)}, u32[]{:S(2)}) copy-start(f32[8,128,128]{1,2,0:T(8,128)} %get-tuple-element.44) | copy-start | bytes 1572868
  72.2 1.0 %copy-start.13 = (bf16[128,256]{1,0:T(8,128)(2,1)S(1)}, bf16[128,256]{1,0:T(8,128)(2,1)}, u32[]{:S(2)}) copy-start(bf16[128,256]{1,0:T(8,128)(2,1)} %copy-done.12) | copy-start | bytes 196612
  75.2 1.2 %copy-start.5 = (f32[8,128,128]{1,2,0:T(8,128)S(1)}, f32[8,128,128]{1,2,0:T(8,128)}, u32[]{:S(2)}) copy-start(f32[8,128,128]{1,2,0:T(8,128)} %copy.157) | copy-start | bytes 1572868
  75.2 1.2 %copy-start.11 = (bf16[128,256]{1,0:T(8,128)(2,1)S(1)}, bf16[128,256]{1,0:T(8,128)(2,1)}, u32[]{:S(2)}) copy-start(bf16[128,256]{1,0:T(8,128)(2,1)} %copy-done.10) | copy-start | bytes 196612
  82.3 4.1 %copy-start.23 = (bf16[128,128]{0,1:T(8,128)(2,1)S(1)}, bf16[128,128]{0,1:T(8,128)(2,1)}, u32[]{:S(2)}) copy-start(bf16[128,128]{0,1:T(8,128)(2,1)} %fusion.40) | copy-start | bytes 98308
  82.3 5.4 %copy-start.22 = (bf16[128,128]{0,1:T(8,128)(2,1)S(1)}, bf16[128,128]{0,1:T(8,128)(2,1)}, u32[]{:S(2)}) copy-start(bf16[128,128]{0,1:T(8,128)(2,1)} %fusion.41) | copy-start | bytes 98308
  82.3 13.3 %collective-permute-start.5 = (bf16[128,256]{0,1:T(8,128)(2,1)S(1)}, bf16[128,256]{0,1:T(8,128)(2,1)S(1)}, u32[]{:S(2)}, u32[]{:S(2)}) collective-permute-start(bf16[128,256]{0,1:T(8,128)(2,1)S(1)} %pad_maximum_fusion.1), channel_id=1, source_target_pairs={{4,0},{8,4},{12,8},{16,12},{20,16},{24,20},{28,24},{5,1},{9,5},{13... | collective-permute-start | bytes 196616 | tf_op jit(solution)/shard_map/ppermute | solution.py:14
  86.4 2.6 %copy-start.21 = (bf16[128,128]{0,1:T(8,128)(2,1)S(1)}, bf16[128,128]{0,1:T(8,128)(2,1)}, u32[]{:S(2)}) copy-start(bf16[128,128]{0,1:T(8,128)(2,1)} %fusion.42) | copy-start | bytes 98308
  86.4 9.2 %collective-permute-start.6 = (bf16[128,256]{0,1:T(8,128)(2,1)S(1)}, bf16[128,256]{0,1:T(8,128)(2,1)S(1)}, u32[]{:S(2)}, u32[]{:S(2)}) collective-permute-start(bf16[128,256]{0,1:T(8,128)(2,1)S(1)} %pad_maximum_fusion.2), channel_id=1, source_target_pairs={{8,0},{12,4},{16,8},{20,12},{24,16},{28,20},{9,1},{13,5},{17,9},{2... | collective-permute-start | bytes 196616 | tf_op jit(solution)/shard_map/ppermute | solution.py:14
  87.7 8.7 %collective-permute-start.7 = (bf16[128,256]{0,1:T(8,128)(2,1)S(1)}, bf16[128,256]{0,1:T(8,128)(2,1)S(1)}, u32[]{:S(2)}, u32[]{:S(2)}) collective-permute-start(bf16[128,256]{0,1:T(8,128)(2,1)S(1)} %pad_maximum_fusion.3), channel_id=1, source_target_pairs={{12,0},{16,4},{20,8},{24,12},{28,16},{13,1},{17,5},{21,9},{25,13},... | collective-permute-start | bytes 196616 | tf_op jit(solution)/shard_map/ppermute | solution.py:14
  89.0 7.3 %collective-permute-start.8 = (bf16[128,256]{0,1:T(8,128)(2,1)S(1)}, bf16[128,256]{0,1:T(8,128)(2,1)S(1)}, u32[]{:S(2)}, u32[]{:S(2)}) collective-permute-start(bf16[128,256]{0,1:T(8,128)(2,1)S(1)} %pad_maximum_fusion.4), channel_id=1, source_target_pairs={{16,0},{20,4},{24,8},{28,12},{17,1},{21,5},{25,9},{29,13},{18,2},{... | collective-permute-start | bytes 196616 | tf_op jit(solution)/shard_map/ppermute | solution.py:14
  90.4 10.0 %collective-permute-start.9 = (bf16[128,256]{0,1:T(8,128)(2,1)S(1)}, bf16[128,256]{0,1:T(8,128)(2,1)S(1)}, u32[]{:S(2)}, u32[]{:S(2)}) collective-permute-start(bf16[128,256]{0,1:T(8,128)(2,1)S(1)} %pad_maximum_fusion.5), channel_id=1, source_target_pairs={{20,0},{24,4},{28,8},{21,1},{25,5},{29,9},{22,2},{26,6},{30,10},{2... | collective-permute-start | bytes 196616 | tf_op jit(solution)/shard_map/ppermute | solution.py:14
  94.8 5.6 %copy-start.18 = (f32[128,128]{0,1:T(8,128)S(1)}, f32[128,128]{0,1:T(8,128)}, u32[]{:S(2)}) copy-start(f32[128,128]{0,1:T(8,128)} %fusion.38) | copy-start | bytes 196612
  (16 other events, 13.3 us)
where the time goes:
time: 103 us; the launch traced here: 102 us
  starting transfers between devices  39.8 us (39%)
  local copies, waits for them, and re-layouts  25.9 us (25%)
  matrix products  15.6 us (15%)
  other arithmetic  10.8 us (10%)
  waiting for transfers between devices  8.48 us (8%)
  between operations  1.3 us (1%)
    ppermute x10, starting transfers between devices, passed_along(): lax.ppermute(value, axis, [(source, source + steps) for source in range(i...  22.8 us
    unnamed x60, local copies, waits for them, and re-layouts  14 us
    all_to_all x1, starting transfers between devices, per_device(): lax.all_to_all(key_pairs[send_order], 'dcp', split_axis=0, concat_axis=0,...  6.34 us
    all_to_all x1, starting transfers between devices, per_device(): lax.all_to_all(query[send_order], 'dcp', split_axis=0, concat_axis=0, til...  6.14 us
    ppermute x10, waiting for transfers between devices, passed_along(): lax.ppermute(value, axis, [(source, source + steps) for source in range(i...  4.78 us
    all_to_all x1, starting transfers between devices, per_device(): lax.all_to_all(grad_out[send_order], 'dcp', split_axis=0, concat_axis=0,...  4.51 us
    scatter x1, local copies, waits for them, and re-layouts, per_device(): inverse = jnp.zeros((total_rows,), jnp.int32).at[loader_pos].set(jnp.aran...  4.31 us
    dot_general x6, matrix products, backward_step(): jnp.einsum('hqk,qhd->kd', prob_low, grad_rows, preferred_element_type=jnp...  3.92 us
  transfers between devices with their start and end apart: 13, of which 3 were waited for; matrix products, arithmetic and copies ran while one was open for 22% of the time, Pallas kernels for 0%

commit v1 on v0

v1 whole, which is shorter than its diff:
```python
import functools
import math

import jax
import jax.numpy as jnp
from jax import lax
from jax.experimental import pallas as pl
from jax.experimental.pallas import tpu as pltpu
from jax.sharding import PartitionSpec as P

SPAN = 5
LANES = 128
NEG = -1e30
F32 = jnp.float32
BF16 = jnp.bfloat16


def dot(a, b, dims):
    return lax.dot_general(a, b, (dims, ((), ())), preferred_element_type=F32)


def pack_kernel(per_peer, pos_ref, q_ref, k_ref, v_ref, g_ref, out_ref):
    tok, width = q_ref.shape
    head = k_ref.shape[1]
    me = lax.axis_index("dcp")
    pos_row = pos_ref[pl.ds(me, 1), :]
    pos_col = jnp.transpose(jnp.broadcast_to(pos_row, (tok, tok)))
    smaller = (pos_col < pos_row).astype(jnp.int32)
    rank = jnp.sum(smaller, axis=0, keepdims=True)
    slot = jnp.broadcast_to((pos_row % tok).astype(F32), (tok, tok))
    want = lax.broadcasted_iota(jnp.int32, (tok, tok), 0)
    lane = lax.broadcasted_iota(jnp.int32, (tok, LANES), 1)
    perm = (rank == want).astype(BF16)
    out_ref[:, :width] = dot(perm, q_ref[...], ((1,), (0,))).astype(BF16)
    out_ref[:, width : 2 * width] = dot(perm, g_ref[...], ((1,), (0,))).astype(BF16)
    slots = jnp.zeros((tok, LANES), F32)
    for block in range(SPAN + 1):
        chosen = rank == want + (block - SPAN) * per_peer
        perm = chosen.astype(BF16)
        first = 2 * width + 2 * head * block
        out_ref[:, first : first + head] = dot(perm, k_ref[...], ((1,), (0,))).astype(BF16)
        out_ref[:, first + head : first + 2 * head] = dot(perm, v_ref[...], ((1,), (0,))).astype(BF16)
        column = jnp.sum(jnp.where(chosen, slot, 0.0), axis=1, keepdims=True)
        slots = jnp.where(lane == block, column, slots)
    first = 2 * width + 2 * head * (SPAN + 1)
    out_ref[:, first : first + LANES] = slots.astype(BF16)


def attend_kernel(width, head, len_ref, in_ref, attn_ref, dq_ref, own_ref, *part_refs):
    tok = in_ref.shape[0]
    heads = width // head
    me = lax.axis_index("dcp")
    scale = 1.0 / math.sqrt(head)
    factor = scale * math.log2(math.e)
    base = 2 * width
    slots = in_ref[:, base + 2 * head * (SPAN + 1) :].astype(F32)
    target = lax.broadcasted_iota(jnp.int32, (tok, tok), 1).astype(F32)
    keys, values = [], []
    place = None
    for block in range(SPAN + 1):
        place = (slots[:, block : block + 1] == target).astype(BF16)
        first = base + 2 * head * block
        both = dot(place, in_ref[:, first : first + 2 * head], ((0,), (0,))).astype(BF16)
        keys.append(both[:, :head])
        values.append(both[:, head:])
    key = jnp.concatenate(keys, axis=0)
    value = jnp.concatenate(values, axis=0)
    queries = dot(place, in_ref[:, :width], ((0,), (0,))).astype(BF16)
    grads = dot(place, in_ref[:, width:base], ((0,), (0,))).astype(BF16)

    pairs = 2
    cols = pairs * tok
    window = (SPAN + 1) * tok
    lane = lax.broadcasted_iota(jnp.int32, (1, cols), 1)
    q_pos = me * tok + lane % tok
    q_start = jnp.zeros((1, cols), jnp.int32)
    end = jnp.int32(0)
    for doc in range(len_ref.shape[0]):
        end = end + len_ref[doc]
        q_start = jnp.where(q_pos >= end, end, q_start)
    k_pos = (me - SPAN) * tok + lax.broadcasted_iota(jnp.int32, (window, cols), 0)
    allowed = (k_pos >= q_start) & (k_pos <= q_pos)

    key_grad = jnp.zeros((window, head), F32)
    value_grad = jnp.zeros((window, head), F32)
    for first in range(0, heads, pairs):
        spans = [slice(h * head, (h + 1) * head) for h in range(first, first + pairs)]
        q_two = jnp.concatenate([queries[:, s] for s in spans], axis=0)
        g_two = jnp.concatenate([grads[:, s] for s in spans], axis=0)
        scores = jnp.where(allowed, dot(key, q_two, ((1,), (1,))), NEG)
        top = jnp.max(scores, axis=0, keepdims=True)
        weights = jnp.exp2((scores - top) * factor)
        inverse = 1.0 / jnp.sum(weights, axis=0, keepdims=True)
        prob = weights * inverse
        prob_low = prob.astype(BF16)
        grad_prob = dot(value, g_two, ((1,), (1,)))
        delta = jnp.sum(prob * grad_prob, axis=0, keepdims=True)
        grad_score = (prob * (grad_prob - delta)).astype(BF16)
        value_grad += dot(prob_low, g_two, ((1,), (0,)))
        key_grad += dot(grad_score, q_two, ((1,), (0,)))
        out_t = dot(value, prob_low, ((0,), (0,)))
        dq_t = dot(key, grad_score, ((0,), (0,))) * scale
        for i, s in enumerate(spans):
            attn_ref[:, s] = jnp.transpose(out_t[:, i * tok : (i + 1) * tok]).astype(BF16)
            dq_ref[:, s] = jnp.transpose(dq_t[:, i * tok : (i + 1) * tok]).astype(BF16)
    key_grad = key_grad * scale
    own_ref[:, :head] = key_grad[SPAN * tok :, :]
    own_ref[:, head:] = value_grad[SPAN * tok :, :]
    for offset in range(1, SPAN + 1):
        rows = slice((SPAN - offset) * tok, (SPAN - offset + 1) * tok)
        part_refs[offset - 1][:, :head] = key_grad[rows, :].astype(BF16)
        part_refs[offset - 1][:, head:] = value_grad[rows, :].astype(BF16)


def per_device(query, key, value, grad_out, loader_pos, doc_lengths):
    tok, width = query.shape
    head = key.shape[1]
    devices = lax.axis_size("dcp")
    per_peer = tok // devices
    vmem = pl.BlockSpec(memory_space=pltpu.VMEM)
    smem = pl.BlockSpec(memory_space=pltpu.SMEM)
    params = pltpu.CompilerParams(vmem_limit_bytes=48 << 20)
    total = 2 * width + 2 * head * (SPAN + 1) + LANES
    packed = pl.pallas_call(
        functools.partial(pack_kernel, per_peer),
        out_shape=jax.ShapeDtypeStruct((tok, total), BF16),
        in_specs=[vmem] * 5,
        out_specs=vmem,
        compiler_params=params,
        name="pack",
    )(loader_pos.reshape(devices, tok), query, key, value, grad_out)
    arrived = lax.all_to_all(packed, "dcp", split_axis=0, concat_axis=0, tiled=True)
    wide = jax.ShapeDtypeStruct((tok, width), BF16)
    part = jax.ShapeDtypeStruct((tok, 2 * head), BF16)
    attn_out, dquery, summed, *parts = pl.pallas_call(
        functools.partial(attend_kernel, width, head),
        out_shape=[wide, wide, jax.ShapeDtypeStruct((tok, 2 * head), F32)] + [part] * SPAN,
        in_specs=[smem, vmem],
        out_specs=[vmem] * (3 + SPAN),
        compiler_params=params,
        name="attend",
    )(doc_lengths, arrived)
    for offset in range(1, SPAN + 1):
        pairs = [(source, source - offset) for source in range(offset, devices)]
        summed = summed + lax.ppermute(parts[offset - 1], "dcp", pairs).astype(F32)
    return attn_out, dquery, summed[:, :head].astype(BF16), summed[:, head:].astype(BF16)


def solution(mesh):
    rows = P(("rep", "dcp"), None)
    return jax.shard_map(
        per_device,
        mesh=mesh,
        in_specs=(rows, rows, rows, rows, P("rep"), P("rep")),
        out_specs=(rows, rows, rows, rows),
        check_vma=False,
    )
```

time: 103 us -> 61.7 us (0.60)
  the two profiles are of different devices: /device:TPU:4 before, /device:TPU:0 now
where the time goes in v1:
time: 61.7 us; the launch traced here: 61.2 us
  blocking collectives  31 us (50%)
  waiting for transfers between devices  11.4 us (18%)
  starting transfers between devices  6.45 us (10%)
  Pallas kernels  6.22 us (10%)
  local copies, waits for them, and re-layouts  5.38 us (9%)
  between operations  0.71 us (1%)
    all_to_all x1, blocking collectives, per_device(): lax.all_to_all(packed, 'dcp', split_axis=0, concat_axis=0, tiled=True)  31 us
    ppermute x5, waiting for transfers between devices, per_device(): summed = summed + lax.ppermute(parts[offset - 1], 'dcp', pairs).astype(F32)  11.4 us
    ppermute x5, starting transfers between devices, per_device(): summed = summed + lax.ppermute(parts[offset - 1], 'dcp', pairs).astype(F32)  6.45 us
    pallas_call x1, Pallas kernels, per_device(): pl.pallas_call(functools.partial(attend_kernel, width, head), out_shape=[...  5.68 us
    unnamed x12, local copies, waits for them, and re-layouts  4.75 us
  transfers between devices with their start and end apart: 5, of which 4 were waited for; matrix products, arithmetic and copies ran while one was open for 0% of the time, Pallas kernels for 0%

profile of v1, /device:TPU:0, one launch (start us, length us, event | category | flops | bytes accessed | tf_op | source)
XLA Modules:
  0.0 61.2 jit_solution(6313121313877164906)
XLA Ops:
  0.6 0.0 copy-start
  0.6 0.9 %copy-done = bf16[128,1024]{1,0:T(8,128)(2,1)S(1)} copy-done((bf16[128,1024]{1,0:T(8,128)(2,1)S(1)}, bf16[128,1024]{1,0:T(8,128)(2,1)}, u32[]{:S(2)}) %copy-start) | copy-done | bytes 262168
  1.6 0.0 copy-start.1
  1.6 0.9 %copy-done.1 = bf16[128,1024]{1,0:T(8,128)(2,1)S(1)} copy-done((bf16[128,1024]{1,0:T(8,128)(2,1)S(1)}, bf16[128,1024]{1,0:T(8,128)(2,1)}, u32[]{:S(2)}) %copy-start.1) | copy-done | bytes 262168
  2.5 0.0 copy-start.2
  2.5 0.8 %copy-done.2 = bf16[128,128]{1,0:T(8,128)(2,1)S(1)} copy-done((bf16[128,128]{1,0:T(8,128)(2,1)S(1)}, bf16[128,128]{1,0:T(8,128)(2,1)}, u32[]{:S(2)}) %copy-start.2) | copy-done | bytes 32792
  3.3 0.8 %copy-done.3 = bf16[128,128]{1,0:T(8,128)(2,1)S(1)} copy-done((bf16[128,128]{1,0:T(8,128)(2,1)S(1)}, bf16[128,128]{1,0:T(8,128)(2,1)}, u32[]{:S(2)}) %copy-start.3) | copy-done | bytes 32792
  4.1 0.7 %copy-done.4 = s32[1024]{0:T(1024)S(1)} copy-done((s32[1024]{0:T(1024)S(1)}, s32[1024]{0:T(1024)}, u32[]{:S(2)}) %copy-start.4) | copy-done | bytes 4120
  4.7 0.5 pack.1
  5.3 31.0 %all_to_all.11 = bf16[8,16,3712]{2,1,0:T(8,128)(2,1)S(1)} all-to-all(bf16[8,16,3712]{2,1,0:T(8,128)(2,1)S(1)} %bitcast.4), channel_id=1, replica_groups=mesh['dcp'=8,'rep'=4] {'dcp'}, dimensions={0} | all-to-all | bytes 1900544 | tf_op jit(solution)/shard_map/all_to_all | solution.py:132
  36.3 0.7 %copy-done.5 = s32[3]{0:T(128)S(1)} copy-done((s32[3]{0:T(128)S(1)}, s32[3]{0:T(128)}, u32[]{:S(2)}) %copy-start.5) | copy-done | bytes 36
  36.9 5.7 %attend.1 = (bf16[128,1024]{1,0:T(8,128)(2,1)}, bf16[128,1024]{1,0:T(8,128)(2,1)}, f32[128,256]{1,0:T(8,128)S(1)}, bf16[128,256]{1,0:T(8,128)(2,1)S(1)}, bf16[12...) custom-call(s32[3]{0:T(128)S(1)} %copy-done.5, ...), custom_call_target="tpu_custom_call" | custom-call | tf_op jit(solution)/shard_map/attend/pallas_call | solution.py:135
  42.6 1.3 %collective-permute-start = (bf16[128,256]{1,0:T(8,128)(2,1)S(1)}, bf16[128,256]{1,0:T(8,128)(2,1)S(1)}, u32[]{:S(2)}, u32[]{:S(2)}) collective-permute-start(bf16[128,256]{1,0:T(8,128)(2,1)S(1)} %get-tuple-element.15), channel_id=1, source_target_pairs={{4,0},{8,4},{12,8},{16,12},{20,16},{24,20},{28,24},{5,1},{9,5},{13... | collective-permute-start | bytes 196616 | tf_op jit(solution)/shard_map/ppermute | solution.py:145
  43.9 1.3 %collective-permute-start.1 = (bf16[128,256]{1,0:T(8,128)(2,1)S(1)}, bf16[128,256]{1,0:T(8,128)(2,1)S(1)}, u32[]{:S(2)}, u32[]{:S(2)}) collective-permute-start(bf16[128,256]{1,0:T(8,128)(2,1)S(1)} %get-tuple-element.16), channel_id=1, source_target_pairs={{8,0},{12,4},{16,8},{20,12},{24,16},{28,20},{9,1},{13,5},{17,9},{2... | collective-permute-start | bytes 196616 | tf_op jit(solution)/shard_map/ppermute | solution.py:145
  45.2 1.3 %collective-permute-start.2 = (bf16[128,256]{1,0:T(8,128)(2,1)S(1)}, bf16[128,256]{1,0:T(8,128)(2,1)S(1)}, u32[]{:S(2)}, u32[]{:S(2)}) collective-permute-start(bf16[128,256]{1,0:T(8,128)(2,1)S(1)} %get-tuple-element.17), channel_id=1, source_target_pairs={{12,0},{16,4},{20,8},{24,12},{28,16},{13,1},{17,5},{21,9},{25,13},... | collective-permute-start | bytes 196616 | tf_op jit(solution)/shard_map/ppermute | solution.py:145
  46.5 1.3 %collective-permute-start.3 = (bf16[128,256]{1,0:T(8,128)(2,1)S(1)}, bf16[128,256]{1,0:T(8,128)(2,1)S(1)}, u32[]{:S(2)}, u32[]{:S(2)}) collective-permute-start(bf16[128,256]{1,0:T(8,128)(2,1)S(1)} %get-tuple-element.18), channel_id=1, source_target_pairs={{16,0},{20,4},{24,8},{28,12},{17,1},{21,5},{25,9},{29,13},{18,2},{... | collective-permute-start | bytes 196616 | tf_op jit(solution)/shard_map/ppermute | solution.py:145
  47.8 1.3 %collective-permute-start.4 = (bf16[128,256]{1,0:T(8,128)(2,1)S(1)}, bf16[128,256]{1,0:T(8,128)(2,1)S(1)}, u32[]{:S(2)}, u32[]{:S(2)}) collective-permute-start(bf16[128,256]{1,0:T(8,128)(2,1)S(1)} %get-tuple-element.19), channel_id=1, source_target_pairs={{20,0},{24,4},{28,8},{21,1},{25,5},{29,9},{22,2},{26,6},{30,10},{2... | collective-permute-start | bytes 196616 | tf_op jit(solution)/shard_map/ppermute | solution.py:145
  49.1 0.0 collective-permute-done
  49.1 2.2 %collective-permute-done.1 = bf16[128,256]{1,0:T(8,128)(2,1)S(1)} collective-permute-done((bf16[128,256]{1,0:T(8,128)(2,1)S(1)}, bf16[128,256]{1,0:T(8,128)(2,1)S(1)}, u32[]{:S(2)}, u32[]{:S(2)}) %collective-permute-start.1) | collective-permute-done | bytes 65568 | tf_op jit(solution)/shard_map/ppermute | solution.py:145
  51.3 2.7 %collective-permute-done.2 = bf16[128,256]{1,0:T(8,128)(2,1)S(1)} collective-permute-done((bf16[128,256]{1,0:T(8,128)(2,1)S(1)}, bf16[128,256]{1,0:T(8,128)(2,1)S(1)}, u32[]{:S(2)}, u32[]{:S(2)}) %collective-permute-start.2) | collective-permute-done | bytes 65568 | tf_op jit(solution)/shard_map/ppermute | solution.py:145
  54.1 5.4 %collective-permute-done.3 = bf16[128,256]{1,0:T(8,128)(2,1)S(1)} collective-permute-done((bf16[128,256]{1,0:T(8,128)(2,1)S(1)}, bf16[128,256]{1,0:T(8,128)(2,1)S(1)}, u32[]{:S(2)}, u32[]{:S(2)}) %collective-permute-start.3) | collective-permute-done | bytes 65568 | tf_op jit(solution)/shard_map/ppermute | solution.py:145
  59.5 1.0 %collective-permute-done.4 = bf16[128,256]{1,0:T(8,128)(2,1)S(1)} collective-permute-done((bf16[128,256]{1,0:T(8,128)(2,1)S(1)}, bf16[128,256]{1,0:T(8,128)(2,1)S(1)}, u32[]{:S(2)}, u32[]{:S(2)}) %collective-permute-start.4) | collective-permute-done | bytes 65568 | tf_op jit(solution)/shard_map/ppermute | solution.py:145
  60.5 0.1 add_convert_fusion
  60.6 0.6 %fusion = (bf16[128,128]{1,0:T(8,128)(2,1)}, bf16[128,128]{1,0:T(8,128)(2,1)}) fusion(bf16[128,256]{1,0:T(8,128)(2,1)S(1)} %add_convert_fusion), kind=kLoop, calls=%fused_computation.1 | loop fusion | bytes 131072 | tf_op jit(solution)/shard_map/slice | solution.py:146
  (3 shorter events, 0.0 us)
Async XLA Ops:
  0.6 1.0 %copy-start = (bf16[128,1024]{1,0:T(8,128)(2,1)S(1)}, bf16[128,1024]{1,0:T(8,128)(2,1)}, u32[]{:S(2)}) copy-start(bf16[128,1024]{1,0:T(8,128)(2,1)} %q_ref.1) | copy-start | bytes 786436
  1.6 0.9 %copy-start.1 = (bf16[128,1024]{1,0:T(8,128)(2,1)S(1)}, bf16[128,1024]{1,0:T(8,128)(2,1)}, u32[]{:S(2)}) copy-start(bf16[128,1024]{1,0:T(8,128)(2,1)} %g_ref.1) | copy-start | bytes 786436
  2.5 0.8 %copy-start.2 = (bf16[128,128]{1,0:T(8,128)(2,1)S(1)}, bf16[128,128]{1,0:T(8,128)(2,1)}, u32[]{:S(2)}) copy-start(bf16[128,128]{1,0:T(8,128)(2,1)} %k_ref.1) | copy-start | bytes 98308
  3.3 0.8 %copy-start.3 = (bf16[128,128]{1,0:T(8,128)(2,1)S(1)}, bf16[128,128]{1,0:T(8,128)(2,1)}, u32[]{:S(2)}) copy-start(bf16[128,128]{1,0:T(8,128)(2,1)} %v_ref.1) | copy-start | bytes 98308
  4.1 0.7 %copy-start.4 = (s32[1024]{0:T(1024)S(1)}, s32[1024]{0:T(1024)}, u32[]{:S(2)}) copy-start(s32[1024]{0:T(1024)} %param.10) | copy-start | bytes 12292
  36.3 0.7 %copy-start.5 = (s32[3]{0:T(128)S(1)}, s32[3]{0:T(128)}, u32[]{:S(2)}) copy-start(s32[3]{0:T(128)} %len_ref.1) | copy-start | bytes 40
  42.6 6.5 %collective-permute-start = (bf16[128,256]{1,0:T(8,128)(2,1)S(1)}, bf16[128,256]{1,0:T(8,128)(2,1)S(1)}, u32[]{:S(2)}, u32[]{:S(2)}) collective-permute-start(bf16[128,256]{1,0:T(8,128)(2,1)S(1)} %get-tuple-element.15), channel_id=1, source_target_pairs={{4,0},{8,4},{12,8},{16,12},{20,16},{24,20},{28,24},{5,1},{9,5},{13... | collective-permute-start | bytes 196616 | tf_op jit(solution)/shard_map/ppermute | solution.py:145
  43.9 7.4 %collective-permute-start.1 = (bf16[128,256]{1,0:T(8,128)(2,1)S(1)}, bf16[128,256]{1,0:T(8,128)(2,1)S(1)}, u32[]{:S(2)}, u32[]{:S(2)}) collective-permute-start(bf16[128,256]{1,0:T(8,128)(2,1)S(1)} %get-tuple-element.16), channel_id=1, source_target_pairs={{8,0},{12,4},{16,8},{20,12},{24,16},{28,20},{9,1},{13,5},{17,9},{2... | collective-permute-start | bytes 196616 | tf_op jit(solution)/shard_map/ppermute | solution.py:145
  45.2 8.9 %collective-permute-start.2 = (bf16[128,256]{1,0:T(8,128)(2,1)S(1)}, bf16[128,256]{1,0:T(8,128)(2,1)S(1)}, u32[]{:S(2)}, u32[]{:S(2)}) collective-permute-start(bf16[128,256]{1,0:T(8,128)(2,1)S(1)} %get-tuple-element.17), channel_id=1, source_target_pairs={{12,0},{16,4},{20,8},{24,12},{28,16},{13,1},{17,5},{21,9},{25,13},... | collective-permute-start | bytes 196616 | tf_op jit(solution)/shard_map/ppermute | solution.py:145
  46.5 13.0 %collective-permute-start.3 = (bf16[128,256]{1,0:T(8,128)(2,1)S(1)}, bf16[128,256]{1,0:T(8,128)(2,1)S(1)}, u32[]{:S(2)}, u32[]{:S(2)}) collective-permute-start(bf16[128,256]{1,0:T(8,128)(2,1)S(1)} %get-tuple-element.18), channel_id=1, source_target_pairs={{16,0},{20,4},{24,8},{28,12},{17,1},{21,5},{25,9},{29,13},{18,2},{... | collective-permute-start | bytes 196616 | tf_op jit(solution)/shard_map/ppermute | solution.py:145
  47.8 12.7 %collective-permute-start.4 = (bf16[128,256]{1,0:T(8,128)(2,1)S(1)}, bf16[128,256]{1,0:T(8,128)(2,1)S(1)}, u32[]{:S(2)}, u32[]{:S(2)}) collective-permute-start(bf16[128,256]{1,0:T(8,128)(2,1)S(1)} %get-tuple-element.19), channel_id=1, source_target_pairs={{20,0},{24,4},{28,8},{21,1},{25,5},{29,9},{22,2},{26,6},{30,10},{2... | collective-permute-start | bytes 196616 | tf_op jit(solution)/shard_map/ppermute | solution.py:145

commit v2 on v1

--- a/solution.py
+++ b/solution.py
@@ -19,41 +19,84 @@
     return lax.dot_general(a, b, (dims, ((), ())), preferred_element_type=F32)
 
 
-def pack_kernel(per_peer, pos_ref, q_ref, k_ref, v_ref, g_ref, out_ref):
+def pack_kernel(
+    per_peer, pos_hbm, len_hbm, q_hbm, k_hbm, v_hbm, g_hbm, out_ref, slot_ref, start_ref,
+    pos_ref, len_ref, q_ref, k_ref, v_ref, g_ref, sems,
+):
+    sources = (pos_hbm, len_hbm, k_hbm, v_hbm, q_hbm, g_hbm)
+    targets = (pos_ref, len_ref, k_ref, v_ref, q_ref, g_ref)
+    copies = [
+        pltpu.make_async_copy(source, target, sems.at[i])
+        for i, (source, target) in enumerate(zip(sources, targets))
+    ]
+    for copy in copies:
+        copy.start()
     tok, width = q_ref.shape
     head = k_ref.shape[1]
+    devices = pos_ref.shape[0]
     me = lax.axis_index("dcp")
-    pos_row = pos_ref[pl.ds(me, 1), :]
-    pos_col = jnp.transpose(jnp.broadcast_to(pos_row, (tok, tok)))
-    smaller = (pos_col < pos_row).astype(jnp.int32)
-    rank = jnp.sum(smaller, axis=0, keepdims=True)
-    slot = jnp.broadcast_to((pos_row % tok).astype(F32), (tok, tok))
     want = lax.broadcasted_iota(jnp.int32, (tok, tok), 0)
-    lane = lax.broadcasted_iota(jnp.int32, (tok, LANES), 1)
-    perm = (rank == want).astype(BF16)
-    out_ref[:, :width] = dot(perm, q_ref[...], ((1,), (0,))).astype(BF16)
-    out_ref[:, width : 2 * width] = dot(perm, g_ref[...], ((1,), (0,))).astype(BF16)
-    slots = jnp.zeros((tok, LANES), F32)
+    copies[0].wait()
+
+    def rank_of(device):
+        pos_row = pos_ref[pl.ds(device, 1), :]
+        pos_col = jnp.transpose(jnp.broadcast_to(pos_row, (tok, tok)))
+        return pos_row, jnp.sum((pos_col < pos_row).astype(jnp.int32), axis=0, keepdims=True)
+
+    rows = (SPAN + 1) * per_peer
+    window = (me - SPAN) * per_peer + lax.broadcasted_iota(jnp.int32, (rows, tok), 0)
+    lane = lax.broadcasted_iota(jnp.int32, (per_peer, LANES), 1)
+
+    def slots_from(source):
+        pos_row, rank = rank_of(source)
+        slot = (pos_row % tok).astype(F32)
+        column = jnp.sum(jnp.where(rank == window, slot, 0.0), axis=1, keepdims=True)
+        slots = jnp.zeros((per_peer, LANES), F32)
+        for block in range(SPAN + 1):
+            slots = jnp.where(lane == block, column[block * per_peer : (block + 1) * per_peer], slots)
+        return slots
+
+    if devices <= 16:
+        for source in range(devices):
+            slot_ref[source * per_peer : (source + 1) * per_peer, :] = slots_from(source)
+    else:
+
+        @pl.loop(0, devices)
+        def _(source):
+            slot_ref[pl.ds(source * per_peer, per_peer), :] = slots_from(source)
+
+    copies[1].wait()
+    q_pos = me * tok + lax.broadcasted_iota(jnp.int32, start_ref.shape, 1) % tok
+    q_start = jnp.zeros(start_ref.shape, jnp.int32)
+    end = jnp.int32(0)
+    for doc in range(len_ref.shape[0]):
+        end = end + len_ref[doc]
+        q_start = jnp.where(q_pos >= end, end, q_start)
+    start_ref[...] = q_start
+
+    _, rank = rank_of(me)
+    copies[2].wait()
+    copies[3].wait()
     for block in range(SPAN + 1):
-        chosen = rank == want + (block - SPAN) * per_peer
-        perm = chosen.astype(BF16)
+        perm = (rank == want + (block - SPAN) * per_peer).astype(BF16)
         first = 2 * width + 2 * head * block
         out_ref[:, first : first + head] = dot(perm, k_ref[...], ((1,), (0,))).astype(BF16)
         out_ref[:, first + head : first + 2 * head] = dot(perm, v_ref[...], ((1,), (0,))).astype(BF16)
-        column = jnp.sum(jnp.where(chosen, slot, 0.0), axis=1, keepdims=True)
-        slots = jnp.where(lane == block, column, slots)
-    first = 2 * width + 2 * head * (SPAN + 1)
-    out_ref[:, first : first + LANES] = slots.astype(BF16)
-
-
-def attend_kernel(width, head, len_ref, in_ref, attn_ref, dq_ref, own_ref, *part_refs):
+    perm = (rank == want).astype(BF16)
+    copies[4].wait()
+    out_ref[:, :width] = dot(perm, q_ref[...], ((1,), (0,))).astype(BF16)
+    copies[5].wait()
+    out_ref[:, width : 2 * width] = dot(perm, g_ref[...], ((1,), (0,))).astype(BF16)
+
+
+def attend_kernel(width, head, start_ref, slot_ref, in_ref, attn_ref, dq_ref, own_ref, *part_refs):
     tok = in_ref.shape[0]
     heads = width // head
     me = lax.axis_index("dcp")
     scale = 1.0 / math.sqrt(head)
     factor = scale * math.log2(math.e)
     base = 2 * width
-    slots = in_ref[:, base + 2 * head * (SPAN + 1) :].astype(F32)
+    slots = slot_ref[...]
     target = lax.broadcasted_iota(jnp.int32, (tok, tok), 1).astype(F32)
     keys, values = [], []
     place = None
@@ -73,11 +116,7 @@
     window = (SPAN + 1) * tok
     lane = lax.broadcasted_iota(jnp.int32, (1, cols), 1)
     q_pos = me * tok + lane % tok
-    q_start = jnp.zeros((1, cols), jnp.int32)
-    end = jnp.int32(0)
-    for doc in range(len_ref.shape[0]):
-        end = end + len_ref[doc]
-        q_start = jnp.where(q_pos >= end, end, q_start)
+    q_start = start_ref[:1, :]
     k_pos = (me - SPAN) * tok + lax.broadcasted_iota(jnp.int32, (window, cols), 0)
     allowed = (k_pos >= q_start) & (k_pos <= q_pos)
 
@@ -118,29 +157,42 @@
     devices = lax.axis_size("dcp")
     per_peer = tok // devices
     vmem = pl.BlockSpec(memory_space=pltpu.VMEM)
-    smem = pl.BlockSpec(memory_space=pltpu.SMEM)
     params = pltpu.CompilerParams(vmem_limit_bytes=48 << 20)
-    total = 2 * width + 2 * head * (SPAN + 1) + LANES
-    packed = pl.pallas_call(
+    hbm = pl.BlockSpec(memory_space=pltpu.HBM)
+    total = 2 * width + 2 * head * (SPAN + 1)
+    packed, slots, starts = pl.pallas_call(
         functools.partial(pack_kernel, per_peer),
-        out_shape=jax.ShapeDtypeStruct((tok, total), BF16),
-        in_specs=[vmem] * 5,
-        out_specs=vmem,
+        out_shape=[
+            jax.ShapeDtypeStruct((tok, total), BF16),
+            jax.ShapeDtypeStruct((tok, LANES), F32),
+            jax.ShapeDtypeStruct((8, 2 * tok), jnp.int32),
+        ],
+        in_specs=[hbm] * 6,
+        out_specs=[vmem] * 3,
+        scratch_shapes=[
+            pltpu.VMEM((devices, tok), jnp.int32),
+            pltpu.SMEM(doc_lengths.shape, jnp.int32),
+            pltpu.VMEM(query.shape, BF16),
+            pltpu.VMEM(key.shape, BF16),
+            pltpu.VMEM(value.shape, BF16),
+            pltpu.VMEM(grad_out.shape, BF16),
+            pltpu.SemaphoreType.DMA((6,)),
+        ],
         compiler_params=params,
         name="pack",
-    )(loader_pos.reshape(devices, tok), query, key, value, grad_out)
+    )(loader_pos.reshape(devices, tok), doc_lengths, query, key, value, grad_out)
     arrived = lax.all_to_all(packed, "dcp", split_axis=0, concat_axis=0, tiled=True)
     wide = jax.ShapeDtypeStruct((tok, width), BF16)
     part = jax.ShapeDtypeStruct((tok, 2 * head), BF16)
     attn_out, dquery, summed, *parts = pl.pallas_call(
         functools.partial(attend_kernel, width, head),
         out_shape=[wide, wide, jax.ShapeDtypeStruct((tok, 2 * head), F32)] + [part] * SPAN,
-        in_specs=[smem, vmem],
+        in_specs=[vmem] * 3,
         out_specs=[vmem] * (3 + SPAN),
         compiler_params=params,
         name="attend",
-    )(doc_lengths, arrived)
-    for offset in range(1, SPAN + 1):
+    )(starts, slots, arrived)
+    for offset in (4, 5, 3, 2, 1):
         pairs = [(source, source - offset) for source in range(offset, devices)]
         summed = summed + lax.ppermute(parts[offset - 1], "dcp", pairs).astype(F32)
     return attn_out, dquery, summed[:, :head].astype(BF16), summed[:, head:].astype(BF16)

time: 61.7 us -> 56.4 us (0.914)
  the two profiles are of different devices: /device:TPU:0 before, /device:TPU:14 now
where the time goes in v2:
time: 56.4 us; the launch traced here: 55.5 us
  blocking collectives  27.2 us (48%)
  starting transfers between devices  10.5 us (19%)
  Pallas kernels  6.57 us (12%)
  local copies, waits for them, and re-layouts  5.38 us (10%)
  waiting for transfers between devices  5.11 us (9%)
  between operations  0.72 us (1%)
    all_to_all x1, blocking collectives, per_device(): lax.all_to_all(packed, 'dcp', split_axis=0, concat_axis=0, tiled=True)  27.2 us
    ppermute x5, starting transfers between devices, per_device(): summed = summed + lax.ppermute(parts[offset - 1], 'dcp', pairs).astype(F32)  10.5 us
    pallas_call x1, Pallas kernels, per_device(): pl.pallas_call(functools.partial(attend_kernel, width, head), out_shape=[...  5.17 us
    ppermute x5, waiting for transfers between devices, per_device(): summed = summed + lax.ppermute(parts[offset - 1], 'dcp', pairs).astype(F32)  5.11 us
    unnamed x12, local copies, waits for them, and re-layouts  4.75 us
    pallas_call x1, Pallas kernels, per_device(): pl.pallas_call(functools.partial(pack_kernel, per_peer), out_shape=[jax.S...  1.4 us
  transfers between devices with their start and end apart: 5, of which 3 were waited for; matrix products, arithmetic and copies ran while one was open for 0% of the time, Pallas kernels for 0%

profile of v2, /device:TPU:14, one launch (start us, length us, event | category | flops | bytes accessed | tf_op | source)
XLA Modules:
  0.0 55.5 jit_solution(11425066714612075019)
XLA Ops:
  0.6 0.0 copy-start.5
  0.6 0.6 %copy-done.5 = s32[3]{0:T(128)S(1)} copy-done((s32[3]{0:T(128)S(1)}, s32[3]{0:T(128)}, u32[]{:S(2)}) %copy-start.5) | copy-done | bytes 36
  1.3 0.0 copy-start
  1.3 0.9 %copy-done = bf16[128,1024]{1,0:T(8,128)(2,1)S(1)} copy-done((bf16[128,1024]{1,0:T(8,128)(2,1)S(1)}, bf16[128,1024]{1,0:T(8,128)(2,1)}, u32[]{:S(2)}) %copy-start) | copy-done | bytes 262168
  2.2 0.0 copy-start.1
  2.2 0.9 %copy-done.1 = bf16[128,1024]{1,0:T(8,128)(2,1)S(1)} copy-done((bf16[128,1024]{1,0:T(8,128)(2,1)S(1)}, bf16[128,1024]{1,0:T(8,128)(2,1)}, u32[]{:S(2)}) %copy-start.1) | copy-done | bytes 262168
  3.2 0.8 %copy-done.2 = bf16[128,128]{1,0:T(8,128)(2,1)S(1)} copy-done((bf16[128,128]{1,0:T(8,128)(2,1)S(1)}, bf16[128,128]{1,0:T(8,128)(2,1)}, u32[]{:S(2)}) %copy-start.2) | copy-done | bytes 32792
  4.0 0.8 %copy-done.3 = bf16[128,128]{1,0:T(8,128)(2,1)S(1)} copy-done((bf16[128,128]{1,0:T(8,128)(2,1)S(1)}, bf16[128,128]{1,0:T(8,128)(2,1)}, u32[]{:S(2)}) %copy-start.3) | copy-done | bytes 32792
  4.7 0.7 %copy-done.4 = s32[1024]{0:T(1024)S(1)} copy-done((s32[1024]{0:T(1024)S(1)}, s32[1024]{0:T(1024)}, u32[]{:S(2)}) %copy-start.4) | copy-done | bytes 4120
  5.4 1.4 %pack.1 = (bf16[128,3584]{1,0:T(8,128)(2,1)S(1)}, f32[128,128]{1,0:T(8,128)S(1)}, s32[8,256]{1,0:T(8,128)S(1)}) custom-call(s32[8,128]{1,0:T(8,128)S(1)} %bitcast.5, s32[3]{0:T(128)S(1)} %copy-done.5, bf16[128,1024]{1,0:T(8,128)(2,1)S(1)} %copy-done, bf16[128,128]{1,0:T(8,128)(2,1)S(1)} %copy-done.2, bf16[128,128]{1,0:T(8,128)(2,1)S(1)} %copy-done.3, ...), custom_call_target="tpu_custom_call" | custom-call | tf_op jit(solution)/shard_map/pack/pallas_call | solution.py:163
  6.8 27.2 %all_to_all.11 = bf16[8,16,3584]{2,1,0:T(8,128)(2,1)S(1)} all-to-all(bf16[8,16,3584]{2,1,0:T(8,128)(2,1)S(1)} %bitcast.4), channel_id=1, replica_groups=mesh['dcp'=8,'rep'=4] {'dcp'}, dimensions={0} | all-to-all | bytes 1835008 | tf_op jit(solution)/shard_map/all_to_all | solution.py:184
  34.0 5.2 %attend.1 = (bf16[128,1024]{1,0:T(8,128)(2,1)}, bf16[128,1024]{1,0:T(8,128)(2,1)}, f32[128,256]{1,0:T(8,128)S(1)}, bf16[128,256]{1,0:T(8,128)(2,1)S(1)}, bf16[12...) custom-call(s32[8,256]{1,0:T(8,128)S(1)} %get-tuple-element.15.start, ...), custom_call_target="tpu_custom_call" | custom-call | tf_op jit(solution)/shard_map/attend/pallas_call | solution.py:187
  39.1 1.3 %collective-permute-start = (bf16[128,256]{1,0:T(8,128)(2,1)S(1)}, bf16[128,256]{1,0:T(8,128)(2,1)S(1)}, u32[]{:S(2)}, u32[]{:S(2)}) collective-permute-start(bf16[128,256]{1,0:T(8,128)(2,1)S(1)} %get-tuple-element.21), channel_id=1, source_target_pairs={{16,0},{20,4},{24,8},{28,12},{17,1},{21,5},{25,9},{29,13},{18,2},{... | collective-permute-start | bytes 196616 | tf_op jit(solution)/shard_map/ppermute | solution.py:197
  40.4 0.7 %collective-permute-start.1 = (bf16[128,256]{1,0:T(8,128)(2,1)S(1)}, bf16[128,256]{1,0:T(8,128)(2,1)S(1)}, u32[]{:S(2)}, u32[]{:S(2)}) collective-permute-start(bf16[128,256]{1,0:T(8,128)(2,1)S(1)} %get-tuple-element.22), channel_id=1, source_target_pairs={{20,0},{24,4},{28,8},{21,1},{25,5},{29,9},{22,2},{26,6},{30,10},{2... | collective-permute-start | bytes 196616 | tf_op jit(solution)/shard_map/ppermute | solution.py:197
  41.1 4.7 %collective-permute-start.2 = (bf16[128,256]{1,0:T(8,128)(2,1)S(1)}, bf16[128,256]{1,0:T(8,128)(2,1)S(1)}, u32[]{:S(2)}, u32[]{:S(2)}) collective-permute-start(bf16[128,256]{1,0:T(8,128)(2,1)S(1)} %get-tuple-element.23), channel_id=1, source_target_pairs={{12,0},{16,4},{20,8},{24,12},{28,16},{13,1},{17,5},{21,9},{25,13},... | collective-permute-start | bytes 196616 | tf_op jit(solution)/shard_map/ppermute | solution.py:197
  45.8 1.9 %collective-permute-start.3 = (bf16[128,256]{1,0:T(8,128)(2,1)S(1)}, bf16[128,256]{1,0:T(8,128)(2,1)S(1)}, u32[]{:S(2)}, u32[]{:S(2)}) collective-permute-start(bf16[128,256]{1,0:T(8,128)(2,1)S(1)} %get-tuple-element.24), channel_id=1, source_target_pairs={{8,0},{12,4},{16,8},{20,12},{24,16},{28,20},{9,1},{13,5},{17,9},{2... | collective-permute-start | bytes 196616 | tf_op jit(solution)/shard_map/ppermute | solution.py:197
  47.8 1.9 %collective-permute-start.4 = (bf16[128,256]{1,0:T(8,128)(2,1)S(1)}, bf16[128,256]{1,0:T(8,128)(2,1)S(1)}, u32[]{:S(2)}, u32[]{:S(2)}) collective-permute-start(bf16[128,256]{1,0:T(8,128)(2,1)S(1)} %get-tuple-element.25), channel_id=1, source_target_pairs={{4,0},{8,4},{12,8},{16,12},{20,16},{24,20},{28,24},{5,1},{9,5},{13... | collective-permute-start | bytes 196616 | tf_op jit(solution)/shard_map/ppermute | solution.py:197
  49.7 0.0 collective-permute-done
  49.7 0.0 collective-permute-done.1
  49.7 1.7 %collective-permute-done.2 = bf16[128,256]{1,0:T(8,128)(2,1)S(1)} collective-permute-done((bf16[128,256]{1,0:T(8,128)(2,1)S(1)}, bf16[128,256]{1,0:T(8,128)(2,1)S(1)}, u32[]{:S(2)}, u32[]{:S(2)}) %collective-permute-start.2) | collective-permute-done | bytes 65568 | tf_op jit(solution)/shard_map/ppermute | solution.py:197
  51.4 0.8 %collective-permute-done.3 = bf16[128,256]{1,0:T(8,128)(2,1)S(1)} collective-permute-done((bf16[128,256]{1,0:T(8,128)(2,1)S(1)}, bf16[128,256]{1,0:T(8,128)(2,1)S(1)}, u32[]{:S(2)}, u32[]{:S(2)}) %collective-permute-start.3) | collective-permute-done | bytes 65568 | tf_op jit(solution)/shard_map/ppermute | solution.py:197
  52.2 2.6 %collective-permute-done.4 = bf16[128,256]{1,0:T(8,128)(2,1)S(1)} collective-permute-done((bf16[128,256]{1,0:T(8,128)(2,1)S(1)}, bf16[128,256]{1,0:T(8,128)(2,1)S(1)}, u32[]{:S(2)}, u32[]{:S(2)}) %collective-permute-start.4) | collective-permute-done | bytes 65568 | tf_op jit(solution)/shard_map/ppermute | solution.py:197
  54.8 0.1 add_convert_fusion
  54.9 0.6 %fusion = (bf16[128,128]{1,0:T(8,128)(2,1)}, bf16[128,128]{1,0:T(8,128)(2,1)}) fusion(bf16[128,256]{1,0:T(8,128)(2,1)S(1)} %add_convert_fusion), kind=kLoop, calls=%fused_computation.1 | loop fusion | bytes 131072 | tf_op jit(solution)/shard_map/slice | solution.py:198
  (3 shorter events, 0.0 us)
Async XLA Ops:
  0.6 0.7 %copy-start.5 = (s32[3]{0:T(128)S(1)}, s32[3]{0:T(128)}, u32[]{:S(2)}) copy-start(s32[3]{0:T(128)} %len_hbm.1) | copy-start | bytes 40
  1.3 0.9 %copy-start = (bf16[128,1024]{1,0:T(8,128)(2,1)S(1)}, bf16[128,1024]{1,0:T(8,128)(2,1)}, u32[]{:S(2)}) copy-start(bf16[128,1024]{1,0:T(8,128)(2,1)} %q_hbm.1) | copy-start | bytes 786436
  2.2 0.9 %copy-start.1 = (bf16[128,1024]{1,0:T(8,128)(2,1)S(1)}, bf16[128,1024]{1,0:T(8,128)(2,1)}, u32[]{:S(2)}) copy-start(bf16[128,1024]{1,0:T(8,128)(2,1)} %g_hbm.1) | copy-start | bytes 786436
  3.2 0.8 %copy-start.2 = (bf16[128,128]{1,0:T(8,128)(2,1)S(1)}, bf16[128,128]{1,0:T(8,128)(2,1)}, u32[]{:S(2)}) copy-start(bf16[128,128]{1,0:T(8,128)(2,1)} %k_hbm.1) | copy-start | bytes 98308
  3.9 0.8 %copy-start.3 = (bf16[128,128]{1,0:T(8,128)(2,1)S(1)}, bf16[128,128]{1,0:T(8,128)(2,1)}, u32[]{:S(2)}) copy-start(bf16[128,128]{1,0:T(8,128)(2,1)} %v_hbm.1) | copy-start | bytes 98308
  4.7 0.7 %copy-start.4 = (s32[1024]{0:T(1024)S(1)}, s32[1024]{0:T(1024)}, u32[]{:S(2)}) copy-start(s32[1024]{0:T(1024)} %param.10) | copy-start | bytes 12292
  39.1 10.6 %collective-permute-start = (bf16[128,256]{1,0:T(8,128)(2,1)S(1)}, bf16[128,256]{1,0:T(8,128)(2,1)S(1)}, u32[]{:S(2)}, u32[]{:S(2)}) collective-permute-start(bf16[128,256]{1,0:T(8,128)(2,1)S(1)} %get-tuple-element.21), channel_id=1, source_target_pairs={{16,0},{20,4},{24,8},{28,12},{17,1},{21,5},{25,9},{29,13},{18,2},{... | collective-permute-start | bytes 196616 | tf_op jit(solution)/shard_map/ppermute | solution.py:197
  40.4 9.3 %collective-permute-start.1 = (bf16[128,256]{1,0:T(8,128)(2,1)S(1)}, bf16[128,256]{1,0:T(8,128)(2,1)S(1)}, u32[]{:S(2)}, u32[]{:S(2)}) collective-permute-start(bf16[128,256]{1,0:T(8,128)(2,1)S(1)} %get-tuple-element.22), channel_id=1, source_target_pairs={{20,0},{24,4},{28,8},{21,1},{25,5},{29,9},{22,2},{26,6},{30,10},{2... | collective-permute-start | bytes 196616 | tf_op jit(solution)/shard_map/ppermute | solution.py:197
  41.1 10.3 %collective-permute-start.2 = (bf16[128,256]{1,0:T(8,128)(2,1)S(1)}, bf16[128,256]{1,0:T(8,128)(2,1)S(1)}, u32[]{:S(2)}, u32[]{:S(2)}) collective-permute-start(bf16[128,256]{1,0:T(8,128)(2,1)S(1)} %get-tuple-element.23), channel_id=1, source_target_pairs={{12,0},{16,4},{20,8},{24,12},{28,16},{13,1},{17,5},{21,9},{25,13},... | collective-permute-start | bytes 196616 | tf_op jit(solution)/shard_map/ppermute | solution.py:197
  45.8 6.4 %collective-permute-start.3 = (bf16[128,256]{1,0:T(8,128)(2,1)S(1)}, bf16[128,256]{1,0:T(8,128)(2,1)S(1)}, u32[]{:S(2)}, u32[]{:S(2)}) collective-permute-start(bf16[128,256]{1,0:T(8,128)(2,1)S(1)} %get-tuple-element.24), channel_id=1, source_target_pairs={{8,0},{12,4},{16,8},{20,12},{24,16},{28,20},{9,1},{13,5},{17,9},{2... | collective-permute-start | bytes 196616 | tf_op jit(solution)/shard_map/ppermute | solution.py:197
  47.8 7.1 %collective-permute-start.4 = (bf16[128,256]{1,0:T(8,128)(2,1)S(1)}, bf16[128,256]{1,0:T(8,128)(2,1)S(1)}, u32[]{:S(2)}, u32[]{:S(2)}) collective-permute-start(bf16[128,256]{1,0:T(8,128)(2,1)S(1)} %get-tuple-element.25), channel_id=1, source_target_pairs={{4,0},{8,4},{12,8},{16,12},{20,16},{24,20},{28,24},{5,1},{9,5},{13... | collective-permute-start | bytes 196616 | tf_op jit(solution)/shard_map/ppermute | solution.py:197

commit v3 on v2

--- a/solution.py
+++ b/solution.py
@@ -180,7 +180,7 @@
         ],
         compiler_params=params,
         name="pack",
-    )(loader_pos.reshape(devices, tok), doc_lengths, query, key, value, grad_out)
+    )(*[pltpu.with_memory_space_constraint(x, pltpu.HBM) for x in (loader_pos.reshape(devices, tok), doc_lengths, query, key, value, grad_out)])
     arrived = lax.all_to_all(packed, "dcp", split_axis=0, concat_axis=0, tiled=True)
     wide = jax.ShapeDtypeStruct((tok, width), BF16)
     part = jax.ShapeDtypeStruct((tok, 2 * head), BF16)

time: 56.4 us -> 51.9 us (0.920)
  local copies, waits for them, and re-layouts: 5.38 us -> 0.63 us
    unnamed x12 -> x0, local copies, waits for them, and re-layouts: 4.75 us -> none
where the time goes in v3:
time: 51.9 us; the launch traced here: 51.2 us
  blocking collectives  27.2 us (52%)
  starting transfers between devices  10.5 us (20%)
  Pallas kernels  7.06 us (14%)
  waiting for transfers between devices  5.11 us (10%)
  between operations  0.7 us (1%)
  local copies, waits for them, and re-layouts  0.63 us (1%)
    all_to_all x1, blocking collectives, per_device(): lax.all_to_all(packed, 'dcp', split_axis=0, concat_axis=0, tiled=True)  27.2 us
    ppermute x5, starting transfers between devices, per_device(): summed = summed + lax.ppermute(parts[offset - 1], 'dcp', pairs).astype(F32)  10.5 us
    pallas_call x1, Pallas kernels, per_device(): pl.pallas_call(functools.partial(attend_kernel, width, head), out_shape=[...  5.17 us
    ppermute x5, waiting for transfers between devices, per_device(): summed = summed + lax.ppermute(parts[offset - 1], 'dcp', pairs).astype(F32)  5.11 us
    pallas_call x1, Pallas kernels, per_device(): pl.pallas_call(functools.partial(pack_kernel, per_peer), out_shape=[jax.S...  1.89 us
  transfers between devices with their start and end apart: 5, of which 3 were waited for; matrix products, arithmetic and copies ran while one was open for 0% of the time, Pallas kernels for 0%

profile of v3, /device:TPU:14, one launch (start us, length us, event | category | flops | bytes accessed | tf_op | source)
XLA Modules:
  0.0 51.2 jit_solution(2384941924211721988)
XLA Ops:
  0.6 1.9 %pack.1 = (bf16[128,3584]{1,0:T(8,128)(2,1)S(1)}, f32[128,128]{1,0:T(8,128)S(1)}, s32[8,256]{1,0:T(8,128)S(1)}) custom-call(s32[8,128]{1,0:T(8,128)} %bitcast.5, s32[3]{0:T(128)} %len_hbm.1, bf16[128,1024]{1,0:T(8,128)(2,1)} %q_hbm.1, bf16[128,128]{1,0:T(8,128)(2,1)} %k_hbm.1, bf16[128,128]{1,0:T(8,128)(2,1)} %v_hbm.1, bf16[128,1024]{1,0:T(8,128)(2,1)} %g_hbm.1), custom_call_target="tpu_custom_call" | custom-call | tf_op jit(solution)/shard_map/pack/pallas_call | solution.py:163
  2.5 27.2 %all_to_all.11 = bf16[8,16,3584]{2,1,0:T(8,128)(2,1)S(1)} all-to-all(bf16[8,16,3584]{2,1,0:T(8,128)(2,1)S(1)} %bitcast.4), channel_id=1, replica_groups=mesh['dcp'=8,'rep'=4] {'dcp'}, dimensions={0} | all-to-all | bytes 1835008 | tf_op jit(solution)/shard_map/all_to_all | solution.py:184
  29.7 5.2 %attend.1 = (bf16[128,1024]{1,0:T(8,128)(2,1)}, bf16[128,1024]{1,0:T(8,128)(2,1)}, f32[128,256]{1,0:T(8,128)S(1)}, bf16[128,256]{1,0:T(8,128)(2,1)S(1)}, bf16[12...) custom-call(s32[8,256]{1,0:T(8,128)S(1)} %get-tuple-element.15.start, ...), custom_call_target="tpu_custom_call" | custom-call | tf_op jit(solution)/shard_map/attend/pallas_call | solution.py:187
  34.9 1.3 %collective-permute-start = (bf16[128,256]{1,0:T(8,128)(2,1)S(1)}, bf16[128,256]{1,0:T(8,128)(2,1)S(1)}, u32[]{:S(2)}, u32[]{:S(2)}) collective-permute-start(bf16[128,256]{1,0:T(8,128)(2,1)S(1)} %get-tuple-element.21), channel_id=1, source_target_pairs={{16,0},{20,4},{24,8},{28,12},{17,1},{21,5},{25,9},{29,13},{18,2},{... | collective-permute-start | bytes 196616 | tf_op jit(solution)/shard_map/ppermute | solution.py:197
  36.2 0.7 %collective-permute-start.1 = (bf16[128,256]{1,0:T(8,128)(2,1)S(1)}, bf16[128,256]{1,0:T(8,128)(2,1)S(1)}, u32[]{:S(2)}, u32[]{:S(2)}) collective-permute-start(bf16[128,256]{1,0:T(8,128)(2,1)S(1)} %get-tuple-element.22), channel_id=1, source_target_pairs={{20,0},{24,4},{28,8},{21,1},{25,5},{29,9},{22,2},{26,6},{30,10},{2... | collective-permute-start | bytes 196616 | tf_op jit(solution)/shard_map/ppermute | solution.py:197
  36.8 4.7 %collective-permute-start.2 = (bf16[128,256]{1,0:T(8,128)(2,1)S(1)}, bf16[128,256]{1,0:T(8,128)(2,1)S(1)}, u32[]{:S(2)}, u32[]{:S(2)}) collective-permute-start(bf16[128,256]{1,0:T(8,128)(2,1)S(1)} %get-tuple-element.23), channel_id=1, source_target_pairs={{12,0},{16,4},{20,8},{24,12},{28,16},{13,1},{17,5},{21,9},{25,13},... | collective-permute-start | bytes 196616 | tf_op jit(solution)/shard_map/ppermute | solution.py:197
  41.6 1.9 %collective-permute-start.3 = (bf16[128,256]{1,0:T(8,128)(2,1)S(1)}, bf16[128,256]{1,0:T(8,128)(2,1)S(1)}, u32[]{:S(2)}, u32[]{:S(2)}) collective-permute-start(bf16[128,256]{1,0:T(8,128)(2,1)S(1)} %get-tuple-element.24), channel_id=1, source_target_pairs={{8,0},{12,4},{16,8},{20,12},{24,16},{28,20},{9,1},{13,5},{17,9},{2... | collective-permute-start | bytes 196616 | tf_op jit(solution)/shard_map/ppermute | solution.py:197
  43.5 1.9 %collective-permute-start.4 = (bf16[128,256]{1,0:T(8,128)(2,1)S(1)}, bf16[128,256]{1,0:T(8,128)(2,1)S(1)}, u32[]{:S(2)}, u32[]{:S(2)}) collective-permute-start(bf16[128,256]{1,0:T(8,128)(2,1)S(1)} %get-tuple-element.25), channel_id=1, source_target_pairs={{4,0},{8,4},{12,8},{16,12},{20,16},{24,20},{28,24},{5,1},{9,5},{13... | collective-permute-start | bytes 196616 | tf_op jit(solution)/shard_map/ppermute | solution.py:197
  45.4 0.0 collective-permute-done
  45.4 0.0 collective-permute-done.1
  45.4 1.7 %collective-permute-done.2 = bf16[128,256]{1,0:T(8,128)(2,1)S(1)} collective-permute-done((bf16[128,256]{1,0:T(8,128)(2,1)S(1)}, bf16[128,256]{1,0:T(8,128)(2,1)S(1)}, u32[]{:S(2)}, u32[]{:S(2)}) %collective-permute-start.2) | collective-permute-done | bytes 65568 | tf_op jit(solution)/shard_map/ppermute | solution.py:197
  47.1 0.8 %collective-permute-done.3 = bf16[128,256]{1,0:T(8,128)(2,1)S(1)} collective-permute-done((bf16[128,256]{1,0:T(8,128)(2,1)S(1)}, bf16[128,256]{1,0:T(8,128)(2,1)S(1)}, u32[]{:S(2)}, u32[]{:S(2)}) %collective-permute-start.3) | collective-permute-done | bytes 65568 | tf_op jit(solution)/shard_map/ppermute | solution.py:197
  47.9 2.6 %collective-permute-done.4 = bf16[128,256]{1,0:T(8,128)(2,1)S(1)} collective-permute-done((bf16[128,256]{1,0:T(8,128)(2,1)S(1)}, bf16[128,256]{1,0:T(8,128)(2,1)S(1)}, u32[]{:S(2)}, u32[]{:S(2)}) %collective-permute-start.4) | collective-permute-done | bytes 65568 | tf_op jit(solution)/shard_map/ppermute | solution.py:197
  50.6 0.1 add_convert_fusion
  50.6 0.6 %fusion = (bf16[128,128]{1,0:T(8,128)(2,1)}, bf16[128,128]{1,0:T(8,128)(2,1)}) fusion(bf16[128,256]{1,0:T(8,128)(2,1)S(1)} %add_convert_fusion), kind=kLoop, calls=%fused_computation.1 | loop fusion | bytes 131072 | tf_op jit(solution)/shard_map/slice | solution.py:198
Async XLA Ops:
  34.9 10.6 %collective-permute-start = (bf16[128,256]{1,0:T(8,128)(2,1)S(1)}, bf16[128,256]{1,0:T(8,128)(2,1)S(1)}, u32[]{:S(2)}, u32[]{:S(2)}) collective-permute-start(bf16[128,256]{1,0:T(8,128)(2,1)S(1)} %get-tuple-element.21), channel_id=1, source_target_pairs={{16,0},{20,4},{24,8},{28,12},{17,1},{21,5},{25,9},{29,13},{18,2},{... | collective-permute-start | bytes 196616 | tf_op jit(solution)/shard_map/ppermute | solution.py:197
  36.2 9.3 %collective-permute-start.1 = (bf16[128,256]{1,0:T(8,128)(2,1)S(1)}, bf16[128,256]{1,0:T(8,128)(2,1)S(1)}, u32[]{:S(2)}, u32[]{:S(2)}) collective-permute-start(bf16[128,256]{1,0:T(8,128)(2,1)S(1)} %get-tuple-element.22), channel_id=1, source_target_pairs={{20,0},{24,4},{28,8},{21,1},{25,5},{29,9},{22,2},{26,6},{30,10},{2... | collective-permute-start | bytes 196616 | tf_op jit(solution)/shard_map/ppermute | solution.py:197
  36.8 10.3 %collective-permute-start.2 = (bf16[128,256]{1,0:T(8,128)(2,1)S(1)}, bf16[128,256]{1,0:T(8,128)(2,1)S(1)}, u32[]{:S(2)}, u32[]{:S(2)}) collective-permute-start(bf16[128,256]{1,0:T(8,128)(2,1)S(1)} %get-tuple-element.23), channel_id=1, source_target_pairs={{12,0},{16,4},{20,8},{24,12},{28,16},{13,1},{17,5},{21,9},{25,13},... | collective-permute-start | bytes 196616 | tf_op jit(solution)/shard_map/ppermute | solution.py:197
  41.6 6.4 %collective-permute-start.3 = (bf16[128,256]{1,0:T(8,128)(2,1)S(1)}, bf16[128,256]{1,0:T(8,128)(2,1)S(1)}, u32[]{:S(2)}, u32[]{:S(2)}) collective-permute-start(bf16[128,256]{1,0:T(8,128)(2,1)S(1)} %get-tuple-element.24), channel_id=1, source_target_pairs={{8,0},{12,4},{16,8},{20,12},{24,16},{28,20},{9,1},{13,5},{17,9},{2... | collective-permute-start | bytes 196616 | tf_op jit(solution)/shard_map/ppermute | solution.py:197
  43.5 7.1 %collective-permute-start.4 = (bf16[128,256]{1,0:T(8,128)(2,1)S(1)}, bf16[128,256]{1,0:T(8,128)(2,1)S(1)}, u32[]{:S(2)}, u32[]{:S(2)}) collective-permute-start(bf16[128,256]{1,0:T(8,128)(2,1)S(1)} %get-tuple-element.25), channel_id=1, source_target_pairs={{4,0},{8,4},{12,8},{16,12},{20,16},{24,20},{28,24},{5,1},{9,5},{13... | collective-permute-start | bytes 196616 | tf_op jit(solution)/shard_map/ppermute | solution.py:197

commit v4 on v3

--- a/solution.py
+++ b/solution.py
@@ -20,9 +20,10 @@
 
 
 def pack_kernel(
-    per_peer, pos_hbm, len_hbm, q_hbm, k_hbm, v_hbm, g_hbm, out_ref, slot_ref, start_ref,
-    pos_ref, len_ref, q_ref, k_ref, v_ref, g_ref, sems,
+    per_peer, paired, pos_hbm, len_hbm, q_hbm, k_hbm, v_hbm, g_hbm, *rest
 ):
+    out_refs = rest[:-9]
+    slot_ref, start_ref, pos_ref, len_ref, q_ref, k_ref, v_ref, g_ref, sems = rest[-9:]
     sources = (pos_hbm, len_hbm, k_hbm, v_hbm, q_hbm, g_hbm)
     targets = (pos_ref, len_ref, k_ref, v_ref, q_ref, g_ref)
     copies = [
@@ -36,7 +37,15 @@
     devices = pos_ref.shape[0]
     me = lax.axis_index("dcp")
     want = lax.broadcasted_iota(jnp.int32, (tok, tok), 0)
+    if paired:
+        want = ((want // per_peer) ^ me) * per_peer + want % per_peer
     copies[0].wait()
+
+    def put(first, rows):
+        rows = rows.astype(BF16)
+        step = tok // len(out_refs)
+        for i, out_ref in enumerate(out_refs):
+            out_ref[:, first : first + rows.shape[1]] = rows[i * step : (i + 1) * step]
 
     def rank_of(device):
         pos_row = pos_ref[pl.ds(device, 1), :]
@@ -58,7 +67,8 @@
 
     if devices <= 16:
         for source in range(devices):
-            slot_ref[source * per_peer : (source + 1) * per_peer, :] = slots_from(source)
+            device = source ^ me if paired else source
+            slot_ref[source * per_peer : (source + 1) * per_peer, :] = slots_from(device)
     else:
 
         @pl.loop(0, devices)
@@ -80,17 +90,19 @@
     for block in range(SPAN + 1):
         perm = (rank == want + (block - SPAN) * per_peer).astype(BF16)
         first = 2 * width + 2 * head * block
-        out_ref[:, first : first + head] = dot(perm, k_ref[...], ((1,), (0,))).astype(BF16)
-        out_ref[:, first + head : first + 2 * head] = dot(perm, v_ref[...], ((1,), (0,))).astype(BF16)
+        put(first, dot(perm, k_ref[...], ((1,), (0,))))
+        put(first + head, dot(perm, v_ref[...], ((1,), (0,))))
     perm = (rank == want).astype(BF16)
     copies[4].wait()
-    out_ref[:, :width] = dot(perm, q_ref[...], ((1,), (0,))).astype(BF16)
+    put(0, dot(perm, q_ref[...], ((1,), (0,))))
     copies[5].wait()
-    out_ref[:, width : 2 * width] = dot(perm, g_ref[...], ((1,), (0,))).astype(BF16)
-
-
-def attend_kernel(width, head, start_ref, slot_ref, in_ref, attn_ref, dq_ref, own_ref, *part_refs):
-    tok = in_ref.shape[0]
+    put(width, dot(perm, g_ref[...], ((1,), (0,))))
+
+
+def attend_kernel(width, head, pieces, start_ref, slot_ref, *refs):
+    in_refs = refs[:pieces]
+    attn_ref, dq_ref, own_ref, *part_refs = refs[pieces:]
+    tok = attn_ref.shape[0]
     heads = width // head
     me = lax.axis_index("dcp")
     scale = 1.0 / math.sqrt(head)
@@ -98,18 +110,22 @@
     base = 2 * width
     slots = slot_ref[...]
     target = lax.broadcasted_iota(jnp.int32, (tok, tok), 1).astype(F32)
+
+    def arrived(first, last):
+        return jnp.concatenate([ref[:, first:last] for ref in in_refs], axis=0)
+
     keys, values = [], []
     place = None
     for block in range(SPAN + 1):
         place = (slots[:, block : block + 1] == target).astype(BF16)
         first = base + 2 * head * block
-        both = dot(place, in_ref[:, first : first + 2 * head], ((0,), (0,))).astype(BF16)
+        both = dot(place, arrived(first, first + 2 * head), ((0,), (0,))).astype(BF16)
         keys.append(both[:, :head])
         values.append(both[:, head:])
     key = jnp.concatenate(keys, axis=0)
     value = jnp.concatenate(values, axis=0)
-    queries = dot(place, in_ref[:, :width], ((0,), (0,))).astype(BF16)
-    grads = dot(place, in_ref[:, width:base], ((0,), (0,))).astype(BF16)
+    queries = dot(place, arrived(0, width), ((0,), (0,))).astype(BF16)
+    grads = dot(place, arrived(width, base), ((0,), (0,))).astype(BF16)
 
     pairs = 2
     cols = pairs * tok
@@ -160,15 +176,17 @@
     params = pltpu.CompilerParams(vmem_limit_bytes=48 << 20)
     hbm = pl.BlockSpec(memory_space=pltpu.HBM)
     total = 2 * width + 2 * head * (SPAN + 1)
-    packed, slots, starts = pl.pallas_call(
-        functools.partial(pack_kernel, per_peer),
-        out_shape=[
-            jax.ShapeDtypeStruct((tok, total), BF16),
+    paired = devices <= 16 and devices & (devices - 1) == 0
+    pieces = devices if paired else 1
+    *packed, slots, starts = pl.pallas_call(
+        functools.partial(pack_kernel, per_peer, paired),
+        out_shape=[jax.ShapeDtypeStruct((tok // pieces, total), BF16)] * pieces
+        + [
             jax.ShapeDtypeStruct((tok, LANES), F32),
             jax.ShapeDtypeStruct((8, 2 * tok), jnp.int32),
         ],
         in_specs=[hbm] * 6,
-        out_specs=[vmem] * 3,
+        out_specs=[vmem] * (pieces + 2),
         scratch_shapes=[
             pltpu.VMEM((devices, tok), jnp.int32),
             pltpu.SMEM(doc_lengths.shape, jnp.int32),
@@ -181,17 +199,22 @@
         compiler_params=params,
         name="pack",
     )(*[pltpu.with_memory_space_constraint(x, pltpu.HBM) for x in (loader_pos.reshape(devices, tok), doc_lengths, query, key, value, grad_out)])
-    arrived = lax.all_to_all(packed, "dcp", split_axis=0, concat_axis=0, tiled=True)
+    if paired:
+        for step in range(1, devices):
+            partners = [(source, source ^ step) for source in range(devices)]
+            packed[step] = lax.ppermute(packed[step], "dcp", partners)
+    else:
+        packed = [lax.all_to_all(packed[0], "dcp", split_axis=0, concat_axis=0, tiled=True)]
     wide = jax.ShapeDtypeStruct((tok, width), BF16)
     part = jax.ShapeDtypeStruct((tok, 2 * head), BF16)
     attn_out, dquery, summed, *parts = pl.pallas_call(
-        functools.partial(attend_kernel, width, head),
+        functools.partial(attend_kernel, width, head, pieces),
         out_shape=[wide, wide, jax.ShapeDtypeStruct((tok, 2 * head), F32)] + [part] * SPAN,
-        in_specs=[vmem] * 3,
+        in_specs=[vmem] * (2 + pieces),
         out_specs=[vmem] * (3 + SPAN),
         compiler_params=params,
         name="attend",
-    )(starts, slots, arrived)
+    )(starts, slots, *packed)
     for offset in (4, 5, 3, 2, 1):
         pairs = [(source, source - offset) for source in range(offset, devices)]
         summed = summed + lax.ppermute(parts[offset - 1], "dcp", pairs).astype(F32)

time: 51.9 us -> 48.9 us (0.942)
  blocking collectives: 27.2 us -> 0 us
  waiting for transfers between devices: 5.11 us -> 20.6 us
  starting transfers between devices: 10.5 us -> 19.3 us
    all_to_all x1 -> x0, blocking collectives: 27.2 us -> none  [per_device(): lax.all_to_all(packed, 'dcp', split_axis=0, concat_axis=0, tiled=True)]
    ppermute x0 -> x7, waiting for transfers between devices: none -> 15.3 us  [per_device(): packed[step] = lax.ppermute(packed[step], 'dcp', partners)]
    ppermute x0 -> x7, starting transfers between devices: none -> 10.2 us  [per_device(): packed[step] = lax.ppermute(packed[step], 'dcp', partners)]
    ppermute x5, starting transfers between devices: 10.5 us -> 9.17 us  [per_device(): summed = summed + lax.ppermute(parts[offset - 1], 'dcp', pairs).astype(F32)]
  transfers between devices with their start and end apart: 5 -> 12, of which waited for: 3 -> 7; matrix products, arithmetic and copies ran while one was open for 0% -> 0% of each run, Pallas kernels for 0% -> 0%
where the time goes in v4:
time: 48.9 us; the launch traced here: 48.4 us
  waiting for transfers between devices  20.6 us (42%)
  starting transfers between devices  19.3 us (39%)
  Pallas kernels  7.07 us (14%)
  between operations  0.71 us (1%)
  local copies, waits for them, and re-layouts  0.63 us (1%)
    ppermute x7, waiting for transfers between devices, per_device(): packed[step] = lax.ppermute(packed[step], 'dcp', partners)  15.3 us
    ppermute x7, starting transfers between devices, per_device(): packed[step] = lax.ppermute(packed[step], 'dcp', partners)  10.2 us
    ppermute x5, starting transfers between devices, per_device(): summed = summed + lax.ppermute(parts[offset - 1], 'dcp', pairs).astype(F32)  9.17 us
    ppermute x5, waiting for transfers between devices, per_device(): summed = summed + lax.ppermute(parts[offset - 1], 'dcp', pairs).astype(F32)  5.34 us
    pallas_call x1, Pallas kernels, per_device(): pl.pallas_call(functools.partial(attend_kernel, width, head, pieces), out...  5.17 us
    pallas_call x1, Pallas kernels, per_device(): pl.pallas_call(functools.partial(pack_kernel, per_peer, paired), out_shap...  1.9 us
  transfers between devices with their start and end apart: 12, of which 7 were waited for; matrix products, arithmetic and copies ran while one was open for 0% of the time, Pallas kernels for 0%

profile of v4, /device:TPU:14, one launch (start us, length us, event | category | flops | bytes accessed | tf_op | source)
XLA Modules:
  0.0 48.4 jit_solution(9579337013700699175)
XLA Ops:
  0.6 1.9 %pack.1 = (bf16[16,3584]{1,0:T(8,128)(2,1)S(1)}, bf16[16,3584]{1,0:T(8,128)(2,1)S(1)}, bf16[16,3584]{1,0:T(8,128)(2,1)S(1)}, bf16[16,3584]{1,0:T(8,128)(2,1)S(1)...) custom-call(s32[8,128]{1,0:T(8,128)} %bitcast.1, ...), custom_call_target="tpu_custom_call" | custom-call | tf_op jit(solution)/shard_map/pack/pallas_call | solution.py:181
  2.5 0.6 %collective-permute-start = (bf16[16,3584]{1,0:T(8,128)(2,1)S(1)}, bf16[16,3584]{1,0:T(8,128)(2,1)S(1)}, u32[]{:S(2)}, u32[]{:S(2)}) collective-permute-start(bf16[16,3584]{1,0:T(8,128)(2,1)S(1)} %get-tuple-element.25), channel_id=1, source_target_pairs={{0,4},{4,0},{8,12},{12,8},{16,20},{20,16},{24,28},{28,24},{1,5},{5... | collective-permute-start | bytes 344072 | tf_op jit(solution)/shard_map/ppermute | solution.py:205
  3.1 0.5 collective-permute-start.1
  3.6 2.5 %collective-permute-start.2 = (bf16[16,3584]{1,0:T(8,128)(2,1)S(1)}, bf16[16,3584]{1,0:T(8,128)(2,1)S(1)}, u32[]{:S(2)}, u32[]{:S(2)}) collective-permute-start(bf16[16,3584]{1,0:T(8,128)(2,1)S(1)} %get-tuple-element.27), channel_id=1, source_target_pairs={{0,12},{4,8},{8,4},{12,0},{16,28},{20,24},{24,20},{28,16},{1,13},{... | collective-permute-start | bytes 344072 | tf_op jit(solution)/shard_map/ppermute | solution.py:205
  6.1 2.6 %collective-permute-start.3 = (bf16[16,3584]{1,0:T(8,128)(2,1)S(1)}, bf16[16,3584]{1,0:T(8,128)(2,1)S(1)}, u32[]{:S(2)}, u32[]{:S(2)}) collective-permute-start(bf16[16,3584]{1,0:T(8,128)(2,1)S(1)} %get-tuple-element.28), channel_id=1, source_target_pairs={{0,16},{4,20},{8,24},{12,28},{16,0},{20,4},{24,8},{28,12},{1,17},{... | collective-permute-start | bytes 344072 | tf_op jit(solution)/shard_map/ppermute | solution.py:205
  8.7 0.3 collective-permute-start.4
  9.0 0.0 collective-permute-done.refs_1_
  9.0 1.6 %collective-permute-start.5 = (bf16[16,3584]{1,0:T(8,128)(2,1)S(1)}, bf16[16,3584]{1,0:T(8,128)(2,1)S(1)}, u32[]{:S(2)}, u32[]{:S(2)}) collective-permute-start(bf16[16,3584]{1,0:T(8,128)(2,1)S(1)} %get-tuple-element.30), channel_id=1, source_target_pairs={{0,24},{4,28},{8,16},{12,20},{16,8},{20,12},{24,0},{28,4},{1,25},{... | collective-permute-start | bytes 344072 | tf_op jit(solution)/shard_map/ppermute | solution.py:205
  10.5 2.2 %collective-permute-start.6 = (bf16[16,3584]{1,0:T(8,128)(2,1)S(1)}, bf16[16,3584]{1,0:T(8,128)(2,1)S(1)}, u32[]{:S(2)}, u32[]{:S(2)}) collective-permute-start(bf16[16,3584]{1,0:T(8,128)(2,1)S(1)} %get-tuple-element.31), channel_id=1, source_target_pairs={{0,28},{4,24},{8,20},{12,16},{16,12},{20,8},{24,4},{28,0},{1,29},{... | collective-permute-start | bytes 344072 | tf_op jit(solution)/shard_map/ppermute | solution.py:205
  12.7 8.4 %collective-permute-done.3.refs_4_ = bf16[16,3584]{1,0:T(8,128)(2,1)S(1)} collective-permute-done((bf16[16,3584]{1,0:T(8,128)(2,1)S(1)}, bf16[16,3584]{1,0:T(8,128)(2,1)S(1)}, u32[]{:S(2)}, u32[]{:S(2)}) %collective-permute-start.3) | collective-permute-done | bytes 114720 | tf_op jit(solution)/shard_map/ppermute | solution.py:205
  21.1 2.5 %collective-permute-done.4.refs_5_ = bf16[16,3584]{1,0:T(8,128)(2,1)S(1)} collective-permute-done((bf16[16,3584]{1,0:T(8,128)(2,1)S(1)}, bf16[16,3584]{1,0:T(8,128)(2,1)S(1)}, u32[]{:S(2)}, u32[]{:S(2)}) %collective-permute-start.4) | collective-permute-done | bytes 114720 | tf_op jit(solution)/shard_map/ppermute | solution.py:205
  23.5 2.9 %collective-permute-done.5.refs_6_ = bf16[16,3584]{1,0:T(8,128)(2,1)S(1)} collective-permute-done((bf16[16,3584]{1,0:T(8,128)(2,1)S(1)}, bf16[16,3584]{1,0:T(8,128)(2,1)S(1)}, u32[]{:S(2)}, u32[]{:S(2)}) %collective-permute-start.5) | collective-permute-done | bytes 114720 | tf_op jit(solution)/shard_map/ppermute | solution.py:205
  26.5 1.5 %collective-permute-done.6.refs_7_ = bf16[16,3584]{1,0:T(8,128)(2,1)S(1)} collective-permute-done((bf16[16,3584]{1,0:T(8,128)(2,1)S(1)}, bf16[16,3584]{1,0:T(8,128)(2,1)S(1)}, u32[]{:S(2)}, u32[]{:S(2)}) %collective-permute-start.6) | collective-permute-done | bytes 114720 | tf_op jit(solution)/shard_map/ppermute | solution.py:205
  28.0 5.2 %attend.1 = (bf16[128,1024]{1,0:T(8,128)(2,1)}, bf16[128,1024]{1,0:T(8,128)(2,1)}, f32[128,256]{1,0:T(8,128)S(1)}, bf16[128,256]{1,0:T(8,128)(2,1)S(1)}, bf16[12...) custom-call(s32[8,256]{1,0:T(8,128)S(1)} %get-tuple-element.22.start, ...), custom_call_target="tpu_custom_call" | custom-call | tf_op jit(solution)/shard_map/attend/pallas_call | solution.py:210
  33.1 1.3 %collective-permute-start.7 = (bf16[128,256]{1,0:T(8,128)(2,1)S(1)}, bf16[128,256]{1,0:T(8,128)(2,1)S(1)}, u32[]{:S(2)}, u32[]{:S(2)}) collective-permute-start(bf16[128,256]{1,0:T(8,128)(2,1)S(1)} %get-tuple-element.35), channel_id=1, source_target_pairs={{16,0},{20,4},{24,8},{28,12},{17,1},{21,5},{25,9},{29,13},{18,2},{... | collective-permute-start | bytes 196616 | tf_op jit(solution)/shard_map/ppermute | solution.py:220
  34.4 0.7 %collective-permute-start.8 = (bf16[128,256]{1,0:T(8,128)(2,1)S(1)}, bf16[128,256]{1,0:T(8,128)(2,1)S(1)}, u32[]{:S(2)}, u32[]{:S(2)}) collective-permute-start(bf16[128,256]{1,0:T(8,128)(2,1)S(1)} %get-tuple-element.36), channel_id=1, source_target_pairs={{20,0},{24,4},{28,8},{21,1},{25,5},{29,9},{22,2},{26,6},{30,10},{2... | collective-permute-start | bytes 196616 | tf_op jit(solution)/shard_map/ppermute | solution.py:220
  35.1 1.9 %collective-permute-start.9 = (bf16[128,256]{1,0:T(8,128)(2,1)S(1)}, bf16[128,256]{1,0:T(8,128)(2,1)S(1)}, u32[]{:S(2)}, u32[]{:S(2)}) collective-permute-start(bf16[128,256]{1,0:T(8,128)(2,1)S(1)} %get-tuple-element.37), channel_id=1, source_target_pairs={{12,0},{16,4},{20,8},{24,12},{28,16},{13,1},{17,5},{21,9},{25,13},... | collective-permute-start | bytes 196616 | tf_op jit(solution)/shard_map/ppermute | solution.py:220
  37.0 1.9 %collective-permute-start.10 = (bf16[128,256]{1,0:T(8,128)(2,1)S(1)}, bf16[128,256]{1,0:T(8,128)(2,1)S(1)}, u32[]{:S(2)}, u32[]{:S(2)}) collective-permute-start(bf16[128,256]{1,0:T(8,128)(2,1)S(1)} %get-tuple-element.38), channel_id=1, source_target_pairs={{8,0},{12,4},{16,8},{20,12},{24,16},{28,20},{9,1},{13,5},{17,9},{2... | collective-permute-start | bytes 196616 | tf_op jit(solution)/shard_map/ppermute | solution.py:220
  39.0 3.4 %collective-permute-start.11 = (bf16[128,256]{1,0:T(8,128)(2,1)S(1)}, bf16[128,256]{1,0:T(8,128)(2,1)S(1)}, u32[]{:S(2)}, u32[]{:S(2)}) collective-permute-start(bf16[128,256]{1,0:T(8,128)(2,1)S(1)} %get-tuple-element.39), channel_id=1, source_target_pairs={{4,0},{8,4},{12,8},{16,12},{20,16},{24,20},{28,24},{5,1},{9,5},{13... | collective-permute-start | bytes 196616 | tf_op jit(solution)/shard_map/ppermute | solution.py:220
  42.4 1.9 %collective-permute-done.9 = bf16[128,256]{1,0:T(8,128)(2,1)S(1)} collective-permute-done((bf16[128,256]{1,0:T(8,128)(2,1)S(1)}, bf16[128,256]{1,0:T(8,128)(2,1)S(1)}, u32[]{:S(2)}, u32[]{:S(2)}) %collective-permute-start.9) | collective-permute-done | bytes 65568 | tf_op jit(solution)/shard_map/ppermute | solution.py:220
  44.2 0.5 %collective-permute-done.10 = bf16[128,256]{1,0:T(8,128)(2,1)S(1)} collective-permute-done((bf16[128,256]{1,0:T(8,128)(2,1)S(1)}, bf16[128,256]{1,0:T(8,128)(2,1)S(1)}, u32[]{:S(2)}, u32[]{:S(2)}) %collective-permute-start.10) | collective-permute-done | bytes 65568 | tf_op jit(solution)/shard_map/ppermute | solution.py:220
  44.8 2.9 %collective-permute-done.11 = bf16[128,256]{1,0:T(8,128)(2,1)S(1)} collective-permute-done((bf16[128,256]{1,0:T(8,128)(2,1)S(1)}, bf16[128,256]{1,0:T(8,128)(2,1)S(1)}, u32[]{:S(2)}, u32[]{:S(2)}) %collective-permute-start.11) | collective-permute-done | bytes 65568 | tf_op jit(solution)/shard_map/ppermute | solution.py:220
  47.7 0.1 add_convert_fusion
  47.8 0.6 %fusion = (bf16[128,128]{1,0:T(8,128)(2,1)}, bf16[128,128]{1,0:T(8,128)(2,1)}) fusion(bf16[128,256]{1,0:T(8,128)(2,1)S(1)} %add_convert_fusion), kind=kLoop, calls=%fused_computation.1 | loop fusion | bytes 131072 | tf_op jit(solution)/shard_map/slice | solution.py:221
  (4 shorter events, 0.0 us)
Async XLA Ops:
  2.5 6.4 %collective-permute-start = (bf16[16,3584]{1,0:T(8,128)(2,1)S(1)}, bf16[16,3584]{1,0:T(8,128)(2,1)S(1)}, u32[]{:S(2)}, u32[]{:S(2)}) collective-permute-start(bf16[16,3584]{1,0:T(8,128)(2,1)S(1)} %get-tuple-element.25), channel_id=1, source_target_pairs={{0,4},{4,0},{8,12},{12,8},{16,20},{20,16},{24,28},{28,24},{1,5},{5... | collective-permute-start | bytes 344072 | tf_op jit(solution)/shard_map/ppermute | solution.py:205
  3.1 7.4 %collective-permute-start.1 = (bf16[16,3584]{1,0:T(8,128)(2,1)S(1)}, bf16[16,3584]{1,0:T(8,128)(2,1)S(1)}, u32[]{:S(2)}, u32[]{:S(2)}) collective-permute-start(bf16[16,3584]{1,0:T(8,128)(2,1)S(1)} %get-tuple-element.26), channel_id=1, source_target_pairs={{0,8},{4,12},{8,0},{12,4},{16,24},{20,28},{24,16},{28,20},{1,9},{5... | collective-permute-start | bytes 344072 | tf_op jit(solution)/shard_map/ppermute | solution.py:205
  3.6 9.1 %collective-permute-start.2 = (bf16[16,3584]{1,0:T(8,128)(2,1)S(1)}, bf16[16,3584]{1,0:T(8,128)(2,1)S(1)}, u32[]{:S(2)}, u32[]{:S(2)}) collective-permute-start(bf16[16,3584]{1,0:T(8,128)(2,1)S(1)} %get-tuple-element.27), channel_id=1, source_target_pairs={{0,12},{4,8},{8,4},{12,0},{16,28},{20,24},{24,20},{28,16},{1,13},{... | collective-permute-start | bytes 344072 | tf_op jit(solution)/shard_map/ppermute | solution.py:205
  6.1 15.0 %collective-permute-start.3 = (bf16[16,3584]{1,0:T(8,128)(2,1)S(1)}, bf16[16,3584]{1,0:T(8,128)(2,1)S(1)}, u32[]{:S(2)}, u32[]{:S(2)}) collective-permute-start(bf16[16,3584]{1,0:T(8,128)(2,1)S(1)} %get-tuple-element.28), channel_id=1, source_target_pairs={{0,16},{4,20},{8,24},{12,28},{16,0},{20,4},{24,8},{28,12},{1,17},{... | collective-permute-start | bytes 344072 | tf_op jit(solution)/shard_map/ppermute | solution.py:205
  8.7 14.8 %collective-permute-start.4 = (bf16[16,3584]{1,0:T(8,128)(2,1)S(1)}, bf16[16,3584]{1,0:T(8,128)(2,1)S(1)}, u32[]{:S(2)}, u32[]{:S(2)}) collective-permute-start(bf16[16,3584]{1,0:T(8,128)(2,1)S(1)} %get-tuple-element.29), channel_id=1, source_target_pairs={{0,20},{4,16},{8,28},{12,24},{16,4},{20,0},{24,12},{28,8},{1,21},{... | collective-permute-start | bytes 344072 | tf_op jit(solution)/shard_map/ppermute | solution.py:205
  9.0 17.5 %collective-permute-start.5 = (bf16[16,3584]{1,0:T(8,128)(2,1)S(1)}, bf16[16,3584]{1,0:T(8,128)(2,1)S(1)}, u32[]{:S(2)}, u32[]{:S(2)}) collective-permute-start(bf16[16,3584]{1,0:T(8,128)(2,1)S(1)} %get-tuple-element.30), channel_id=1, source_target_pairs={{0,24},{4,28},{8,16},{12,20},{16,8},{20,12},{24,0},{28,4},{1,25},{... | collective-permute-start | bytes 344072 | tf_op jit(solution)/shard_map/ppermute | solution.py:205
  10.5 17.4 %collective-permute-start.6 = (bf16[16,3584]{1,0:T(8,128)(2,1)S(1)}, bf16[16,3584]{1,0:T(8,128)(2,1)S(1)}, u32[]{:S(2)}, u32[]{:S(2)}) collective-permute-start(bf16[16,3584]{1,0:T(8,128)(2,1)S(1)} %get-tuple-element.31), channel_id=1, source_target_pairs={{0,28},{4,24},{8,20},{12,16},{16,12},{20,8},{24,4},{28,0},{1,29},{... | collective-permute-start | bytes 344072 | tf_op jit(solution)/shard_map/ppermute | solution.py:205
  33.1 9.2 %collective-permute-start.7 = (bf16[128,256]{1,0:T(8,128)(2,1)S(1)}, bf16[128,256]{1,0:T(8,128)(2,1)S(1)}, u32[]{:S(2)}, u32[]{:S(2)}) collective-permute-start(bf16[128,256]{1,0:T(8,128)(2,1)S(1)} %get-tuple-element.35), channel_id=1, source_target_pairs={{16,0},{20,4},{24,8},{28,12},{17,1},{21,5},{25,9},{29,13},{18,2},{... | collective-permute-start | bytes 196616 | tf_op jit(solution)/shard_map/ppermute | solution.py:220
  34.4 7.9 %collective-permute-start.8 = (bf16[128,256]{1,0:T(8,128)(2,1)S(1)}, bf16[128,256]{1,0:T(8,128)(2,1)S(1)}, u32[]{:S(2)}, u32[]{:S(2)}) collective-permute-start(bf16[128,256]{1,0:T(8,128)(2,1)S(1)} %get-tuple-element.36), channel_id=1, source_target_pairs={{20,0},{24,4},{28,8},{21,1},{25,5},{29,9},{22,2},{26,6},{30,10},{2... | collective-permute-start | bytes 196616 | tf_op jit(solution)/shard_map/ppermute | solution.py:220
  35.1 9.1 %collective-permute-start.9 = (bf16[128,256]{1,0:T(8,128)(2,1)S(1)}, bf16[128,256]{1,0:T(8,128)(2,1)S(1)}, u32[]{:S(2)}, u32[]{:S(2)}) collective-permute-start(bf16[128,256]{1,0:T(8,128)(2,1)S(1)} %get-tuple-element.37), channel_id=1, source_target_pairs={{12,0},{16,4},{20,8},{24,12},{28,16},{13,1},{17,5},{21,9},{25,13},... | collective-permute-start | bytes 196616 | tf_op jit(solution)/shard_map/ppermute | solution.py:220
  37.0 7.7 %collective-permute-start.10 = (bf16[128,256]{1,0:T(8,128)(2,1)S(1)}, bf16[128,256]{1,0:T(8,128)(2,1)S(1)}, u32[]{:S(2)}, u32[]{:S(2)}) collective-permute-start(bf16[128,256]{1,0:T(8,128)(2,1)S(1)} %get-tuple-element.38), channel_id=1, source_target_pairs={{8,0},{12,4},{16,8},{20,12},{24,16},{28,20},{9,1},{13,5},{17,9},{2... | collective-permute-start | bytes 196616 | tf_op jit(solution)/shard_map/ppermute | solution.py:220
  39.0 8.8 %collective-permute-start.11 = (bf16[128,256]{1,0:T(8,128)(2,1)S(1)}, bf16[128,256]{1,0:T(8,128)(2,1)S(1)}, u32[]{:S(2)}, u32[]{:S(2)}) collective-permute-start(bf16[128,256]{1,0:T(8,128)(2,1)S(1)} %get-tuple-element.39), channel_id=1, source_target_pairs={{4,0},{8,4},{12,8},{16,12},{20,16},{24,20},{28,24},{5,1},{9,5},{13... | collective-permute-start | bytes 196616 | tf_op jit(solution)/shard_map/ppermute | solution.py:220

commit v5 on v4

v5 whole, which is shorter than its diff:
```python
import functools
import math

import jax
import jax.numpy as jnp
from jax import lax
from jax.experimental import pallas as pl
from jax.experimental.pallas import tpu as pltpu
from jax.sharding import PartitionSpec as P

SPAN = 5
LANES = 128
NEG = -1e30
F32 = jnp.float32
BF16 = jnp.bfloat16


def dot(a, b, dims):
    return lax.dot_general(a, b, (dims, ((), ())), preferred_element_type=F32)


def rank_of(pos_ref, device):
    tok = pos_ref.shape[1]
    pos_row = pos_ref[pl.ds(device, 1), :]
    pos_col = jnp.transpose(jnp.broadcast_to(pos_row, (tok, tok)))
    return pos_row, jnp.sum((pos_col < pos_row).astype(jnp.int32), axis=0, keepdims=True)


def slots_kernel(per_peer, paired, pos_hbm, len_hbm, _, slot_ref, start_ref, pos_ref, len_ref, sems):
    copies = [
        pltpu.make_async_copy(pos_hbm, pos_ref, sems.at[0]),
        pltpu.make_async_copy(len_hbm, len_ref, sems.at[1]),
    ]
    for copy in copies:
        copy.start()
    devices, tok = pos_ref.shape
    me = lax.axis_index("dcp")
    rows = (SPAN + 1) * per_peer
    window = (me - SPAN) * per_peer + lax.broadcasted_iota(jnp.int32, (rows, tok), 0)
    lane = lax.broadcasted_iota(jnp.int32, (per_peer, LANES), 1)
    copies[0].wait()

    def slots_from(device):
        pos_row, rank = rank_of(pos_ref, device)
        slot = (pos_row % tok).astype(F32)
        column = jnp.sum(jnp.where(rank == window, slot, 0.0), axis=1, keepdims=True)
        slots = jnp.zeros((per_peer, LANES), F32)
        for block in range(SPAN + 1):
            slots = jnp.where(lane == block, column[block * per_peer : (block + 1) * per_peer], slots)
        return slots

    if devices <= 16:
        for source in range(devices):
            device = source ^ me if paired else source
            slot_ref[source * per_peer : (source + 1) * per_peer, :] = slots_from(device)
    else:

        @pl.loop(0, devices)
        def _(source):
            slot_ref[pl.ds(source * per_peer, per_peer), :] = slots_from(source)

    copies[1].wait()
    q_pos = me * tok + lax.broadcasted_iota(jnp.int32, start_ref.shape, 1) % tok
    q_start = jnp.zeros(start_ref.shape, jnp.int32)
    end = jnp.int32(0)
    for doc in range(len_ref.shape[0]):
        end = end + len_ref[doc]
        q_start = jnp.where(q_pos >= end, end, q_start)
    start_ref[...] = q_start


def pack_kernel(
    per_peer, paired, pos_hbm, q_hbm, k_hbm, v_hbm, g_hbm, *rest
):
    out_refs = rest[:-6]
    pos_ref, q_ref, k_ref, v_ref, g_ref, sems = rest[-6:]
    sources = (pos_hbm, k_hbm, v_hbm, q_hbm, g_hbm)
    targets = (pos_ref, k_ref, v_ref, q_ref, g_ref)
    copies = [
        pltpu.make_async_copy(source, target, sems.at[i])
        for i, (source, target) in enumerate(zip(sources, targets))
    ]
    for copy in copies:
        copy.start()
    tok, width = q_ref.shape
    head = k_ref.shape[1]
    me = lax.axis_index("dcp")
    want = lax.broadcasted_iota(jnp.int32, (tok, tok), 0)
    if paired:
        want = ((want // per_peer) ^ me) * per_peer + want % per_peer

    def put(first, rows):
        rows = rows.astype(BF16)
        step = tok // len(out_refs)
        for i, out_ref in enumerate(out_refs):
            out_ref[:, first : first + rows.shape[1]] = rows[i * step : (i + 1) * step]

    copies[0].wait()
    rank = rank_of(pos_ref, me)[1]
    copies[1].wait()
    copies[2].wait()
    for block in range(SPAN + 1):
        perm = (rank == want + (block - SPAN) * per_peer).astype(BF16)
        first = 2 * width + 2 * head * block
        put(first, dot(perm, k_ref[...], ((1,), (0,))))
        put(first + head, dot(perm, v_ref[...], ((1,), (0,))))
    perm = (rank == want).astype(BF16)
    copies[3].wait()
    put(0, dot(perm, q_ref[...], ((1,), (0,))))
    copies[4].wait()
    put(width, dot(perm, g_ref[...], ((1,), (0,))))


def attend_kernel(width, head, pieces, start_ref, slot_ref, *refs):
    in_refs = refs[:pieces]
    key_ref, value_ref, prob_ref, ds_ref, own_ref, *part_refs = refs[pieces:]
    tok = key_ref.shape[0] // (SPAN + 1)
    heads = width // head
    me = lax.axis_index("dcp")
    scale = 1.0 / math.sqrt(head)
    factor = scale * math.log2(math.e)
    base = 2 * width
    slots = slot_ref[...]
    target = lax.broadcasted_iota(jnp.int32, (tok, tok), 1).astype(F32)

    def arrived(first, last):
        return jnp.concatenate([ref[:, first:last] for ref in in_refs], axis=0)

    keys, values = [], []
    place = None
    for block in range(SPAN + 1):
        place = (slots[:, block : block + 1] == target).astype(BF16)
        first = base + 2 * head * block
        both = dot(place, arrived(first, first + 2 * head), ((0,), (0,))).astype(BF16)
        keys.append(both[:, :head])
        values.append(both[:, head:])
    key = jnp.concatenate(keys, axis=0)
    value = jnp.concatenate(values, axis=0)
    key_ref[...] = key
    value_ref[...] = value
    queries = dot(place, arrived(0, width), ((0,), (0,))).astype(BF16)
    grads = dot(place, arrived(width, base), ((0,), (0,))).astype(BF16)

    pairs = 2
    cols = pairs * tok
    window = (SPAN + 1) * tok
    lane = lax.broadcasted_iota(jnp.int32, (1, cols), 1)
    q_pos = me * tok + lane % tok
    q_start = start_ref[:1, :]
    k_pos = (me - SPAN) * tok + lax.broadcasted_iota(jnp.int32, (window, cols), 0)
    allowed = (k_pos >= q_start) & (k_pos <= q_pos)

    key_grad = jnp.zeros((window, head), F32)
    value_grad = jnp.zeros((window, head), F32)
    for first in range(0, heads, pairs):
        spans = [slice(h * head, (h + 1) * head) for h in range(first, first + pairs)]
        q_two = jnp.concatenate([queries[:, s] for s in spans], axis=0)
        g_two = jnp.concatenate([grads[:, s] for s in spans], axis=0)
        scores = jnp.where(allowed, dot(key, q_two, ((1,), (1,))), NEG)
        top = jnp.max(scores, axis=0, keepdims=True)
        weights = jnp.exp2((scores - top) * factor)
        inverse = 1.0 / jnp.sum(weights, axis=0, keepdims=True)
        prob = weights * inverse
        prob_low = prob.astype(BF16)
        grad_prob = dot(value, g_two, ((1,), (1,)))
        delta = jnp.sum(prob * grad_prob, axis=0, keepdims=True)
        grad_score = (prob * (grad_prob - delta)).astype(BF16)
        value_grad += dot(prob_low, g_two, ((1,), (0,)))
        key_grad += dot(grad_score, q_two, ((1,), (0,)))
        prob_ref[:, first * tok : (first + pairs) * tok] = prob_low
        ds_ref[:, first * tok : (first + pairs) * tok] = grad_score
    key_grad = key_grad * scale
    own_ref[:, :head] = key_grad[SPAN * tok :, :]
    own_ref[:, head:] = value_grad[SPAN * tok :, :]
    for offset in range(1, SPAN + 1):
        rows = slice((SPAN - offset) * tok, (SPAN - offset + 1) * tok)
        part_refs[offset - 1][:, :head] = key_grad[rows, :].astype(BF16)
        part_refs[offset - 1][:, head:] = value_grad[rows, :].astype(BF16)


def output_kernel(key_ref, value_ref, prob_ref, ds_ref, attn_ref, dq_ref):
    tok, width = attn_ref.shape
    head = key_ref.shape[1]
    scale = 1.0 / math.sqrt(head)
    pairs = 2
    for first in range(0, width // head, pairs):
        cols = slice(first * tok, (first + pairs) * tok)
        out_t = dot(value_ref[...], prob_ref[:, cols], ((0,), (0,)))
        dq_t = dot(key_ref[...], ds_ref[:, cols], ((0,), (0,))) * scale
        for i in range(pairs):
            s = slice((first + i) * head, (first + i + 1) * head)
            attn_ref[:, s] = jnp.transpose(out_t[:, i * tok : (i + 1) * tok]).astype(BF16)
            dq_ref[:, s] = jnp.transpose(dq_t[:, i * tok : (i + 1) * tok]).astype(BF16)


def per_device(query, key, value, grad_out, loader_pos, doc_lengths):
    tok, width = query.shape
    head = key.shape[1]
    devices = lax.axis_size("dcp")
    per_peer = tok // devices
    vmem = pl.BlockSpec(memory_space=pltpu.VMEM)
    params = pltpu.CompilerParams(vmem_limit_bytes=48 << 20)
    hbm = pl.BlockSpec(memory_space=pltpu.HBM)
    total = 2 * width + 2 * head * (SPAN + 1)
    paired = devices <= 16 and devices & (devices - 1) == 0
    pieces = devices if paired else 1
    positions = pltpu.with_memory_space_constraint(loader_pos.reshape(devices, tok), pltpu.HBM)
    lengths = pltpu.with_memory_space_constraint(doc_lengths, pltpu.HBM)
    sides = [pltpu.with_memory_space_constraint(x, pltpu.HBM) for x in (query, key, value, grad_out)]
    *packed, = pl.pallas_call(
        functools.partial(pack_kernel, per_peer, paired),
        out_shape=[jax.ShapeDtypeStruct((tok // pieces, total), BF16)] * pieces,
        in_specs=[hbm] * 5,
        out_specs=[vmem] * pieces,
        scratch_shapes=[
            pltpu.VMEM((devices, tok), jnp.int32),
            pltpu.VMEM(query.shape, BF16),
            pltpu.VMEM(key.shape, BF16),
            pltpu.VMEM(value.shape, BF16),
            pltpu.VMEM(grad_out.shape, BF16),
            pltpu.SemaphoreType.DMA((5,)),
        ],
        compiler_params=params,
        name="pack",
    )(positions, *sides)
    slots, starts = pl.pallas_call(
        functools.partial(slots_kernel, per_peer, paired),
        out_shape=[
            jax.ShapeDtypeStruct((tok, LANES), F32),
            jax.ShapeDtypeStruct((8, 2 * tok), jnp.int32),
        ],
        in_specs=[hbm, hbm, pl.BlockSpec(memory_space=pl.ANY)],
        out_specs=[vmem] * 2,
        scratch_shapes=[
            pltpu.VMEM((devices, tok), jnp.int32),
            pltpu.SMEM(doc_lengths.shape, jnp.int32),
            pltpu.SemaphoreType.DMA((2,)),
        ],
        compiler_params=params,
        name="slots",
    )(positions, lengths, packed[0])
    if paired:
        for step in range(1, devices):
            partners = [(source, source ^ step) for source in range(devices)]
            packed[step] = lax.ppermute(packed[step], "dcp", partners)
    else:
        packed = [lax.all_to_all(packed[0], "dcp", split_axis=0, concat_axis=0, tiled=True)]
    wide = jax.ShapeDtypeStruct((tok, width), BF16)
    rows = (SPAN + 1) * tok
    seen = jax.ShapeDtypeStruct((rows, head), BF16)
    square = jax.ShapeDtypeStruct((rows, tok * width // head), BF16)
    part = jax.ShapeDtypeStruct((tok, 2 * head), BF16)
    keys, values, probs, grad_scores, summed, *parts = pl.pallas_call(
        functools.partial(attend_kernel, width, head, pieces),
        out_shape=[seen, seen, square, square, jax.ShapeDtypeStruct((tok, 2 * head), F32)] + [part] * SPAN,
        in_specs=[vmem] * (2 + pieces),
        out_specs=[vmem] * (5 + SPAN),
        compiler_params=params,
        name="attend",
    )(starts, slots, *packed)
    attn_out, dquery = pl.pallas_call(
        output_kernel,
        out_shape=[wide, wide],
        in_specs=[vmem] * 4,
        out_specs=[vmem] * 2,
        compiler_params=params,
        name="outputs",
    )(keys, values, probs, grad_scores)
    for offset in range(SPAN, 0, -1):
        pairs = [(source, source - offset) for source in range(offset, devices)]
        summed = summed + lax.ppermute(parts[offset - 1], "dcp", pairs).astype(F32)
    return attn_out, dquery, summed[:, :head].astype(BF16), summed[:, head:].astype(BF16)


def solution(mesh):
    rows = P(("rep", "dcp"), None)
    return jax.shard_map(
        per_device,
        mesh=mesh,
        in_specs=(rows, rows, rows, rows, P("rep"), P("rep")),
        out_specs=(rows, rows, rows, rows),
        check_vma=False,
    )
```

time: 48.9 us -> 47.5 us (0.971)
  the two profiles are of different devices: /device:TPU:14 before, /device:TPU:20 now
where the time goes in v5:
time: 47.5 us; the launch traced here: 47.2 us
  starting transfers between devices  18.8 us (40%)
  waiting for transfers between devices  18.7 us (39%)
  Pallas kernels  8.31 us (17%)
  between operations  0.72 us (2%)
  local copies, waits for them, and re-layouts  0.63 us (1%)
    ppermute x7, waiting for transfers between devices, per_device(): packed[step] = lax.ppermute(packed[step], 'dcp', partners)  15.3 us
    ppermute x7, starting transfers between devices, per_device(): packed[step] = lax.ppermute(packed[step], 'dcp', partners)  9.4 us
    ppermute x5, starting transfers between devices, per_device(): summed = summed + lax.ppermute(parts[offset - 1], 'dcp', pairs).astype(F32)  9.36 us
    pallas_call x1, Pallas kernels, per_device(): pl.pallas_call(functools.partial(attend_kernel, width, head, pieces), out...  4.02 us
    ppermute x5, waiting for transfers between devices, per_device(): summed = summed + lax.ppermute(parts[offset - 1], 'dcp', pairs).astype(F32)  3.44 us
    pallas_call x1, Pallas kernels, per_device(): pl.pallas_call(output_kernel, out_shape=[wide, wide], in_specs=[vmem] * 4...  1.68 us
    pallas_call x1, Pallas kernels, per_device(): pl.pallas_call(functools.partial(pack_kernel, per_peer, paired), out_shap...  1.54 us
    pallas_call x1, Pallas kernels, per_device(): pl.pallas_call(functools.partial(slots_kernel, per_peer, paired), out_sha...  1.06 us
  transfers between devices with their start and end apart: 12, of which 6 were waited for; matrix products, arithmetic and copies ran while one was open for 0% of the time, Pallas kernels for 6%

profile of v5, /device:TPU:20, one launch (start us, length us, event | category | flops | bytes accessed | tf_op | source)
XLA Modules:
  0.0 47.2 jit_solution(15186633239014638715)
XLA Ops:
  0.6 1.5 %pack.1 = (bf16[16,3584]{1,0:T(8,128)(2,1)S(1)}, bf16[16,3584]{1,0:T(8,128)(2,1)S(1)}, bf16[16,3584]{1,0:T(8,128)(2,1)S(1)}, bf16[16,3584]{1,0:T(8,128)(2,1)S(1)...) custom-call(s32[8,128]{1,0:T(8,128)} %bitcast.1, ...), custom_call_target="tpu_custom_call" | custom-call | tf_op jit(solution)/shard_map/pack/pallas_call | solution.py:210
  2.2 0.6 %collective-permute-start = (bf16[16,3584]{1,0:T(8,128)(2,1)S(1)}, bf16[16,3584]{1,0:T(8,128)(2,1)S(1)}, u32[]{:S(2)}, u32[]{:S(2)}) collective-permute-start(bf16[16,3584]{1,0:T(8,128)(2,1)S(1)} %get-tuple-element.29), channel_id=1, source_target_pairs={{0,4},{4,0},{8,12},{12,8},{16,20},{20,16},{24,28},{28,24},{1,5},{5... | collective-permute-start | bytes 344072 | tf_op jit(solution)/shard_map/ppermute | solution.py:245
  2.8 1.6 %collective-permute-start.1 = (bf16[16,3584]{1,0:T(8,128)(2,1)S(1)}, bf16[16,3584]{1,0:T(8,128)(2,1)S(1)}, u32[]{:S(2)}, u32[]{:S(2)}) collective-permute-start(bf16[16,3584]{1,0:T(8,128)(2,1)S(1)} %get-tuple-element.30), channel_id=1, source_target_pairs={{0,8},{4,12},{8,0},{12,4},{16,24},{20,28},{24,16},{28,20},{1,9},{5... | collective-permute-start | bytes 344072 | tf_op jit(solution)/shard_map/ppermute | solution.py:245
  4.3 1.4 %collective-permute-start.2 = (bf16[16,3584]{1,0:T(8,128)(2,1)S(1)}, bf16[16,3584]{1,0:T(8,128)(2,1)S(1)}, u32[]{:S(2)}, u32[]{:S(2)}) collective-permute-start(bf16[16,3584]{1,0:T(8,128)(2,1)S(1)} %get-tuple-element.31), channel_id=1, source_target_pairs={{0,12},{4,8},{8,4},{12,0},{16,28},{20,24},{24,20},{28,16},{1,13},{... | collective-permute-start | bytes 344072 | tf_op jit(solution)/shard_map/ppermute | solution.py:245
  5.7 0.3 collective-permute-start.3
  6.1 2.5 %collective-permute-start.4 = (bf16[16,3584]{1,0:T(8,128)(2,1)S(1)}, bf16[16,3584]{1,0:T(8,128)(2,1)S(1)}, u32[]{:S(2)}, u32[]{:S(2)}) collective-permute-start(bf16[16,3584]{1,0:T(8,128)(2,1)S(1)} %get-tuple-element.33), channel_id=1, source_target_pairs={{0,20},{4,16},{8,28},{12,24},{16,4},{20,0},{24,12},{28,8},{1,21},{... | collective-permute-start | bytes 344072 | tf_op jit(solution)/shard_map/ppermute | solution.py:245
  8.6 0.4 collective-permute-start.5
  9.1 2.5 %collective-permute-start.6 = (bf16[16,3584]{1,0:T(8,128)(2,1)S(1)}, bf16[16,3584]{1,0:T(8,128)(2,1)S(1)}, u32[]{:S(2)}, u32[]{:S(2)}) collective-permute-start(bf16[16,3584]{1,0:T(8,128)(2,1)S(1)} %get-tuple-element.35), channel_id=1, source_target_pairs={{0,28},{4,24},{8,20},{12,16},{16,12},{20,8},{24,4},{28,0},{1,29},{... | collective-permute-start | bytes 344072 | tf_op jit(solution)/shard_map/ppermute | solution.py:245
  11.6 1.1 %slots.1 = (f32[128,128]{1,0:T(8,128)S(1)}, s32[8,256]{1,0:T(8,128)S(1)}) custom-call(s32[8,128]{1,0:T(8,128)} %bitcast.2, s32[3]{0:T(128)} %len_hbm.1, bf16[16,3584]{1,0:T(8,128)(2,1)S(1)} %get-tuple-element.26._.refs_0_), custom_call_target="tpu_custom_call" | custom-call | tf_op jit(solution)/shard_map/slots/pallas_call | solution.py:226
  12.7 1.1 %collective-permute-done.3.refs_4_ = bf16[16,3584]{1,0:T(8,128)(2,1)S(1)} collective-permute-done((bf16[16,3584]{1,0:T(8,128)(2,1)S(1)}, bf16[16,3584]{1,0:T(8,128)(2,1)S(1)}, u32[]{:S(2)}, u32[]{:S(2)}) %collective-permute-start.3) | collective-permute-done | bytes 114720 | tf_op jit(solution)/shard_map/ppermute | solution.py:245
  13.7 7.9 %collective-permute-done.4.refs_5_ = bf16[16,3584]{1,0:T(8,128)(2,1)S(1)} collective-permute-done((bf16[16,3584]{1,0:T(8,128)(2,1)S(1)}, bf16[16,3584]{1,0:T(8,128)(2,1)S(1)}, u32[]{:S(2)}, u32[]{:S(2)}) %collective-permute-start.4) | collective-permute-done | bytes 114720 | tf_op jit(solution)/shard_map/ppermute | solution.py:245
  21.6 4.9 %collective-permute-done.5.refs_6_ = bf16[16,3584]{1,0:T(8,128)(2,1)S(1)} collective-permute-done((bf16[16,3584]{1,0:T(8,128)(2,1)S(1)}, bf16[16,3584]{1,0:T(8,128)(2,1)S(1)}, u32[]{:S(2)}, u32[]{:S(2)}) %collective-permute-start.5) | collective-permute-done | bytes 114720 | tf_op jit(solution)/shard_map/ppermute | solution.py:245
  26.5 1.4 %collective-permute-done.6.refs_7_ = bf16[16,3584]{1,0:T(8,128)(2,1)S(1)} collective-permute-done((bf16[16,3584]{1,0:T(8,128)(2,1)S(1)}, bf16[16,3584]{1,0:T(8,128)(2,1)S(1)}, u32[]{:S(2)}, u32[]{:S(2)}) %collective-permute-start.6) | collective-permute-done | bytes 114720 | tf_op jit(solution)/shard_map/ppermute | solution.py:245
  27.9 4.0 %attend.1 = (bf16[768,128]{1,0:T(8,128)(2,1)S(1)}, bf16[768,128]{1,0:T(8,128)(2,1)S(1)}, bf16[768,1024]{1,0:T(8,128)(2,1)S(1)}, bf16[768,1024]{1,0:T(8,128)(2,1)...) custom-call(s32[8,256]{1,0:T(8,128)S(1)} %get-tuple-element.27.start, ...), custom_call_target="tpu_custom_call" | custom-call | tf_op jit(solution)/shard_map/attend/pallas_call | solution.py:253
  32.0 1.3 %collective-permute-start.7 = (bf16[128,256]{1,0:T(8,128)(2,1)S(1)}, bf16[128,256]{1,0:T(8,128)(2,1)S(1)}, u32[]{:S(2)}, u32[]{:S(2)}) collective-permute-start(bf16[128,256]{1,0:T(8,128)(2,1)S(1)} %get-tuple-element.43), channel_id=1, source_target_pairs={{20,0},{24,4},{28,8},{21,1},{25,5},{29,9},{22,2},{26,6},{30,10},{2... | collective-permute-start | bytes 196616 | tf_op jit(solution)/shard_map/ppermute | solution.py:271
  33.3 1.3 %collective-permute-start.8 = (bf16[128,256]{1,0:T(8,128)(2,1)S(1)}, bf16[128,256]{1,0:T(8,128)(2,1)S(1)}, u32[]{:S(2)}, u32[]{:S(2)}) collective-permute-start(bf16[128,256]{1,0:T(8,128)(2,1)S(1)} %get-tuple-element.44), channel_id=1, source_target_pairs={{16,0},{20,4},{24,8},{28,12},{17,1},{21,5},{25,9},{29,13},{18,2},{... | collective-permute-start | bytes 196616 | tf_op jit(solution)/shard_map/ppermute | solution.py:271
  34.6 2.9 %collective-permute-start.9 = (bf16[128,256]{1,0:T(8,128)(2,1)S(1)}, bf16[128,256]{1,0:T(8,128)(2,1)S(1)}, u32[]{:S(2)}, u32[]{:S(2)}) collective-permute-start(bf16[128,256]{1,0:T(8,128)(2,1)S(1)} %get-tuple-element.45), channel_id=1, source_target_pairs={{12,0},{16,4},{20,8},{24,12},{28,16},{13,1},{17,5},{21,9},{25,13},... | collective-permute-start | bytes 196616 | tf_op jit(solution)/shard_map/ppermute | solution.py:271
  37.5 1.9 %collective-permute-start.10 = (bf16[128,256]{1,0:T(8,128)(2,1)S(1)}, bf16[128,256]{1,0:T(8,128)(2,1)S(1)}, u32[]{:S(2)}, u32[]{:S(2)}) collective-permute-start(bf16[128,256]{1,0:T(8,128)(2,1)S(1)} %get-tuple-element.46), channel_id=1, source_target_pairs={{8,0},{12,4},{16,8},{20,12},{24,16},{28,20},{9,1},{13,5},{17,9},{2... | collective-permute-start | bytes 196616 | tf_op jit(solution)/shard_map/ppermute | solution.py:271
  39.4 1.9 %collective-permute-start.11 = (bf16[128,256]{1,0:T(8,128)(2,1)S(1)}, bf16[128,256]{1,0:T(8,128)(2,1)S(1)}, u32[]{:S(2)}, u32[]{:S(2)}) collective-permute-start(bf16[128,256]{1,0:T(8,128)(2,1)S(1)} %get-tuple-element.47), channel_id=1, source_target_pairs={{4,0},{8,4},{12,8},{16,12},{20,16},{24,20},{28,24},{5,1},{9,5},{13... | collective-permute-start | bytes 196616 | tf_op jit(solution)/shard_map/ppermute | solution.py:271
  41.4 1.7 %outputs.1 = (bf16[128,1024]{1,0:T(8,128)(2,1)}, bf16[128,1024]{1,0:T(8,128)(2,1)}) custom-call(bf16[768,128]{1,0:T(8,128)(2,1)S(1)} %get-tuple-element.36.key_ref, bf16[768,128]{1,0:T(8,128)(2,1)S(1)} %get-tuple-element.37.value_ref, bf16[768,1024]{1,0:T(8,128)(2,1)S(1)} %get-tuple-element.38.prob_ref, bf16[768,1024]{1,0:T(8,128)(2,1)S(1)} %get-tuple-element.39.ds_ref), custom_call_target="tpu_custom_call" | custom-call | tf_op jit(solution)/shard_map/outputs/pallas_call | solution.py:261
  43.1 0.6 %collective-permute-done.10 = bf16[128,256]{1,0:T(8,128)(2,1)S(1)} collective-permute-done((bf16[128,256]{1,0:T(8,128)(2,1)S(1)}, bf16[128,256]{1,0:T(8,128)(2,1)S(1)}, u32[]{:S(2)}, u32[]{:S(2)}) %collective-permute-start.10) | collective-permute-done | bytes 65568 | tf_op jit(solution)/shard_map/ppermute | solution.py:271
  43.7 2.8 %collective-permute-done.11 = bf16[128,256]{1,0:T(8,128)(2,1)S(1)} collective-permute-done((bf16[128,256]{1,0:T(8,128)(2,1)S(1)}, bf16[128,256]{1,0:T(8,128)(2,1)S(1)}, u32[]{:S(2)}, u32[]{:S(2)}) %collective-permute-start.11) | collective-permute-done | bytes 65568 | tf_op jit(solution)/shard_map/ppermute | solution.py:271
  46.5 0.1 add_convert_fusion
  46.6 0.6 %fusion = (bf16[128,128]{1,0:T(8,128)(2,1)}, bf16[128,128]{1,0:T(8,128)(2,1)}) fusion(bf16[128,256]{1,0:T(8,128)(2,1)S(1)} %add_convert_fusion), kind=kLoop, calls=%fused_computation.1 | loop fusion | bytes 131072 | tf_op jit(solution)/shard_map/slice | solution.py:272
  (6 shorter events, 0.0 us)
Async XLA Ops:
  2.2 6.4 %collective-permute-start = (bf16[16,3584]{1,0:T(8,128)(2,1)S(1)}, bf16[16,3584]{1,0:T(8,128)(2,1)S(1)}, u32[]{:S(2)}, u32[]{:S(2)}) collective-permute-start(bf16[16,3584]{1,0:T(8,128)(2,1)S(1)} %get-tuple-element.29), channel_id=1, source_target_pairs={{0,4},{4,0},{8,12},{12,8},{16,20},{20,16},{24,28},{28,24},{1,5},{5... | collective-permute-start | bytes 344072 | tf_op jit(solution)/shard_map/ppermute | solution.py:245
  2.8 6.3 %collective-permute-start.1 = (bf16[16,3584]{1,0:T(8,128)(2,1)S(1)}, bf16[16,3584]{1,0:T(8,128)(2,1)S(1)}, u32[]{:S(2)}, u32[]{:S(2)}) collective-permute-start(bf16[16,3584]{1,0:T(8,128)(2,1)S(1)} %get-tuple-element.30), channel_id=1, source_target_pairs={{0,8},{4,12},{8,0},{12,4},{16,24},{20,28},{24,16},{28,20},{1,9},{5... | collective-permute-start | bytes 344072 | tf_op jit(solution)/shard_map/ppermute | solution.py:245
  4.3 8.3 %collective-permute-start.2 = (bf16[16,3584]{1,0:T(8,128)(2,1)S(1)}, bf16[16,3584]{1,0:T(8,128)(2,1)S(1)}, u32[]{:S(2)}, u32[]{:S(2)}) collective-permute-start(bf16[16,3584]{1,0:T(8,128)(2,1)S(1)} %get-tuple-element.31), channel_id=1, source_target_pairs={{0,12},{4,8},{8,4},{12,0},{16,28},{20,24},{24,20},{28,16},{1,13},{... | collective-permute-start | bytes 344072 | tf_op jit(solution)/shard_map/ppermute | solution.py:245
  5.7 8.0 %collective-permute-start.3 = (bf16[16,3584]{1,0:T(8,128)(2,1)S(1)}, bf16[16,3584]{1,0:T(8,128)(2,1)S(1)}, u32[]{:S(2)}, u32[]{:S(2)}) collective-permute-start(bf16[16,3584]{1,0:T(8,128)(2,1)S(1)} %get-tuple-element.32), channel_id=1, source_target_pairs={{0,16},{4,20},{8,24},{12,28},{16,0},{20,4},{24,8},{28,12},{1,17},{... | collective-permute-start | bytes 344072 | tf_op jit(solution)/shard_map/ppermute | solution.py:245
  6.1 15.6 %collective-permute-start.4 = (bf16[16,3584]{1,0:T(8,128)(2,1)S(1)}, bf16[16,3584]{1,0:T(8,128)(2,1)S(1)}, u32[]{:S(2)}, u32[]{:S(2)}) collective-permute-start(bf16[16,3584]{1,0:T(8,128)(2,1)S(1)} %get-tuple-element.33), channel_id=1, source_target_pairs={{0,20},{4,16},{8,28},{12,24},{16,4},{20,0},{24,12},{28,8},{1,21},{... | collective-permute-start | bytes 344072 | tf_op jit(solution)/shard_map/ppermute | solution.py:245
  8.6 17.9 %collective-permute-start.5 = (bf16[16,3584]{1,0:T(8,128)(2,1)S(1)}, bf16[16,3584]{1,0:T(8,128)(2,1)S(1)}, u32[]{:S(2)}, u32[]{:S(2)}) collective-permute-start(bf16[16,3584]{1,0:T(8,128)(2,1)S(1)} %get-tuple-element.34), channel_id=1, source_target_pairs={{0,24},{4,28},{8,16},{12,20},{16,8},{20,12},{24,0},{28,4},{1,25},{... | collective-permute-start | bytes 344072 | tf_op jit(solution)/shard_map/ppermute | solution.py:245
  9.1 18.9 %collective-permute-start.6 = (bf16[16,3584]{1,0:T(8,128)(2,1)S(1)}, bf16[16,3584]{1,0:T(8,128)(2,1)S(1)}, u32[]{:S(2)}, u32[]{:S(2)}) collective-permute-start(bf16[16,3584]{1,0:T(8,128)(2,1)S(1)} %get-tuple-element.35), channel_id=1, source_target_pairs={{0,28},{4,24},{8,20},{12,16},{16,12},{20,8},{24,4},{28,0},{1,29},{... | collective-permute-start | bytes 344072 | tf_op jit(solution)/shard_map/ppermute | solution.py:245
  32.0 11.1 %collective-permute-start.7 = (bf16[128,256]{1,0:T(8,128)(2,1)S(1)}, bf16[128,256]{1,0:T(8,128)(2,1)S(1)}, u32[]{:S(2)}, u32[]{:S(2)}) collective-permute-start(bf16[128,256]{1,0:T(8,128)(2,1)S(1)} %get-tuple-element.43), channel_id=1, source_target_pairs={{20,0},{24,4},{28,8},{21,1},{25,5},{29,9},{22,2},{26,6},{30,10},{2... | collective-permute-start | bytes 196616 | tf_op jit(solution)/shard_map/ppermute | solution.py:271
  33.3 9.8 %collective-permute-start.8 = (bf16[128,256]{1,0:T(8,128)(2,1)S(1)}, bf16[128,256]{1,0:T(8,128)(2,1)S(1)}, u32[]{:S(2)}, u32[]{:S(2)}) collective-permute-start(bf16[128,256]{1,0:T(8,128)(2,1)S(1)} %get-tuple-element.44), channel_id=1, source_target_pairs={{16,0},{20,4},{24,8},{28,12},{17,1},{21,5},{25,9},{29,13},{18,2},{... | collective-permute-start | bytes 196616 | tf_op jit(solution)/shard_map/ppermute | solution.py:271
  34.6 8.5 %collective-permute-start.9 = (bf16[128,256]{1,0:T(8,128)(2,1)S(1)}, bf16[128,256]{1,0:T(8,128)(2,1)S(1)}, u32[]{:S(2)}, u32[]{:S(2)}) collective-permute-start(bf16[128,256]{1,0:T(8,128)(2,1)S(1)} %get-tuple-element.45), channel_id=1, source_target_pairs={{12,0},{16,4},{20,8},{24,12},{28,16},{13,1},{17,5},{21,9},{25,13},... | collective-permute-start | bytes 196616 | tf_op jit(solution)/shard_map/ppermute | solution.py:271
  37.5 6.2 %collective-permute-start.10 = (bf16[128,256]{1,0:T(8,128)(2,1)S(1)}, bf16[128,256]{1,0:T(8,128)(2,1)S(1)}, u32[]{:S(2)}, u32[]{:S(2)}) collective-permute-start(bf16[128,256]{1,0:T(8,128)(2,1)S(1)} %get-tuple-element.46), channel_id=1, source_target_pairs={{8,0},{12,4},{16,8},{20,12},{24,16},{28,20},{9,1},{13,5},{17,9},{2... | collective-permute-start | bytes 196616 | tf_op jit(solution)/shard_map/ppermute | solution.py:271
  39.4 7.1 %collective-permute-start.11 = (bf16[128,256]{1,0:T(8,128)(2,1)S(1)}, bf16[128,256]{1,0:T(8,128)(2,1)S(1)}, u32[]{:S(2)}, u32[]{:S(2)}) collective-permute-start(bf16[128,256]{1,0:T(8,128)(2,1)S(1)} %get-tuple-element.47), channel_id=1, source_target_pairs={{4,0},{8,4},{12,8},{16,12},{20,16},{24,20},{28,24},{5,1},{9,5},{13... | collective-permute-start | bytes 196616 | tf_op jit(solution)/shard_map/ppermute | solution.py:271

commit v6 on v5

--- a/solution.py
+++ b/solution.py
@@ -69,13 +69,28 @@
     start_ref[...] = q_start
 
 
-def pack_kernel(
-    per_peer, paired, pos_hbm, q_hbm, k_hbm, v_hbm, g_hbm, *rest
-):
-    out_refs = rest[:-6]
-    pos_ref, q_ref, k_ref, v_ref, g_ref, sems = rest[-6:]
-    sources = (pos_hbm, k_hbm, v_hbm, q_hbm, g_hbm)
-    targets = (pos_ref, k_ref, v_ref, q_ref, g_ref)
+def order_kernel(pos_hbm, k_hbm, v_hbm, out_ref, pos_ref, k_ref, v_ref, sems):
+    sources, targets = (pos_hbm, k_hbm, v_hbm), (pos_ref, k_ref, v_ref)
+    copies = [
+        pltpu.make_async_copy(source, target, sems.at[i])
+        for i, (source, target) in enumerate(zip(sources, targets))
+    ]
+    for copy in copies:
+        copy.start()
+    tok, head = k_ref.shape
+    copies[0].wait()
+    rank = rank_of(pos_ref, lax.axis_index("dcp"))[1]
+    perm = (rank == lax.broadcasted_iota(jnp.int32, (tok, tok), 0)).astype(BF16)
+    copies[1].wait()
+    out_ref[:, :head] = dot(perm, k_ref[...], ((1,), (0,))).astype(BF16)
+    copies[2].wait()
+    out_ref[:, head:] = dot(perm, v_ref[...], ((1,), (0,))).astype(BF16)
+
+
+def pack_kernel(per_peer, paired, pos_hbm, q_hbm, g_hbm, both_ref, *rest):
+    out_refs = rest[:-4]
+    pos_ref, q_ref, g_ref, sems = rest[-4:]
+    sources, targets = (pos_hbm, q_hbm, g_hbm), (pos_ref, q_ref, g_ref)
     copies = [
         pltpu.make_async_copy(source, target, sems.at[i])
         for i, (source, target) in enumerate(zip(sources, targets))
@@ -83,37 +98,38 @@
     for copy in copies:
         copy.start()
     tok, width = q_ref.shape
-    head = k_ref.shape[1]
+    two = both_ref.shape[1]
     me = lax.axis_index("dcp")
+    step = tok // len(out_refs)
+    near = max(1, len(out_refs) // 2)
     want = lax.broadcasted_iota(jnp.int32, (tok, tok), 0)
+    lane = lax.broadcasted_iota(jnp.int32, (tok, tok), 1)
     if paired:
         want = ((want // per_peer) ^ me) * per_peer + want % per_peer
 
     def put(first, rows):
         rows = rows.astype(BF16)
-        step = tok // len(out_refs)
-        for i, out_ref in enumerate(out_refs):
-            out_ref[:, first : first + rows.shape[1]] = rows[i * step : (i + 1) * step]
-
+        for i in range(rows.shape[0] // step):
+            out_refs[i][:, first : first + rows.shape[1]] = rows[i * step : (i + 1) * step]
+
+    both = both_ref[...]
+    for block in range(SPAN + 1):
+        perm = (lane == want + (block - SPAN) * per_peer)[: near * step].astype(BF16)
+        put(2 * width + two * block, dot(perm, both, ((1,), (0,))))
     copies[0].wait()
     rank = rank_of(pos_ref, me)[1]
+    perm = (rank == want).astype(BF16)
     copies[1].wait()
+    put(0, dot(perm, q_ref[...], ((1,), (0,))))
     copies[2].wait()
-    for block in range(SPAN + 1):
-        perm = (rank == want + (block - SPAN) * per_peer).astype(BF16)
-        first = 2 * width + 2 * head * block
-        put(first, dot(perm, k_ref[...], ((1,), (0,))))
-        put(first + head, dot(perm, v_ref[...], ((1,), (0,))))
-    perm = (rank == want).astype(BF16)
-    copies[3].wait()
-    put(0, dot(perm, q_ref[...], ((1,), (0,))))
-    copies[4].wait()
     put(width, dot(perm, g_ref[...], ((1,), (0,))))
 
 
 def attend_kernel(width, head, pieces, start_ref, slot_ref, *refs):
+    near = max(1, pieces // 2)
+    count = pieces + (near if pieces > 1 else 0)
     in_refs = refs[:pieces]
-    key_ref, value_ref, prob_ref, ds_ref, own_ref, *part_refs = refs[pieces:]
+    key_ref, value_ref, prob_ref, ds_ref, own_ref, *part_refs = refs[count:]
     tok = key_ref.shape[0] // (SPAN + 1)
     heads = width // head
     me = lax.axis_index("dcp")
@@ -126,12 +142,19 @@
     def arrived(first, last):
         return jnp.concatenate([ref[:, first:last] for ref in in_refs], axis=0)
 
+    def window(block):
+        first = base + 2 * head * block
+        parts = [ref[:, first : first + 2 * head] for ref in in_refs[:near]]
+        step = tok // pieces
+        rows = pl.ds(pl.multiple_of(step * jnp.maximum(me - SPAN + block, 0), step), step)
+        parts += [ref[rows, :] for ref in refs[pieces:count]]
+        return jnp.concatenate(parts, axis=0)
+
     keys, values = [], []
     place = None
     for block in range(SPAN + 1):
         place = (slots[:, block : block + 1] == target).astype(BF16)
-        first = base + 2 * head * block
-        both = dot(place, arrived(first, first + 2 * head), ((0,), (0,))).astype(BF16)
+        both = dot(place, window(block), ((0,), (0,))).astype(BF16)
         keys.append(both[:, :head])
         values.append(both[:, head:])
     key = jnp.concatenate(keys, axis=0)
@@ -201,28 +224,49 @@
     vmem = pl.BlockSpec(memory_space=pltpu.VMEM)
     params = pltpu.CompilerParams(vmem_limit_bytes=48 << 20)
     hbm = pl.BlockSpec(memory_space=pltpu.HBM)
-    total = 2 * width + 2 * head * (SPAN + 1)
+    base = 2 * width
+    total = base + 2 * head * (SPAN + 1)
     paired = devices <= 16 and devices & (devices - 1) == 0
     pieces = devices if paired else 1
     positions = pltpu.with_memory_space_constraint(loader_pos.reshape(devices, tok), pltpu.HBM)
     lengths = pltpu.with_memory_space_constraint(doc_lengths, pltpu.HBM)
     sides = [pltpu.with_memory_space_constraint(x, pltpu.HBM) for x in (query, key, value, grad_out)]
+    near = devices // 2
+    widths = [total] * near + [base] * near if paired else [total]
+    ordered = pl.pallas_call(
+        order_kernel,
+        out_shape=jax.ShapeDtypeStruct((tok, 2 * head), BF16),
+        in_specs=[hbm] * 3,
+        out_specs=vmem,
+        scratch_shapes=[
+            pltpu.VMEM((devices, tok), jnp.int32),
+            pltpu.VMEM(key.shape, BF16),
+            pltpu.VMEM(value.shape, BF16),
+            pltpu.SemaphoreType.DMA((3,)),
+        ],
+        compiler_params=params,
+        name="order",
+    )(positions, sides[1], sides[2])
+
+    def swapped(rows, step):
+        return lax.ppermute(rows, "dcp", [(d, d ^ step) for d in range(devices)])
+
+    across = [swapped(ordered, near)] if paired else []
     *packed, = pl.pallas_call(
         functools.partial(pack_kernel, per_peer, paired),
-        out_shape=[jax.ShapeDtypeStruct((tok // pieces, total), BF16)] * pieces,
-        in_specs=[hbm] * 5,
+        out_shape=[jax.ShapeDtypeStruct((tok // pieces, cols), BF16) for cols in widths],
+        in_specs=[hbm, hbm, hbm, vmem],
         out_specs=[vmem] * pieces,
         scratch_shapes=[
             pltpu.VMEM((devices, tok), jnp.int32),
             pltpu.VMEM(query.shape, BF16),
-            pltpu.VMEM(key.shape, BF16),
-            pltpu.VMEM(value.shape, BF16),
             pltpu.VMEM(grad_out.shape, BF16),
-            pltpu.SemaphoreType.DMA((5,)),
+            pltpu.SemaphoreType.DMA((3,)),
         ],
         compiler_params=params,
+        cost_estimate=pl.CostEstimate(flops=1 << 27, bytes_accessed=3 << 20, transcendentals=0),
         name="pack",
-    )(positions, *sides)
+    )(positions, sides[0], sides[3], ordered)
     slots, starts = pl.pallas_call(
         functools.partial(slots_kernel, per_peer, paired),
         out_shape=[
@@ -240,9 +284,12 @@
         name="slots",
     )(positions, lengths, packed[0])
     if paired:
-        for step in range(1, devices):
-            partners = [(source, source ^ step) for source in range(devices)]
-            packed[step] = lax.ppermute(packed[step], "dcp", partners)
+        for step in range(near, devices):
+            packed[step] = swapped(packed[step], step)
+        across[0], *packed[1:near] = lax.optimization_barrier((across[0], *packed[1:near]))
+        across += [swapped(across[0], step) for step in range(1, near)]
+        for step in range(1, near):
+            packed[step] = swapped(packed[step], step)
     else:
         packed = [lax.all_to_all(packed[0], "dcp", split_axis=0, concat_axis=0, tiled=True)]
     wide = jax.ShapeDtypeStruct((tok, width), BF16)
@@ -253,11 +300,11 @@
     keys, values, probs, grad_scores, summed, *parts = pl.pallas_call(
         functools.partial(attend_kernel, width, head, pieces),
         out_shape=[seen, seen, square, square, jax.ShapeDtypeStruct((tok, 2 * head), F32)] + [part] * SPAN,
-        in_specs=[vmem] * (2 + pieces),
+        in_specs=[vmem] * (2 + pieces + len(across)),
         out_specs=[vmem] * (5 + SPAN),
         compiler_params=params,
         name="attend",
-    )(starts, slots, *packed)
+    )(starts, slots, *packed, *across)
     attn_out, dquery = pl.pallas_call(
         output_kernel,
         out_shape=[wide, wide],

time: 47.5 us -> 45.7 us (0.962)
  the two profiles are of different devices: /device:TPU:20 before, /device:TPU:14 now
where the time goes in v6:
time: 45.7 us; the launch traced here: 44.9 us
  starting transfers between devices  27.6 us (60%)
  Pallas kernels  9.34 us (20%)
  waiting for transfers between devices  6.55 us (14%)
  between operations  0.72 us (2%)
  local copies, waits for them, and re-layouts  0.63 us (1%)
    ppermute x11, starting transfers between devices, swapped(): return lax.ppermute(rows, 'dcp', [(d, d ^ step) for d in range(devices)])  18.8 us
    ppermute x5, starting transfers between devices, per_device(): summed = summed + lax.ppermute(parts[offset - 1], 'dcp', pairs).astype(F32)  8.76 us
    pallas_call x1, Pallas kernels, per_device(): pl.pallas_call(functools.partial(attend_kernel, width, head, pieces), out...  4.03 us
    ppermute x5, waiting for transfers between devices, per_device(): summed = summed + lax.ppermute(parts[offset - 1], 'dcp', pairs).astype(F32)  3.44 us
    ppermute x11, waiting for transfers between devices, swapped(): return lax.ppermute(rows, 'dcp', [(d, d ^ step) for d in range(devices)])  3.11 us
    pallas_call x1, Pallas kernels, per_device(): pl.pallas_call(output_kernel, out_shape=[wide, wide], in_specs=[vmem] * 4...  1.68 us
    pallas_call x1, Pallas kernels, per_device(): pl.pallas_call(functools.partial(pack_kernel, per_peer, paired), out_shap...  1.44 us
    pallas_call x1, Pallas kernels, per_device(): pl.pallas_call(order_kernel, out_shape=jax.ShapeDtypeStruct((tok, 2 * hea...  1.13 us
  transfers between devices with their start and end apart: 16, of which 5 were waited for; matrix products, arithmetic and copies ran while one was open for 0% of the time, Pallas kernels for 9%

profile of v6, /device:TPU:14, one launch (start us, length us, event | category | flops | bytes accessed | tf_op | source)
XLA Modules:
  0.0 44.9 jit_solution(10408824580337965321)
XLA Ops:
  0.6 1.1 %order.1.both_ref = bf16[128,256]{1,0:T(8,128)(2,1)S(1)} custom-call(s32[8,128]{1,0:T(8,128)} %bitcast.1, bf16[128,128]{1,0:T(8,128)(2,1)} %k_hbm.1, bf16[128,128]{1,0:T(8,128)(2,1)} %v_hbm.1), custom_call_target="tpu_custom_call" | custom-call | tf_op jit(solution)/shard_map/order/pallas_call | solution.py:236
  1.8 2.7 %collective-permute-start = (bf16[128,256]{1,0:T(8,128)(2,1)S(1)}, bf16[128,256]{1,0:T(8,128)(2,1)S(1)}, u32[]{:S(2)}, u32[]{:S(2)}) collective-permute-start(bf16[128,256]{1,0:T(8,128)(2,1)S(1)} %order.1.both_ref), channel_id=1, source_target_pairs={{0,16},{4,20},{8,24},{12,28},{16,0},{20,4},{24,8},{28,12},{1,17},{... | collective-permute-start | bytes 196616 | tf_op jit(solution)/shard_map/ppermute | solution.py:252
  4.4 1.4 %pack.1 = (bf16[16,3584]{1,0:T(8,128)(2,1)S(1)}, bf16[16,3584]{1,0:T(8,128)(2,1)S(1)}, bf16[16,3584]{1,0:T(8,128)(2,1)S(1)}, bf16[16,3584]{1,0:T(8,128)(2,1)S(1)...) custom-call(s32[8,128]{1,0:T(8,128)} %bitcast.2, ...), custom_call_target="tpu_custom_call" | custom-call | flops 134217728 | bytes 3145728 | tf_op jit(solution)/shard_map/pack/pallas_call | solution.py:255
  6.3 2.5 %collective-permute-start.5 = (bf16[16,2048]{1,0:T(8,128)(2,1)S(1)}, bf16[16,2048]{1,0:T(8,128)(2,1)S(1)}, u32[]{:S(2)}, u32[]{:S(2)}) collective-permute-start(bf16[16,2048]{1,0:T(8,128)(2,1)S(1)} %get-tuple-element.40), channel_id=1, source_target_pairs={{0,20},{4,16},{8,28},{12,24},{16,4},{20,0},{24,12},{28,8},{1,21},{... | collective-permute-start | bytes 196616 | tf_op jit(solution)/shard_map/ppermute | solution.py:252
  8.8 3.0 %collective-permute-start.7 = (bf16[16,2048]{1,0:T(8,128)(2,1)S(1)}, bf16[16,2048]{1,0:T(8,128)(2,1)S(1)}, u32[]{:S(2)}, u32[]{:S(2)}) collective-permute-start(bf16[16,2048]{1,0:T(8,128)(2,1)S(1)} %get-tuple-element.42), channel_id=1, source_target_pairs={{0,28},{4,24},{8,20},{12,16},{16,12},{20,8},{24,4},{28,0},{1,29},{... | collective-permute-start | bytes 196616 | tf_op jit(solution)/shard_map/ppermute | solution.py:252
  11.8 2.2 %collective-permute-start.10 = (bf16[128,256]{1,0:T(8,128)(2,1)S(1)}, bf16[128,256]{1,0:T(8,128)(2,1)S(1)}, u32[]{:S(2)}, u32[]{:S(2)}) collective-permute-start(bf16[128,256]{1,0:T(8,128)(2,1)S(1)} %collective-permute-done.refs_8_), channel_id=1, source_target_pairs={{0,12},{4,8},{8,4},{12,0},{16,28},{20,24},{24,20},{28,16},{1,13},{... | collective-permute-start | bytes 196616 | tf_op jit(solution)/shard_map/ppermute | solution.py:252
  14.0 1.5 %collective-permute-start.1 = (bf16[16,3584]{1,0:T(8,128)(2,1)S(1)}, bf16[16,3584]{1,0:T(8,128)(2,1)S(1)}, u32[]{:S(2)}, u32[]{:S(2)}) collective-permute-start(bf16[16,3584]{1,0:T(8,128)(2,1)S(1)} %get-tuple-element.36), channel_id=1, source_target_pairs={{0,4},{4,0},{8,12},{12,8},{16,20},{20,16},{24,28},{28,24},{1,5},{5... | collective-permute-start | bytes 344072 | tf_op jit(solution)/shard_map/ppermute | solution.py:252
  15.8 3.1 %collective-permute-start.2 = (bf16[16,3584]{1,0:T(8,128)(2,1)S(1)}, bf16[16,3584]{1,0:T(8,128)(2,1)S(1)}, u32[]{:S(2)}, u32[]{:S(2)}) collective-permute-start(bf16[16,3584]{1,0:T(8,128)(2,1)S(1)} %get-tuple-element.37), channel_id=1, source_target_pairs={{0,8},{4,12},{8,0},{12,4},{16,24},{20,28},{24,16},{28,20},{1,9},{5... | collective-permute-start | bytes 344072 | tf_op jit(solution)/shard_map/ppermute | solution.py:252
  18.9 1.0 %collective-permute-start.3 = (bf16[16,3584]{1,0:T(8,128)(2,1)S(1)}, bf16[16,3584]{1,0:T(8,128)(2,1)S(1)}, u32[]{:S(2)}, u32[]{:S(2)}) collective-permute-start(bf16[16,3584]{1,0:T(8,128)(2,1)S(1)} %get-tuple-element.38), channel_id=1, source_target_pairs={{0,12},{4,8},{8,4},{12,0},{16,28},{20,24},{24,20},{28,16},{1,13},{... | collective-permute-start | bytes 344072 | tf_op jit(solution)/shard_map/ppermute | solution.py:252
  19.9 2.0 %collective-permute-start.9 = (bf16[128,256]{1,0:T(8,128)(2,1)S(1)}, bf16[128,256]{1,0:T(8,128)(2,1)S(1)}, u32[]{:S(2)}, u32[]{:S(2)}) collective-permute-start(bf16[128,256]{1,0:T(8,128)(2,1)S(1)} %collective-permute-done.refs_8_), channel_id=1, source_target_pairs={{0,8},{4,12},{8,0},{12,4},{16,24},{20,28},{24,16},{28,20},{1,9},{5... | collective-permute-start | bytes 196616 | tf_op jit(solution)/shard_map/ppermute | solution.py:252
  22.0 0.4 collective-permute-start.8
  22.4 1.1 %slots.1 = (f32[128,128]{1,0:T(8,128)S(1)}, s32[8,256]{1,0:T(8,128)S(1)}) custom-call(s32[8,128]{1,0:T(8,128)} %bitcast.3, s32[3]{0:T(128)} %len_hbm.1, bf16[16,3584]{1,0:T(8,128)(2,1)S(1)} %get-tuple-element.30._.refs_0_), custom_call_target="tpu_custom_call" | custom-call | tf_op jit(solution)/shard_map/slots/pallas_call | solution.py:270
  23.5 2.0 %collective-permute-done.9.refs_10_ = bf16[128,256]{1,0:T(8,128)(2,1)S(1)} collective-permute-done((bf16[128,256]{1,0:T(8,128)(2,1)S(1)}, bf16[128,256]{1,0:T(8,128)(2,1)S(1)}, u32[]{:S(2)}, u32[]{:S(2)}) %collective-permute-start.9) | collective-permute-done | bytes 65568 | tf_op jit(solution)/shard_map/ppermute | solution.py:252
  25.4 0.8 %collective-permute-done.8.refs_9_ = bf16[128,256]{1,0:T(8,128)(2,1)S(1)} collective-permute-done((bf16[128,256]{1,0:T(8,128)(2,1)S(1)}, bf16[128,256]{1,0:T(8,128)(2,1)S(1)}, u32[]{:S(2)}, u32[]{:S(2)}) %collective-permute-start.8) | collective-permute-done | bytes 65568 | tf_op jit(solution)/shard_map/ppermute | solution.py:252
  26.2 4.0 %attend.1 = (bf16[768,128]{1,0:T(8,128)(2,1)S(1)}, bf16[768,128]{1,0:T(8,128)(2,1)S(1)}, bf16[768,1024]{1,0:T(8,128)(2,1)S(1)}, bf16[768,1024]{1,0:T(8,128)(2,1)...) custom-call(s32[8,256]{1,0:T(8,128)S(1)} %get-tuple-element.31.start, ...), custom_call_target="tpu_custom_call" | custom-call | tf_op jit(solution)/shard_map/attend/pallas_call | solution.py:300
  30.3 0.7 %collective-permute-start.11 = (bf16[128,256]{1,0:T(8,128)(2,1)S(1)}, bf16[128,256]{1,0:T(8,128)(2,1)S(1)}, u32[]{:S(2)}, u32[]{:S(2)}) collective-permute-start(bf16[128,256]{1,0:T(8,128)(2,1)S(1)} %get-tuple-element.51), channel_id=1, source_target_pairs={{20,0},{24,4},{28,8},{21,1},{25,5},{29,9},{22,2},{26,6},{30,10},{2... | collective-permute-start | bytes 196616 | tf_op jit(solution)/shard_map/ppermute | solution.py:318
  30.9 1.3 %collective-permute-start.12 = (bf16[128,256]{1,0:T(8,128)(2,1)S(1)}, bf16[128,256]{1,0:T(8,128)(2,1)S(1)}, u32[]{:S(2)}, u32[]{:S(2)}) collective-permute-start(bf16[128,256]{1,0:T(8,128)(2,1)S(1)} %get-tuple-element.52), channel_id=1, source_target_pairs={{16,0},{20,4},{24,8},{28,12},{17,1},{21,5},{25,9},{29,13},{18,2},{... | collective-permute-start | bytes 196616 | tf_op jit(solution)/shard_map/ppermute | solution.py:318
  32.2 3.0 %collective-permute-start.13 = (bf16[128,256]{1,0:T(8,128)(2,1)S(1)}, bf16[128,256]{1,0:T(8,128)(2,1)S(1)}, u32[]{:S(2)}, u32[]{:S(2)}) collective-permute-start(bf16[128,256]{1,0:T(8,128)(2,1)S(1)} %get-tuple-element.53), channel_id=1, source_target_pairs={{12,0},{16,4},{20,8},{24,12},{28,16},{13,1},{17,5},{21,9},{25,13},... | collective-permute-start | bytes 196616 | tf_op jit(solution)/shard_map/ppermute | solution.py:318
  35.2 1.9 %collective-permute-start.14 = (bf16[128,256]{1,0:T(8,128)(2,1)S(1)}, bf16[128,256]{1,0:T(8,128)(2,1)S(1)}, u32[]{:S(2)}, u32[]{:S(2)}) collective-permute-start(bf16[128,256]{1,0:T(8,128)(2,1)S(1)} %get-tuple-element.54), channel_id=1, source_target_pairs={{8,0},{12,4},{16,8},{20,12},{24,16},{28,20},{9,1},{13,5},{17,9},{2... | collective-permute-start | bytes 196616 | tf_op jit(solution)/shard_map/ppermute | solution.py:318
  37.1 1.9 %collective-permute-start.15 = (bf16[128,256]{1,0:T(8,128)(2,1)S(1)}, bf16[128,256]{1,0:T(8,128)(2,1)S(1)}, u32[]{:S(2)}, u32[]{:S(2)}) collective-permute-start(bf16[128,256]{1,0:T(8,128)(2,1)S(1)} %get-tuple-element.55), channel_id=1, source_target_pairs={{4,0},{8,4},{12,8},{16,12},{20,16},{24,20},{28,24},{5,1},{9,5},{13... | collective-permute-start | bytes 196616 | tf_op jit(solution)/shard_map/ppermute | solution.py:318
  39.1 1.7 %outputs.1 = (bf16[128,1024]{1,0:T(8,128)(2,1)}, bf16[128,1024]{1,0:T(8,128)(2,1)}) custom-call(bf16[768,128]{1,0:T(8,128)(2,1)S(1)} %get-tuple-element.44.key_ref, bf16[768,128]{1,0:T(8,128)(2,1)S(1)} %get-tuple-element.45.value_ref, bf16[768,1024]{1,0:T(8,128)(2,1)S(1)} %get-tuple-element.46.prob_ref, bf16[768,1024]{1,0:T(8,128)(2,1)S(1)} %get-tuple-element.47.ds_ref), custom_call_target="tpu_custom_call" | custom-call | tf_op jit(solution)/shard_map/outputs/pallas_call | solution.py:308
  40.8 0.6 %collective-permute-done.14 = bf16[128,256]{1,0:T(8,128)(2,1)S(1)} collective-permute-done((bf16[128,256]{1,0:T(8,128)(2,1)S(1)}, bf16[128,256]{1,0:T(8,128)(2,1)S(1)}, u32[]{:S(2)}, u32[]{:S(2)}) %collective-permute-start.14) | collective-permute-done | bytes 65568 | tf_op jit(solution)/shard_map/ppermute | solution.py:318
  41.4 2.8 %collective-permute-done.15 = bf16[128,256]{1,0:T(8,128)(2,1)S(1)} collective-permute-done((bf16[128,256]{1,0:T(8,128)(2,1)S(1)}, bf16[128,256]{1,0:T(8,128)(2,1)S(1)}, u32[]{:S(2)}, u32[]{:S(2)}) %collective-permute-start.15) | collective-permute-done | bytes 65568 | tf_op jit(solution)/shard_map/ppermute | solution.py:318
  44.3 0.6 %fusion = (bf16[128,128]{1,0:T(8,128)(2,1)}, bf16[128,128]{1,0:T(8,128)(2,1)}) fusion(bf16[128,256]{1,0:T(8,128)(2,1)S(1)} %add_convert_fusion), kind=kLoop, calls=%fused_computation.1 | loop fusion | bytes 131072 | tf_op jit(solution)/shard_map/slice | solution.py:319
  (15 shorter events, 0.8 us)
Async XLA Ops:
  1.8 10.0 %collective-permute-start = (bf16[128,256]{1,0:T(8,128)(2,1)S(1)}, bf16[128,256]{1,0:T(8,128)(2,1)S(1)}, u32[]{:S(2)}, u32[]{:S(2)}) collective-permute-start(bf16[128,256]{1,0:T(8,128)(2,1)S(1)} %order.1.both_ref), channel_id=1, source_target_pairs={{0,16},{4,20},{8,24},{12,28},{16,0},{20,4},{24,8},{28,12},{1,17},{... | collective-permute-start | bytes 196616 | tf_op jit(solution)/shard_map/ppermute | solution.py:252
  5.9 8.1 %collective-permute-start.4 = (bf16[16,2048]{1,0:T(8,128)(2,1)S(1)}, bf16[16,2048]{1,0:T(8,128)(2,1)S(1)}, u32[]{:S(2)}, u32[]{:S(2)}) collective-permute-start(bf16[16,2048]{1,0:T(8,128)(2,1)S(1)} %get-tuple-element.39), channel_id=1, source_target_pairs={{0,16},{4,20},{8,24},{12,28},{16,0},{20,4},{24,8},{28,12},{1,17},{... | collective-permute-start | bytes 196616 | tf_op jit(solution)/shard_map/ppermute | solution.py:252
  6.3 9.6 %collective-permute-start.5 = (bf16[16,2048]{1,0:T(8,128)(2,1)S(1)}, bf16[16,2048]{1,0:T(8,128)(2,1)S(1)}, u32[]{:S(2)}, u32[]{:S(2)}) collective-permute-start(bf16[16,2048]{1,0:T(8,128)(2,1)S(1)} %get-tuple-element.40), channel_id=1, source_target_pairs={{0,20},{4,16},{8,28},{12,24},{16,4},{20,0},{24,12},{28,8},{1,21},{... | collective-permute-start | bytes 196616 | tf_op jit(solution)/shard_map/ppermute | solution.py:252
  8.8 10.1 %collective-permute-start.6 = (bf16[16,2048]{1,0:T(8,128)(2,1)S(1)}, bf16[16,2048]{1,0:T(8,128)(2,1)S(1)}, u32[]{:S(2)}, u32[]{:S(2)}) collective-permute-start(bf16[16,2048]{1,0:T(8,128)(2,1)S(1)} %get-tuple-element.41), channel_id=1, source_target_pairs={{0,24},{4,28},{8,16},{12,20},{16,8},{20,12},{24,0},{28,4},{1,25},{... | collective-permute-start | bytes 196616 | tf_op jit(solution)/shard_map/ppermute | solution.py:252
  8.8 11.1 %collective-permute-start.7 = (bf16[16,2048]{1,0:T(8,128)(2,1)S(1)}, bf16[16,2048]{1,0:T(8,128)(2,1)S(1)}, u32[]{:S(2)}, u32[]{:S(2)}) collective-permute-start(bf16[16,2048]{1,0:T(8,128)(2,1)S(1)} %get-tuple-element.42), channel_id=1, source_target_pairs={{0,28},{4,24},{8,20},{12,16},{16,12},{20,8},{24,4},{28,0},{1,29},{... | collective-permute-start | bytes 196616 | tf_op jit(solution)/shard_map/ppermute | solution.py:252
  11.8 10.2 %collective-permute-start.10 = (bf16[128,256]{1,0:T(8,128)(2,1)S(1)}, bf16[128,256]{1,0:T(8,128)(2,1)S(1)}, u32[]{:S(2)}, u32[]{:S(2)}) collective-permute-start(bf16[128,256]{1,0:T(8,128)(2,1)S(1)} %collective-permute-done.refs_8_), channel_id=1, source_target_pairs={{0,12},{4,8},{8,4},{12,0},{16,28},{20,24},{24,20},{28,16},{1,13},{... | collective-permute-start | bytes 196616 | tf_op jit(solution)/shard_map/ppermute | solution.py:252
  14.0 12.2 %collective-permute-start.1 = (bf16[16,3584]{1,0:T(8,128)(2,1)S(1)}, bf16[16,3584]{1,0:T(8,128)(2,1)S(1)}, u32[]{:S(2)}, u32[]{:S(2)}) collective-permute-start(bf16[16,3584]{1,0:T(8,128)(2,1)S(1)} %get-tuple-element.36), channel_id=1, source_target_pairs={{0,4},{4,0},{8,12},{12,8},{16,20},{20,16},{24,28},{28,24},{1,5},{5... | collective-permute-start | bytes 344072 | tf_op jit(solution)/shard_map/ppermute | solution.py:252
  15.8 10.4 %collective-permute-start.2 = (bf16[16,3584]{1,0:T(8,128)(2,1)S(1)}, bf16[16,3584]{1,0:T(8,128)(2,1)S(1)}, u32[]{:S(2)}, u32[]{:S(2)}) collective-permute-start(bf16[16,3584]{1,0:T(8,128)(2,1)S(1)} %get-tuple-element.37), channel_id=1, source_target_pairs={{0,8},{4,12},{8,0},{12,4},{16,24},{20,28},{24,16},{28,20},{1,9},{5... | collective-permute-start | bytes 344072 | tf_op jit(solution)/shard_map/ppermute | solution.py:252
  18.9 7.3 %collective-permute-start.3 = (bf16[16,3584]{1,0:T(8,128)(2,1)S(1)}, bf16[16,3584]{1,0:T(8,128)(2,1)S(1)}, u32[]{:S(2)}, u32[]{:S(2)}) collective-permute-start(bf16[16,3584]{1,0:T(8,128)(2,1)S(1)} %get-tuple-element.38), channel_id=1, source_target_pairs={{0,12},{4,8},{8,4},{12,0},{16,28},{20,24},{24,20},{28,16},{1,13},{... | collective-permute-start | bytes 344072 | tf_op jit(solution)/shard_map/ppermute | solution.py:252
  19.9 5.5 %collective-permute-start.9 = (bf16[128,256]{1,0:T(8,128)(2,1)S(1)}, bf16[128,256]{1,0:T(8,128)(2,1)S(1)}, u32[]{:S(2)}, u32[]{:S(2)}) collective-permute-start(bf16[128,256]{1,0:T(8,128)(2,1)S(1)} %collective-permute-done.refs_8_), channel_id=1, source_target_pairs={{0,8},{4,12},{8,0},{12,4},{16,24},{20,28},{24,16},{28,20},{1,9},{5... | collective-permute-start | bytes 196616 | tf_op jit(solution)/shard_map/ppermute | solution.py:252
  22.0 4.3 %collective-permute-start.8 = (bf16[128,256]{1,0:T(8,128)(2,1)S(1)}, bf16[128,256]{1,0:T(8,128)(2,1)S(1)}, u32[]{:S(2)}, u32[]{:S(2)}) collective-permute-start(bf16[128,256]{1,0:T(8,128)(2,1)S(1)} %collective-permute-done.refs_8_), channel_id=1, source_target_pairs={{0,4},{4,0},{8,12},{12,8},{16,20},{20,16},{24,28},{28,24},{1,5},{5... | collective-permute-start | bytes 196616 | tf_op jit(solution)/shard_map/ppermute | solution.py:252
  30.3 10.5 %collective-permute-start.11 = (bf16[128,256]{1,0:T(8,128)(2,1)S(1)}, bf16[128,256]{1,0:T(8,128)(2,1)S(1)}, u32[]{:S(2)}, u32[]{:S(2)}) collective-permute-start(bf16[128,256]{1,0:T(8,128)(2,1)S(1)} %get-tuple-element.51), channel_id=1, source_target_pairs={{20,0},{24,4},{28,8},{21,1},{25,5},{29,9},{22,2},{26,6},{30,10},{2... | collective-permute-start | bytes 196616 | tf_op jit(solution)/shard_map/ppermute | solution.py:318
  30.9 9.8 %collective-permute-start.12 = (bf16[128,256]{1,0:T(8,128)(2,1)S(1)}, bf16[128,256]{1,0:T(8,128)(2,1)S(1)}, u32[]{:S(2)}, u32[]{:S(2)}) collective-permute-start(bf16[128,256]{1,0:T(8,128)(2,1)S(1)} %get-tuple-element.52), channel_id=1, source_target_pairs={{16,0},{20,4},{24,8},{28,12},{17,1},{21,5},{25,9},{29,13},{18,2},{... | collective-permute-start | bytes 196616 | tf_op jit(solution)/shard_map/ppermute | solution.py:318
  32.2 8.5 %collective-permute-start.13 = (bf16[128,256]{1,0:T(8,128)(2,1)S(1)}, bf16[128,256]{1,0:T(8,128)(2,1)S(1)}, u32[]{:S(2)}, u32[]{:S(2)}) collective-permute-start(bf16[128,256]{1,0:T(8,128)(2,1)S(1)} %get-tuple-element.53), channel_id=1, source_target_pairs={{12,0},{16,4},{20,8},{24,12},{28,16},{13,1},{17,5},{21,9},{25,13},... | collective-permute-start | bytes 196616 | tf_op jit(solution)/shard_map/ppermute | solution.py:318
  35.2 6.2 %collective-permute-start.14 = (bf16[128,256]{1,0:T(8,128)(2,1)S(1)}, bf16[128,256]{1,0:T(8,128)(2,1)S(1)}, u32[]{:S(2)}, u32[]{:S(2)}) collective-permute-start(bf16[128,256]{1,0:T(8,128)(2,1)S(1)} %get-tuple-element.54), channel_id=1, source_target_pairs={{8,0},{12,4},{16,8},{20,12},{24,16},{28,20},{9,1},{13,5},{17,9},{2... | collective-permute-start | bytes 196616 | tf_op jit(solution)/shard_map/ppermute | solution.py:318
  37.1 7.1 %collective-permute-start.15 = (bf16[128,256]{1,0:T(8,128)(2,1)S(1)}, bf16[128,256]{1,0:T(8,128)(2,1)S(1)}, u32[]{:S(2)}, u32[]{:S(2)}) collective-permute-start(bf16[128,256]{1,0:T(8,128)(2,1)S(1)} %get-tuple-element.55), channel_id=1, source_target_pairs={{4,0},{8,4},{12,8},{16,12},{20,16},{24,20},{28,24},{5,1},{9,5},{13... | collective-permute-start | bytes 196616 | tf_op jit(solution)/shard_map/ppermute | solution.py:318

commit v7 on v5

--- a/solution.py
+++ b/solution.py
@@ -69,51 +69,73 @@
     start_ref[...] = q_start
 
 
-def pack_kernel(
-    per_peer, paired, pos_hbm, q_hbm, k_hbm, v_hbm, g_hbm, *rest
-):
-    out_refs = rest[:-6]
-    pos_ref, q_ref, k_ref, v_ref, g_ref, sems = rest[-6:]
-    sources = (pos_hbm, k_hbm, v_hbm, q_hbm, g_hbm)
-    targets = (pos_ref, k_ref, v_ref, q_ref, g_ref)
+def group_rows(per_peer, paired, tok):
+    want = lax.broadcasted_iota(jnp.int32, (tok, tok), 0)
+    if paired:
+        want = ((want // per_peer) ^ lax.axis_index("dcp")) * per_peer + want % per_peer
+    return want
+
+
+def pack_kernel(per_peer, paired, pos_hbm, k_hbm, v_hbm, q_hbm, g_hbm, *rest):
+    ordered_ref, *out_refs = rest[:-6]
+    *targets, sems = rest[-6:]
     copies = [
         pltpu.make_async_copy(source, target, sems.at[i])
-        for i, (source, target) in enumerate(zip(sources, targets))
+        for i, (source, target) in enumerate(zip((pos_hbm, k_hbm, v_hbm, q_hbm, g_hbm), targets))
     ]
     for copy in copies:
         copy.start()
+    pos_ref, k_ref, v_ref, q_ref, g_ref = targets
     tok, width = q_ref.shape
     head = k_ref.shape[1]
-    me = lax.axis_index("dcp")
-    want = lax.broadcasted_iota(jnp.int32, (tok, tok), 0)
-    if paired:
-        want = ((want // per_peer) ^ me) * per_peer + want % per_peer
-
-    def put(first, rows):
-        rows = rows.astype(BF16)
-        step = tok // len(out_refs)
+    step = tok // len(out_refs)
+    copies[0].wait()
+    rank = rank_of(pos_ref, lax.axis_index("dcp"))[1]
+    perm = (rank == lax.broadcasted_iota(jnp.int32, (tok, tok), 0)).astype(BF16)
+    for side, ref in enumerate((k_ref, v_ref)):
+        copies[1 + side].wait()
+        ordered_ref[:, side * head : (side + 1) * head] = dot(perm, ref[...], ((1,), (0,))).astype(BF16)
+    perm = (rank == group_rows(per_peer, paired, tok)).astype(BF16)
+    for side, ref in enumerate((q_ref, g_ref)):
+        copies[3 + side].wait()
+        rows = dot(perm, ref[...], ((1,), (0,))).astype(BF16)
         for i, out_ref in enumerate(out_refs):
-            out_ref[:, first : first + rows.shape[1]] = rows[i * step : (i + 1) * step]
-
-    copies[0].wait()
-    rank = rank_of(pos_ref, me)[1]
-    copies[1].wait()
-    copies[2].wait()
+            out_ref[:, side * width : (side + 1) * width] = rows[i * step : (i + 1) * step]
+
+
+def near_kernel(per_peer, paired, pairs, *refs):
+    pair_refs, refs = refs[:pairs], refs[pairs:]
+    near = len(refs) // 2
+    step, base = refs[0].shape
+    tok, two = pair_refs[0].shape
+    want = group_rows(per_peer, paired, tok)[: near * step]
+    lane = lax.broadcasted_iota(jnp.int32, want.shape, 1)
+    for i in range(near):
+        refs[near + i][:, :base] = refs[i][...]
     for block in range(SPAN + 1):
-        perm = (rank == want + (block - SPAN) * per_peer).astype(BF16)
-        first = 2 * width + 2 * head * block
-        put(first, dot(perm, k_ref[...], ((1,), (0,))))
-        put(first + head, dot(perm, v_ref[...], ((1,), (0,))))
-    perm = (rank == want).astype(BF16)
-    copies[3].wait()
-    put(0, dot(perm, q_ref[...], ((1,), (0,))))
-    copies[4].wait()
-    put(width, dot(perm, g_ref[...], ((1,), (0,))))
+        perm = (lane == want + (block - SPAN) * per_peer).astype(BF16)
+        for side, ref in enumerate(pair_refs):
+            rows = dot(perm, ref[...], ((1,), (0,))).astype(BF16)
+            first = base + two * (side * (SPAN + 1) + block)
+            for i in range(near):
+                refs[near + i][:, first : first + two] = rows[i * step : (i + 1) * step]
+
+
+def far_kernel(slot_ref, *refs):
+    *in_refs, out_ref = refs
+    rows = jnp.concatenate([ref[...] for ref in in_refs], axis=0)
+    slots = slot_ref[slot_ref.shape[0] - rows.shape[0] :, SPAN : SPAN + 1]
+    target = lax.broadcasted_iota(jnp.int32, (rows.shape[0], out_ref.shape[0]), 1).astype(F32)
+    out_ref[...] = dot((slots == target).astype(BF16), rows, ((0,), (0,))).astype(BF16)
 
 
 def attend_kernel(width, head, pieces, start_ref, slot_ref, *refs):
-    in_refs = refs[:pieces]
-    key_ref, value_ref, prob_ref, ds_ref, own_ref, *part_refs = refs[pieces:]
+    near = max(1, pieces // 2)
+    in_refs = refs[:near]
+    refs = refs[near:]
+    if pieces > near:
+        far_ref, *refs = refs
+    key_ref, value_ref, prob_ref, ds_ref, own_ref, *part_refs = refs
     tok = key_ref.shape[0] // (SPAN + 1)
     heads = width // head
     me = lax.axis_index("dcp")
@@ -126,20 +148,34 @@
     def arrived(first, last):
         return jnp.concatenate([ref[:, first:last] for ref in in_refs], axis=0)
 
+    def window(block):
+        parts = []
+        for side in range(pieces // near):
+            first = base + 2 * head * (side * (SPAN + 1) + block)
+            parts += [ref[:, first : first + 2 * head] for ref in in_refs[:near]]
+        return jnp.concatenate(parts, axis=0)
+
     keys, values = [], []
     place = None
     for block in range(SPAN + 1):
         place = (slots[:, block : block + 1] == target).astype(BF16)
-        first = base + 2 * head * block
-        both = dot(place, arrived(first, first + 2 * head), ((0,), (0,))).astype(BF16)
+        both = dot(place, window(block), ((0,), (0,))).astype(BF16)
         keys.append(both[:, :head])
         values.append(both[:, head:])
     key = jnp.concatenate(keys, axis=0)
     value = jnp.concatenate(values, axis=0)
     key_ref[...] = key
     value_ref[...] = value
-    queries = dot(place, arrived(0, width), ((0,), (0,))).astype(BF16)
-    grads = dot(place, arrived(width, base), ((0,), (0,))).astype(BF16)
+    place = place[: tok // pieces * near]
+
+    def placed(first, last):
+        rows = dot(place, arrived(first, last), ((0,), (0,)))
+        if pieces > near:
+            rows = rows + far_ref[:, first:last].astype(F32)
+        return rows.astype(BF16)
+
+    queries = placed(0, width)
+    grads = placed(width, base)
 
     pairs = 2
     cols = pairs * tok
@@ -201,28 +237,50 @@
     vmem = pl.BlockSpec(memory_space=pltpu.VMEM)
     params = pltpu.CompilerParams(vmem_limit_bytes=48 << 20)
     hbm = pl.BlockSpec(memory_space=pltpu.HBM)
-    total = 2 * width + 2 * head * (SPAN + 1)
+    base = 2 * width
     paired = devices <= 16 and devices & (devices - 1) == 0
     pieces = devices if paired else 1
     positions = pltpu.with_memory_space_constraint(loader_pos.reshape(devices, tok), pltpu.HBM)
     lengths = pltpu.with_memory_space_constraint(doc_lengths, pltpu.HBM)
     sides = [pltpu.with_memory_space_constraint(x, pltpu.HBM) for x in (query, key, value, grad_out)]
-    *packed, = pl.pallas_call(
+    near = max(1, pieces // 2)
+    def swapped(rows, step):
+        return lax.ppermute(rows, "dcp", [(d, d ^ step) for d in range(devices)])
+
+    ordered, *packed = pl.pallas_call(
         functools.partial(pack_kernel, per_peer, paired),
-        out_shape=[jax.ShapeDtypeStruct((tok // pieces, total), BF16)] * pieces,
+        out_shape=[jax.ShapeDtypeStruct((tok, 2 * head), BF16)]
+        + [jax.ShapeDtypeStruct((tok // pieces, base), BF16)] * pieces,
         in_specs=[hbm] * 5,
-        out_specs=[vmem] * pieces,
+        out_specs=[vmem] * (1 + pieces),
         scratch_shapes=[
             pltpu.VMEM((devices, tok), jnp.int32),
-            pltpu.VMEM(query.shape, BF16),
             pltpu.VMEM(key.shape, BF16),
             pltpu.VMEM(value.shape, BF16),
+            pltpu.VMEM(query.shape, BF16),
             pltpu.VMEM(grad_out.shape, BF16),
             pltpu.SemaphoreType.DMA((5,)),
         ],
         compiler_params=params,
         name="pack",
-    )(positions, *sides)
+    )(positions, sides[1], sides[2], sides[0], sides[3])
+    held = [ordered, swapped(ordered, near)] if paired else [ordered]
+    for step in range(near, pieces if paired else 0):
+        packed[step] = swapped(packed[step], step)
+    cols = base + 2 * head * (SPAN + 1) * len(held)
+    packed[:near] = pl.pallas_call(
+        functools.partial(near_kernel, per_peer, paired, len(held)),
+        out_shape=[jax.ShapeDtypeStruct((tok // pieces, cols), BF16)] * near,
+        in_specs=[vmem] * (len(held) + near),
+        out_specs=[vmem] * near,
+        compiler_params=params,
+        name="near",
+    )(*held, *packed[:near])
+    if paired:
+        for step in range(1, near):
+            packed[step] = swapped(packed[step], step)
+    else:
+        packed = [lax.all_to_all(packed[0], "dcp", split_axis=0, concat_axis=0, tiled=True)]
     slots, starts = pl.pallas_call(
         functools.partial(slots_kernel, per_peer, paired),
         out_shape=[
@@ -239,13 +297,18 @@
         compiler_params=params,
         name="slots",
     )(positions, lengths, packed[0])
+    wide = jax.ShapeDtypeStruct((tok, width), BF16)
     if paired:
-        for step in range(1, devices):
-            partners = [(source, source ^ step) for source in range(devices)]
-            packed[step] = lax.ppermute(packed[step], "dcp", partners)
-    else:
-        packed = [lax.all_to_all(packed[0], "dcp", split_axis=0, concat_axis=0, tiled=True)]
-    wide = jax.ShapeDtypeStruct((tok, width), BF16)
+        far = pl.pallas_call(
+            far_kernel,
+            out_shape=jax.ShapeDtypeStruct((tok, base), BF16),
+            in_specs=[vmem] * (1 + pieces - near),
+            out_specs=vmem,
+            compiler_params=params,
+            cost_estimate=pl.CostEstimate(flops=1 << 33, bytes_accessed=1 << 20, transcendentals=0),
+            name="far",
+        )(slots, *packed[near:])
+        packed[near:] = [far]
     rows = (SPAN + 1) * tok
     seen = jax.ShapeDtypeStruct((rows, head), BF16)
     square = jax.ShapeDtypeStruct((rows, tok * width // head), BF16)
@@ -253,7 +316,7 @@
     keys, values, probs, grad_scores, summed, *parts = pl.pallas_call(
         functools.partial(attend_kernel, width, head, pieces),
         out_shape=[seen, seen, square, square, jax.ShapeDtypeStruct((tok, 2 * head), F32)] + [part] * SPAN,
-        in_specs=[vmem] * (2 + pieces),
+        in_specs=[vmem] * (2 + len(packed)),
         out_specs=[vmem] * (5 + SPAN),
         compiler_params=params,
         name="attend",

time: 47.5 us -> 44.8 us (0.943)
  the two profiles are of different devices: /device:TPU:20 before, /device:TPU:14 now
where the time goes in v7:
time: 44.8 us; the launch traced here: 44.2 us
  starting transfers between devices  22.5 us (50%)
  waiting for transfers between devices  11.3 us (25%)
  Pallas kernels  9 us (20%)
  between operations  0.73 us (2%)
  local copies, waits for them, and re-layouts  0.63 us (1%)
    ppermute x8, starting transfers between devices, swapped(): return lax.ppermute(rows, 'dcp', [(d, d ^ step) for d in range(devices)])  12.6 us
    ppermute x5, starting transfers between devices, per_device(): summed = summed + lax.ppermute(parts[offset - 1], 'dcp', pairs).astype(F32)  9.94 us
    ppermute x8, waiting for transfers between devices, swapped(): return lax.ppermute(rows, 'dcp', [(d, d ^ step) for d in range(devices)])  7.71 us
    pallas_call x1, Pallas kernels, per_device(): pl.pallas_call(functools.partial(attend_kernel, width, head, pieces), out...  4.02 us
    ppermute x5, waiting for transfers between devices, per_device(): summed = summed + lax.ppermute(parts[offset - 1], 'dcp', pairs).astype(F32)  3.62 us
    pallas_call x1, Pallas kernels, per_device(): pl.pallas_call(output_kernel, out_shape=[wide, wide], in_specs=[vmem] * 4...  1.69 us
    pallas_call x1, Pallas kernels, per_device(): pl.pallas_call(functools.partial(pack_kernel, per_peer, paired), out_shap...  1.58 us
    pallas_call x1, Pallas kernels, per_device(): pl.pallas_call(functools.partial(slots_kernel, per_peer, paired), out_sha...  1.06 us
  transfers between devices with their start and end apart: 13, of which 9 were waited for; matrix products, arithmetic and copies ran while one was open for 0% of the time, Pallas kernels for 8%

profile of v7, /device:TPU:14, one launch (start us, length us, event | category | flops | bytes accessed | tf_op | source)
XLA Modules:
  0.0 44.2 jit_solution(8438519130214193500)
XLA Ops:
  0.6 1.6 %pack.1 = (bf16[128,256]{1,0:T(8,128)(2,1)S(1)}, bf16[16,2048]{1,0:T(8,128)(2,1)S(1)}, bf16[16,2048]{1,0:T(8,128)(2,1)S(1)}, bf16[16,2048]{1,0:T(8,128)(2,1)S(1)...) custom-call(s32[8,128]{1,0:T(8,128)} %bitcast.1, ...), custom_call_target="tpu_custom_call" | custom-call | tf_op jit(solution)/shard_map/pack/pallas_call | solution.py:250
  2.2 2.7 %collective-permute-start = (bf16[128,256]{1,0:T(8,128)(2,1)S(1)}, bf16[128,256]{1,0:T(8,128)(2,1)S(1)}, u32[]{:S(2)}, u32[]{:S(2)}) collective-permute-start(bf16[128,256]{1,0:T(8,128)(2,1)S(1)} %get-tuple-element.31.refs_0_), channel_id=1, source_target_pairs={{0,16},{4,20},{8,24},{12,28},{16,0},{20,4},{24,8},{28,12},{1,17},{... | collective-permute-start | bytes 196616 | tf_op jit(solution)/shard_map/ppermute | solution.py:248
  4.9 0.3 collective-permute-start.4
  5.2 2.5 %collective-permute-start.5 = (bf16[16,2048]{1,0:T(8,128)(2,1)S(1)}, bf16[16,2048]{1,0:T(8,128)(2,1)S(1)}, u32[]{:S(2)}, u32[]{:S(2)}) collective-permute-start(bf16[16,2048]{1,0:T(8,128)(2,1)S(1)} %get-tuple-element.43), channel_id=1, source_target_pairs={{0,20},{4,16},{8,28},{12,24},{16,4},{20,0},{24,12},{28,8},{1,21},{... | collective-permute-start | bytes 196616 | tf_op jit(solution)/shard_map/ppermute | solution.py:248
  7.7 3.0 %collective-permute-start.7 = (bf16[16,2048]{1,0:T(8,128)(2,1)S(1)}, bf16[16,2048]{1,0:T(8,128)(2,1)S(1)}, u32[]{:S(2)}, u32[]{:S(2)}) collective-permute-start(bf16[16,2048]{1,0:T(8,128)(2,1)S(1)} %get-tuple-element.45), channel_id=1, source_target_pairs={{0,28},{4,24},{8,20},{12,16},{16,12},{20,8},{24,4},{28,0},{1,29},{... | collective-permute-start | bytes 196616 | tf_op jit(solution)/shard_map/ppermute | solution.py:248
  10.7 1.7 %collective-permute-done.refs_1_ = bf16[128,256]{1,0:T(8,128)(2,1)S(1)} collective-permute-done((bf16[128,256]{1,0:T(8,128)(2,1)S(1)}, bf16[128,256]{1,0:T(8,128)(2,1)S(1)}, u32[]{:S(2)}, u32[]{:S(2)}) %collective-permute-start) | collective-permute-done | bytes 65568 | tf_op jit(solution)/shard_map/ppermute | solution.py:248
  12.5 0.3 near.1
  12.8 1.1 %slots.1 = (f32[128,128]{1,0:T(8,128)S(1)}, s32[8,256]{1,0:T(8,128)S(1)}) custom-call(s32[8,128]{1,0:T(8,128)} %bitcast.2, s32[3]{0:T(128)} %len_hbm.1, bf16[16,5120]{1,0:T(8,128)(2,1)S(1)} %get-tuple-element.36._.refs_0_), custom_call_target="tpu_custom_call" | custom-call | tf_op jit(solution)/shard_map/slots/pallas_call | solution.py:284
  13.9 0.7 %collective-permute-done.4.refs_0_ = bf16[16,2048]{1,0:T(8,128)(2,1)S(1)} collective-permute-done((bf16[16,2048]{1,0:T(8,128)(2,1)S(1)}, bf16[16,2048]{1,0:T(8,128)(2,1)S(1)}, u32[]{:S(2)}, u32[]{:S(2)}) %collective-permute-start.4) | collective-permute-done | bytes 65568 | tf_op jit(solution)/shard_map/ppermute | solution.py:248
  14.6 1.2 %collective-permute-start.2 = (bf16[16,5120]{1,0:T(8,128)(2,1)S(1)}, bf16[16,5120]{1,0:T(8,128)(2,1)S(1)}, u32[]{:S(2)}, u32[]{:S(2)}) collective-permute-start(bf16[16,5120]{1,0:T(8,128)(2,1)S(1)} %get-tuple-element.40), channel_id=1, source_target_pairs={{0,8},{4,12},{8,0},{12,4},{16,24},{20,28},{24,16},{28,20},{1,9},{5... | collective-permute-start | bytes 491528 | tf_op jit(solution)/shard_map/ppermute | solution.py:248
  16.0 2.8 %collective-permute-start.3 = (bf16[16,5120]{1,0:T(8,128)(2,1)S(1)}, bf16[16,5120]{1,0:T(8,128)(2,1)S(1)}, u32[]{:S(2)}, u32[]{:S(2)}) collective-permute-start(bf16[16,5120]{1,0:T(8,128)(2,1)S(1)} %get-tuple-element.41), channel_id=1, source_target_pairs={{0,12},{4,8},{8,4},{12,0},{16,28},{20,24},{24,20},{28,16},{1,13},{... | collective-permute-start | bytes 491528 | tf_op jit(solution)/shard_map/ppermute | solution.py:248
  19.0 0.4 far.1.refs_4_
  19.5 1.8 %collective-permute-done.2.refs_2_ = bf16[16,5120]{1,0:T(8,128)(2,1)S(1)} collective-permute-done((bf16[16,5120]{1,0:T(8,128)(2,1)S(1)}, bf16[16,5120]{1,0:T(8,128)(2,1)S(1)}, u32[]{:S(2)}, u32[]{:S(2)}) %collective-permute-start.2) | collective-permute-done | bytes 163872 | tf_op jit(solution)/shard_map/ppermute | solution.py:248
  21.4 2.9 %collective-permute-done.3.refs_3_ = bf16[16,5120]{1,0:T(8,128)(2,1)S(1)} collective-permute-done((bf16[16,5120]{1,0:T(8,128)(2,1)S(1)}, bf16[16,5120]{1,0:T(8,128)(2,1)S(1)}, u32[]{:S(2)}, u32[]{:S(2)}) %collective-permute-start.3) | collective-permute-done | bytes 163872 | tf_op jit(solution)/shard_map/ppermute | solution.py:248
  24.2 4.0 %attend.1 = (bf16[768,128]{1,0:T(8,128)(2,1)S(1)}, bf16[768,128]{1,0:T(8,128)(2,1)S(1)}, bf16[768,1024]{1,0:T(8,128)(2,1)S(1)}, bf16[768,1024]{1,0:T(8,128)(2,1)...) custom-call(s32[8,256]{1,0:T(8,128)S(1)} %get-tuple-element.37.start, ...), custom_call_target="tpu_custom_call" | custom-call | tf_op jit(solution)/shard_map/attend/pallas_call | solution.py:316
  28.3 0.7 %collective-permute-start.8 = (bf16[128,256]{1,0:T(8,128)(2,1)S(1)}, bf16[128,256]{1,0:T(8,128)(2,1)S(1)}, u32[]{:S(2)}, u32[]{:S(2)}) collective-permute-start(bf16[128,256]{1,0:T(8,128)(2,1)S(1)} %get-tuple-element.53), channel_id=1, source_target_pairs={{20,0},{24,4},{28,8},{21,1},{25,5},{29,9},{22,2},{26,6},{30,10},{2... | collective-permute-start | bytes 196616 | tf_op jit(solution)/shard_map/ppermute | solution.py:334
  28.9 1.3 %collective-permute-start.9 = (bf16[128,256]{1,0:T(8,128)(2,1)S(1)}, bf16[128,256]{1,0:T(8,128)(2,1)S(1)}, u32[]{:S(2)}, u32[]{:S(2)}) collective-permute-start(bf16[128,256]{1,0:T(8,128)(2,1)S(1)} %get-tuple-element.54), channel_id=1, source_target_pairs={{16,0},{20,4},{24,8},{28,12},{17,1},{21,5},{25,9},{29,13},{18,2},{... | collective-permute-start | bytes 196616 | tf_op jit(solution)/shard_map/ppermute | solution.py:334
  30.2 4.1 %collective-permute-start.10 = (bf16[128,256]{1,0:T(8,128)(2,1)S(1)}, bf16[128,256]{1,0:T(8,128)(2,1)S(1)}, u32[]{:S(2)}, u32[]{:S(2)}) collective-permute-start(bf16[128,256]{1,0:T(8,128)(2,1)S(1)} %get-tuple-element.55), channel_id=1, source_target_pairs={{12,0},{16,4},{20,8},{24,12},{28,16},{13,1},{17,5},{21,9},{25,13},... | collective-permute-start | bytes 196616 | tf_op jit(solution)/shard_map/ppermute | solution.py:334
  34.4 1.9 %collective-permute-start.11 = (bf16[128,256]{1,0:T(8,128)(2,1)S(1)}, bf16[128,256]{1,0:T(8,128)(2,1)S(1)}, u32[]{:S(2)}, u32[]{:S(2)}) collective-permute-start(bf16[128,256]{1,0:T(8,128)(2,1)S(1)} %get-tuple-element.56), channel_id=1, source_target_pairs={{8,0},{12,4},{16,8},{20,12},{24,16},{28,20},{9,1},{13,5},{17,9},{2... | collective-permute-start | bytes 196616 | tf_op jit(solution)/shard_map/ppermute | solution.py:334
  36.3 1.9 %collective-permute-start.12 = (bf16[128,256]{1,0:T(8,128)(2,1)S(1)}, bf16[128,256]{1,0:T(8,128)(2,1)S(1)}, u32[]{:S(2)}, u32[]{:S(2)}) collective-permute-start(bf16[128,256]{1,0:T(8,128)(2,1)S(1)} %get-tuple-element.57), channel_id=1, source_target_pairs={{4,0},{8,4},{12,8},{16,12},{20,16},{24,20},{28,24},{5,1},{9,5},{13... | collective-permute-start | bytes 196616 | tf_op jit(solution)/shard_map/ppermute | solution.py:334
  38.2 1.7 %outputs.1 = (bf16[128,1024]{1,0:T(8,128)(2,1)}, bf16[128,1024]{1,0:T(8,128)(2,1)}) custom-call(bf16[768,128]{1,0:T(8,128)(2,1)S(1)} %get-tuple-element.46.key_ref, bf16[768,128]{1,0:T(8,128)(2,1)S(1)} %get-tuple-element.47.value_ref, bf16[768,1024]{1,0:T(8,128)(2,1)S(1)} %get-tuple-element.48.prob_ref, bf16[768,1024]{1,0:T(8,128)(2,1)S(1)} %get-tuple-element.49.ds_ref), custom_call_target="tpu_custom_call" | custom-call | tf_op jit(solution)/shard_map/outputs/pallas_call | solution.py:324
  39.9 1.4 %collective-permute-done.11 = bf16[128,256]{1,0:T(8,128)(2,1)S(1)} collective-permute-done((bf16[128,256]{1,0:T(8,128)(2,1)S(1)}, bf16[128,256]{1,0:T(8,128)(2,1)S(1)}, u32[]{:S(2)}, u32[]{:S(2)}) %collective-permute-start.11) | collective-permute-done | bytes 65568 | tf_op jit(solution)/shard_map/ppermute | solution.py:334
  41.3 2.2 %collective-permute-done.12 = bf16[128,256]{1,0:T(8,128)(2,1)S(1)} collective-permute-done((bf16[128,256]{1,0:T(8,128)(2,1)S(1)}, bf16[128,256]{1,0:T(8,128)(2,1)S(1)}, u32[]{:S(2)}, u32[]{:S(2)}) %collective-permute-start.12) | collective-permute-done | bytes 65568 | tf_op jit(solution)/shard_map/ppermute | solution.py:334
  43.6 0.6 %fusion = (bf16[128,128]{1,0:T(8,128)(2,1)}, bf16[128,128]{1,0:T(8,128)(2,1)}) fusion(bf16[128,256]{1,0:T(8,128)(2,1)S(1)} %add_convert_fusion), kind=kLoop, calls=%fused_computation.1 | loop fusion | bytes 131072 | tf_op jit(solution)/shard_map/slice | solution.py:335
  (10 shorter events, 0.7 us)
Async XLA Ops:
  2.2 10.2 %collective-permute-start = (bf16[128,256]{1,0:T(8,128)(2,1)S(1)}, bf16[128,256]{1,0:T(8,128)(2,1)S(1)}, u32[]{:S(2)}, u32[]{:S(2)}) collective-permute-start(bf16[128,256]{1,0:T(8,128)(2,1)S(1)} %get-tuple-element.31.refs_0_), channel_id=1, source_target_pairs={{0,16},{4,20},{8,24},{12,28},{16,0},{20,4},{24,8},{28,12},{1,17},{... | collective-permute-start | bytes 196616 | tf_op jit(solution)/shard_map/ppermute | solution.py:248
  4.9 9.7 %collective-permute-start.4 = (bf16[16,2048]{1,0:T(8,128)(2,1)S(1)}, bf16[16,2048]{1,0:T(8,128)(2,1)S(1)}, u32[]{:S(2)}, u32[]{:S(2)}) collective-permute-start(bf16[16,2048]{1,0:T(8,128)(2,1)S(1)} %get-tuple-element.42), channel_id=1, source_target_pairs={{0,16},{4,20},{8,24},{12,28},{16,0},{20,4},{24,8},{28,12},{1,17},{... | collective-permute-start | bytes 196616 | tf_op jit(solution)/shard_map/ppermute | solution.py:248
  5.2 10.8 %collective-permute-start.5 = (bf16[16,2048]{1,0:T(8,128)(2,1)S(1)}, bf16[16,2048]{1,0:T(8,128)(2,1)S(1)}, u32[]{:S(2)}, u32[]{:S(2)}) collective-permute-start(bf16[16,2048]{1,0:T(8,128)(2,1)S(1)} %get-tuple-element.43), channel_id=1, source_target_pairs={{0,20},{4,16},{8,28},{12,24},{16,4},{20,0},{24,12},{28,8},{1,21},{... | collective-permute-start | bytes 196616 | tf_op jit(solution)/shard_map/ppermute | solution.py:248
  7.7 11.1 %collective-permute-start.6 = (bf16[16,2048]{1,0:T(8,128)(2,1)S(1)}, bf16[16,2048]{1,0:T(8,128)(2,1)S(1)}, u32[]{:S(2)}, u32[]{:S(2)}) collective-permute-start(bf16[16,2048]{1,0:T(8,128)(2,1)S(1)} %get-tuple-element.44), channel_id=1, source_target_pairs={{0,24},{4,28},{8,16},{12,20},{16,8},{20,12},{24,0},{28,4},{1,25},{... | collective-permute-start | bytes 196616 | tf_op jit(solution)/shard_map/ppermute | solution.py:248
  7.7 11.3 %collective-permute-start.7 = (bf16[16,2048]{1,0:T(8,128)(2,1)S(1)}, bf16[16,2048]{1,0:T(8,128)(2,1)S(1)}, u32[]{:S(2)}, u32[]{:S(2)}) collective-permute-start(bf16[16,2048]{1,0:T(8,128)(2,1)S(1)} %get-tuple-element.45), channel_id=1, source_target_pairs={{0,28},{4,24},{8,20},{12,16},{16,12},{20,8},{24,4},{28,0},{1,29},{... | collective-permute-start | bytes 196616 | tf_op jit(solution)/shard_map/ppermute | solution.py:248
  12.7 6.8 %collective-permute-start.1 = (bf16[16,5120]{1,0:T(8,128)(2,1)S(1)}, bf16[16,5120]{1,0:T(8,128)(2,1)S(1)}, u32[]{:S(2)}, u32[]{:S(2)}) collective-permute-start(bf16[16,5120]{1,0:T(8,128)(2,1)S(1)} %get-tuple-element.39), channel_id=1, source_target_pairs={{0,4},{4,0},{8,12},{12,8},{16,20},{20,16},{24,28},{28,24},{1,5},{5... | collective-permute-start | bytes 491528 | tf_op jit(solution)/shard_map/ppermute | solution.py:248
  14.6 6.8 %collective-permute-start.2 = (bf16[16,5120]{1,0:T(8,128)(2,1)S(1)}, bf16[16,5120]{1,0:T(8,128)(2,1)S(1)}, u32[]{:S(2)}, u32[]{:S(2)}) collective-permute-start(bf16[16,5120]{1,0:T(8,128)(2,1)S(1)} %get-tuple-element.40), channel_id=1, source_target_pairs={{0,8},{4,12},{8,0},{12,4},{16,24},{20,28},{24,16},{28,20},{1,9},{5... | collective-permute-start | bytes 491528 | tf_op jit(solution)/shard_map/ppermute | solution.py:248
  16.0 8.2 %collective-permute-start.3 = (bf16[16,5120]{1,0:T(8,128)(2,1)S(1)}, bf16[16,5120]{1,0:T(8,128)(2,1)S(1)}, u32[]{:S(2)}, u32[]{:S(2)}) collective-permute-start(bf16[16,5120]{1,0:T(8,128)(2,1)S(1)} %get-tuple-element.41), channel_id=1, source_target_pairs={{0,12},{4,8},{8,4},{12,0},{16,28},{20,24},{24,20},{28,16},{1,13},{... | collective-permute-start | bytes 491528 | tf_op jit(solution)/shard_map/ppermute | solution.py:248
  28.3 11.7 %collective-permute-start.8 = (bf16[128,256]{1,0:T(8,128)(2,1)S(1)}, bf16[128,256]{1,0:T(8,128)(2,1)S(1)}, u32[]{:S(2)}, u32[]{:S(2)}) collective-permute-start(bf16[128,256]{1,0:T(8,128)(2,1)S(1)} %get-tuple-element.53), channel_id=1, source_target_pairs={{20,0},{24,4},{28,8},{21,1},{25,5},{29,9},{22,2},{26,6},{30,10},{2... | collective-permute-start | bytes 196616 | tf_op jit(solution)/shard_map/ppermute | solution.py:334
  28.9 11.0 %collective-permute-start.9 = (bf16[128,256]{1,0:T(8,128)(2,1)S(1)}, bf16[128,256]{1,0:T(8,128)(2,1)S(1)}, u32[]{:S(2)}, u32[]{:S(2)}) collective-permute-start(bf16[128,256]{1,0:T(8,128)(2,1)S(1)} %get-tuple-element.54), channel_id=1, source_target_pairs={{16,0},{20,4},{24,8},{28,12},{17,1},{21,5},{25,9},{29,13},{18,2},{... | collective-permute-start | bytes 196616 | tf_op jit(solution)/shard_map/ppermute | solution.py:334
  30.2 9.7 %collective-permute-start.10 = (bf16[128,256]{1,0:T(8,128)(2,1)S(1)}, bf16[128,256]{1,0:T(8,128)(2,1)S(1)}, u32[]{:S(2)}, u32[]{:S(2)}) collective-permute-start(bf16[128,256]{1,0:T(8,128)(2,1)S(1)} %get-tuple-element.55), channel_id=1, source_target_pairs={{12,0},{16,4},{20,8},{24,12},{28,16},{13,1},{17,5},{21,9},{25,13},... | collective-permute-start | bytes 196616 | tf_op jit(solution)/shard_map/ppermute | solution.py:334
  34.4 6.9 %collective-permute-start.11 = (bf16[128,256]{1,0:T(8,128)(2,1)S(1)}, bf16[128,256]{1,0:T(8,128)(2,1)S(1)}, u32[]{:S(2)}, u32[]{:S(2)}) collective-permute-start(bf16[128,256]{1,0:T(8,128)(2,1)S(1)} %get-tuple-element.56), channel_id=1, source_target_pairs={{8,0},{12,4},{16,8},{20,12},{24,16},{28,20},{9,1},{13,5},{17,9},{2... | collective-permute-start | bytes 196616 | tf_op jit(solution)/shard_map/ppermute | solution.py:334
  36.3 7.2 %collective-permute-start.12 = (bf16[128,256]{1,0:T(8,128)(2,1)S(1)}, bf16[128,256]{1,0:T(8,128)(2,1)S(1)}, u32[]{:S(2)}, u32[]{:S(2)}) collective-permute-start(bf16[128,256]{1,0:T(8,128)(2,1)S(1)} %get-tuple-element.57), channel_id=1, source_target_pairs={{4,0},{8,4},{12,8},{16,12},{20,16},{24,20},{28,24},{5,1},{9,5},{13... | collective-permute-start | bytes 196616 | tf_op jit(solution)/shard_map/ppermute | solution.py:334

commit v8 on v7

--- a/solution.py
+++ b/solution.py
@@ -26,7 +26,7 @@
     return pos_row, jnp.sum((pos_col < pos_row).astype(jnp.int32), axis=0, keepdims=True)
 
 
-def slots_kernel(per_peer, paired, pos_hbm, len_hbm, _, slot_ref, start_ref, pos_ref, len_ref, sems):
+def slots_kernel(per_peer, paired, pos_hbm, len_hbm, _, place_ref, mask_ref, pos_ref, len_ref, slot_ref, sems):
     copies = [
         pltpu.make_async_copy(pos_hbm, pos_ref, sems.at[0]),
         pltpu.make_async_copy(len_hbm, len_ref, sems.at[1]),
@@ -59,14 +59,21 @@
         def _(source):
             slot_ref[pl.ds(source * per_peer, per_peer), :] = slots_from(source)
 
+    slot = lax.broadcasted_iota(jnp.int32, (tok, tok), 0).astype(F32)
+    arrived = jnp.transpose(slot_ref[...])
+    for block in range(SPAN + 1):
+        rows = slice(block * tok, (block + 1) * tok)
+        place_ref[rows, :] = (arrived[block : block + 1, :] == slot).astype(BF16)
+
     copies[1].wait()
-    q_pos = me * tok + lax.broadcasted_iota(jnp.int32, start_ref.shape, 1) % tok
-    q_start = jnp.zeros(start_ref.shape, jnp.int32)
+    q_pos = me * tok + lax.broadcasted_iota(jnp.int32, (1, tok), 1)
+    q_start = jnp.zeros((1, tok), jnp.int32)
     end = jnp.int32(0)
     for doc in range(len_ref.shape[0]):
         end = end + len_ref[doc]
         q_start = jnp.where(q_pos >= end, end, q_start)
-    start_ref[...] = q_start
+    k_pos = (me - SPAN) * tok + lax.broadcasted_iota(jnp.int32, mask_ref.shape, 0)
+    mask_ref[...] = jnp.where((k_pos >= q_start) & (k_pos <= q_pos), 0.0, NEG)
 
 
 def group_rows(per_peer, paired, tok):
@@ -121,15 +128,14 @@
                 refs[near + i][:, first : first + two] = rows[i * step : (i + 1) * step]
 
 
-def far_kernel(slot_ref, *refs):
+def far_kernel(place_ref, *refs):
     *in_refs, out_ref = refs
     rows = jnp.concatenate([ref[...] for ref in in_refs], axis=0)
-    slots = slot_ref[slot_ref.shape[0] - rows.shape[0] :, SPAN : SPAN + 1]
-    target = lax.broadcasted_iota(jnp.int32, (rows.shape[0], out_ref.shape[0]), 1).astype(F32)
-    out_ref[...] = dot((slots == target).astype(BF16), rows, ((0,), (0,))).astype(BF16)
-
-
-def attend_kernel(width, head, pieces, start_ref, slot_ref, *refs):
+    rows = jnp.concatenate([jnp.zeros_like(rows), rows], axis=0)
+    out_ref[...] = dot(place_ref[SPAN * out_ref.shape[0] :, :], rows, ((1,), (0,))).astype(BF16)
+
+
+def attend_kernel(width, head, pieces, mask_ref, place_ref, *refs):
     near = max(1, pieces // 2)
     in_refs = refs[:near]
     refs = refs[near:]
@@ -142,9 +148,6 @@
     scale = 1.0 / math.sqrt(head)
     factor = scale * math.log2(math.e)
     base = 2 * width
-    slots = slot_ref[...]
-    target = lax.broadcasted_iota(jnp.int32, (tok, tok), 1).astype(F32)
-
     def arrived(first, last):
         return jnp.concatenate([ref[:, first:last] for ref in in_refs], axis=0)
 
@@ -156,43 +159,37 @@
         return jnp.concatenate(parts, axis=0)
 
     keys, values = [], []
-    place = None
     for block in range(SPAN + 1):
-        place = (slots[:, block : block + 1] == target).astype(BF16)
-        both = dot(place, window(block), ((0,), (0,))).astype(BF16)
+        place = place_ref[block * tok : (block + 1) * tok, :]
+        both = dot(place, window(block), ((1,), (0,))).astype(BF16)
         keys.append(both[:, :head])
         values.append(both[:, head:])
     key = jnp.concatenate(keys, axis=0)
     value = jnp.concatenate(values, axis=0)
     key_ref[...] = key
     value_ref[...] = value
-    place = place[: tok // pieces * near]
-
     def placed(first, last):
-        rows = dot(place, arrived(first, last), ((0,), (0,)))
-        if pieces > near:
-            rows = rows + far_ref[:, first:last].astype(F32)
-        return rows.astype(BF16)
+        rows = arrived(first, last)
+        if pieces == near:
+            return dot(place_ref[SPAN * tok :, :], rows, ((1,), (0,))).astype(BF16)
+        rows = jnp.concatenate([rows, jnp.zeros_like(rows)], axis=0)
+        rows = dot(place_ref[SPAN * tok :, :], rows, ((1,), (0,)))
+        return (rows + far_ref[:, first:last].astype(F32)).astype(BF16)
 
     queries = placed(0, width)
     grads = placed(width, base)
 
-    pairs = 2
-    cols = pairs * tok
-    window = (SPAN + 1) * tok
-    lane = lax.broadcasted_iota(jnp.int32, (1, cols), 1)
-    q_pos = me * tok + lane % tok
-    q_start = start_ref[:1, :]
-    k_pos = (me - SPAN) * tok + lax.broadcasted_iota(jnp.int32, (window, cols), 0)
-    allowed = (k_pos >= q_start) & (k_pos <= q_pos)
-
-    key_grad = jnp.zeros((window, head), F32)
-    value_grad = jnp.zeros((window, head), F32)
+    pairs = 4
+    window_rows = (SPAN + 1) * tok
+    mask = jnp.concatenate([mask_ref[...]] * pairs, axis=1)
+
+    key_grad = jnp.zeros((window_rows, head), F32)
+    value_grad = jnp.zeros((window_rows, head), F32)
     for first in range(0, heads, pairs):
         spans = [slice(h * head, (h + 1) * head) for h in range(first, first + pairs)]
         q_two = jnp.concatenate([queries[:, s] for s in spans], axis=0)
         g_two = jnp.concatenate([grads[:, s] for s in spans], axis=0)
-        scores = jnp.where(allowed, dot(key, q_two, ((1,), (1,))), NEG)
+        scores = dot(key, q_two, ((1,), (1,))) + mask
         top = jnp.max(scores, axis=0, keepdims=True)
         weights = jnp.exp2((scores - top) * factor)
         inverse = 1.0 / jnp.sum(weights, axis=0, keepdims=True)
@@ -218,7 +215,7 @@
     tok, width = attn_ref.shape
     head = key_ref.shape[1]
     scale = 1.0 / math.sqrt(head)
-    pairs = 2
+    pairs = 4
     for first in range(0, width // head, pairs):
         cols = slice(first * tok, (first + pairs) * tok)
         out_t = dot(value_ref[...], prob_ref[:, cols], ((0,), (0,)))
@@ -281,17 +278,18 @@
             packed[step] = swapped(packed[step], step)
     else:
         packed = [lax.all_to_all(packed[0], "dcp", split_axis=0, concat_axis=0, tiled=True)]
-    slots, starts = pl.pallas_call(
+    places, mask = pl.pallas_call(
         functools.partial(slots_kernel, per_peer, paired),
         out_shape=[
-            jax.ShapeDtypeStruct((tok, LANES), F32),
-            jax.ShapeDtypeStruct((8, 2 * tok), jnp.int32),
+            jax.ShapeDtypeStruct(((SPAN + 1) * tok, tok), BF16),
+            jax.ShapeDtypeStruct(((SPAN + 1) * tok, tok), F32),
         ],
         in_specs=[hbm, hbm, pl.BlockSpec(memory_space=pl.ANY)],
         out_specs=[vmem] * 2,
         scratch_shapes=[
             pltpu.VMEM((devices, tok), jnp.int32),
             pltpu.SMEM(doc_lengths.shape, jnp.int32),
+            pltpu.VMEM((tok, LANES), F32),
             pltpu.SemaphoreType.DMA((2,)),
         ],
         compiler_params=params,
@@ -307,7 +305,7 @@
             compiler_params=params,
             cost_estimate=pl.CostEstimate(flops=1 << 33, bytes_accessed=1 << 20, transcendentals=0),
             name="far",
-        )(slots, *packed[near:])
+        )(places, *packed[near:])
         packed[near:] = [far]
     rows = (SPAN + 1) * tok
     seen = jax.ShapeDtypeStruct((rows, head), BF16)
@@ -320,7 +318,7 @@
         out_specs=[vmem] * (5 + SPAN),
         compiler_params=params,
         name="attend",
-    )(starts, slots, *packed)
+    )(mask, places, *packed)
     attn_out, dquery = pl.pallas_call(
         output_kernel,
         out_shape=[wide, wide],

time: 44.8 us -> 44.1 us (0.984)
  Pallas kernels: 9 us -> 8.12 us
    pallas_call x1, Pallas kernels: 4.02 us -> 3.29 us  [per_device(): pl.pallas_call(functools.partial(attend_kernel, width, head, pieces), out...]
  transfers between devices with their start and end apart: 13 -> 13, of which waited for: 9 -> 9; matrix products, arithmetic and copies ran while one was open for 0% -> 0% of each run, Pallas kernels for 8% -> 7%
where the time goes in v8:
time: 44.1 us; the launch traced here: 43.6 us
  starting transfers between devices  22.3 us (51%)
  waiting for transfers between devices  11.7 us (27%)
  Pallas kernels  8.12 us (18%)
  between operations  0.73 us (2%)
  local copies, waits for them, and re-layouts  0.63 us (1%)
    ppermute x8, starting transfers between devices, swapped(): return lax.ppermute(rows, 'dcp', [(d, d ^ step) for d in range(devices)])  12.6 us
    ppermute x5, starting transfers between devices, per_device(): summed = summed + lax.ppermute(parts[offset - 1], 'dcp', pairs).astype(F32)  9.79 us
    ppermute x8, waiting for transfers between devices, swapped(): return lax.ppermute(rows, 'dcp', [(d, d ^ step) for d in range(devices)])  7.82 us
    ppermute x5, waiting for transfers between devices, per_device(): summed = summed + lax.ppermute(parts[offset - 1], 'dcp', pairs).astype(F32)  3.89 us
    pallas_call x1, Pallas kernels, per_device(): pl.pallas_call(functools.partial(attend_kernel, width, head, pieces), out...  3.29 us
    pallas_call x1, Pallas kernels, per_device(): pl.pallas_call(functools.partial(pack_kernel, per_peer, paired), out_shap...  1.58 us
    pallas_call x1, Pallas kernels, per_device(): pl.pallas_call(output_kernel, out_shape=[wide, wide], in_specs=[vmem] * 4...  1.51 us
    pallas_call x1, Pallas kernels, per_device(): pl.pallas_call(functools.partial(slots_kernel, per_peer, paired), out_sha...  1.21 us
  transfers between devices with their start and end apart: 13, of which 9 were waited for; matrix products, arithmetic and copies ran while one was open for 0% of the time, Pallas kernels for 7%

profile of v8, /device:TPU:14, one launch (start us, length us, event | category | flops | bytes accessed | tf_op | source)
XLA Modules:
  0.0 43.6 jit_solution(419536882412309006)
XLA Ops:
  0.6 1.6 %pack.1 = (bf16[128,256]{1,0:T(8,128)(2,1)S(1)}, bf16[16,2048]{1,0:T(8,128)(2,1)S(1)}, bf16[16,2048]{1,0:T(8,128)(2,1)S(1)}, bf16[16,2048]{1,0:T(8,128)(2,1)S(1)...) custom-call(s32[8,128]{1,0:T(8,128)} %bitcast.1, ...), custom_call_target="tpu_custom_call" | custom-call | tf_op jit(solution)/shard_map/pack/pallas_call | solution.py:247
  2.2 2.7 %collective-permute-start = (bf16[128,256]{1,0:T(8,128)(2,1)S(1)}, bf16[128,256]{1,0:T(8,128)(2,1)S(1)}, u32[]{:S(2)}, u32[]{:S(2)}) collective-permute-start(bf16[128,256]{1,0:T(8,128)(2,1)S(1)} %get-tuple-element.31.refs_0_), channel_id=1, source_target_pairs={{0,16},{4,20},{8,24},{12,28},{16,0},{20,4},{24,8},{28,12},{1,17},{... | collective-permute-start | bytes 196616 | tf_op jit(solution)/shard_map/ppermute | solution.py:245
  4.9 0.3 collective-permute-start.4
  5.2 2.5 %collective-permute-start.5 = (bf16[16,2048]{1,0:T(8,128)(2,1)S(1)}, bf16[16,2048]{1,0:T(8,128)(2,1)S(1)}, u32[]{:S(2)}, u32[]{:S(2)}) collective-permute-start(bf16[16,2048]{1,0:T(8,128)(2,1)S(1)} %get-tuple-element.43), channel_id=1, source_target_pairs={{0,20},{4,16},{8,28},{12,24},{16,4},{20,0},{24,12},{28,8},{1,21},{... | collective-permute-start | bytes 196616 | tf_op jit(solution)/shard_map/ppermute | solution.py:245
  7.7 3.0 %collective-permute-start.7 = (bf16[16,2048]{1,0:T(8,128)(2,1)S(1)}, bf16[16,2048]{1,0:T(8,128)(2,1)S(1)}, u32[]{:S(2)}, u32[]{:S(2)}) collective-permute-start(bf16[16,2048]{1,0:T(8,128)(2,1)S(1)} %get-tuple-element.45), channel_id=1, source_target_pairs={{0,28},{4,24},{8,20},{12,16},{16,12},{20,8},{24,4},{28,0},{1,29},{... | collective-permute-start | bytes 196616 | tf_op jit(solution)/shard_map/ppermute | solution.py:245
  10.7 1.7 %collective-permute-done.refs_1_ = bf16[128,256]{1,0:T(8,128)(2,1)S(1)} collective-permute-done((bf16[128,256]{1,0:T(8,128)(2,1)S(1)}, bf16[128,256]{1,0:T(8,128)(2,1)S(1)}, u32[]{:S(2)}, u32[]{:S(2)}) %collective-permute-start) | collective-permute-done | bytes 65568 | tf_op jit(solution)/shard_map/ppermute | solution.py:245
  12.8 1.2 %slots.1 = (bf16[768,128]{1,0:T(8,128)(2,1)S(1)}, f32[768,128]{1,0:T(8,128)S(1)}) custom-call(s32[8,128]{1,0:T(8,128)} %bitcast.2, s32[3]{0:T(128)} %len_hbm.1, bf16[16,5120]{1,0:T(8,128)(2,1)S(1)} %get-tuple-element.36._.refs_0_), custom_call_target="tpu_custom_call" | custom-call | tf_op jit(solution)/shard_map/slots/pallas_call | solution.py:281
  14.0 0.5 %collective-permute-done.4.refs_0_ = bf16[16,2048]{1,0:T(8,128)(2,1)S(1)} collective-permute-done((bf16[16,2048]{1,0:T(8,128)(2,1)S(1)}, bf16[16,2048]{1,0:T(8,128)(2,1)S(1)}, u32[]{:S(2)}, u32[]{:S(2)}) %collective-permute-start.4) | collective-permute-done | bytes 65568 | tf_op jit(solution)/shard_map/ppermute | solution.py:245
  14.6 1.2 %collective-permute-start.2 = (bf16[16,5120]{1,0:T(8,128)(2,1)S(1)}, bf16[16,5120]{1,0:T(8,128)(2,1)S(1)}, u32[]{:S(2)}, u32[]{:S(2)}) collective-permute-start(bf16[16,5120]{1,0:T(8,128)(2,1)S(1)} %get-tuple-element.40), channel_id=1, source_target_pairs={{0,8},{4,12},{8,0},{12,4},{16,24},{20,28},{24,16},{28,20},{1,9},{5... | collective-permute-start | bytes 491528 | tf_op jit(solution)/shard_map/ppermute | solution.py:245
  16.0 2.8 %collective-permute-start.3 = (bf16[16,5120]{1,0:T(8,128)(2,1)S(1)}, bf16[16,5120]{1,0:T(8,128)(2,1)S(1)}, u32[]{:S(2)}, u32[]{:S(2)}) collective-permute-start(bf16[16,5120]{1,0:T(8,128)(2,1)S(1)} %get-tuple-element.41), channel_id=1, source_target_pairs={{0,12},{4,8},{8,4},{12,0},{16,28},{20,24},{24,20},{28,16},{1,13},{... | collective-permute-start | bytes 491528 | tf_op jit(solution)/shard_map/ppermute | solution.py:245
  19.0 0.3 far.1.refs_4_
  19.3 0.3 collective-permute-done.1.refs_1_
  19.6 1.8 %collective-permute-done.2.refs_2_ = bf16[16,5120]{1,0:T(8,128)(2,1)S(1)} collective-permute-done((bf16[16,5120]{1,0:T(8,128)(2,1)S(1)}, bf16[16,5120]{1,0:T(8,128)(2,1)S(1)}, u32[]{:S(2)}, u32[]{:S(2)}) %collective-permute-start.2) | collective-permute-done | bytes 163872 | tf_op jit(solution)/shard_map/ppermute | solution.py:245
  21.4 3.0 %collective-permute-done.3.refs_3_ = bf16[16,5120]{1,0:T(8,128)(2,1)S(1)} collective-permute-done((bf16[16,5120]{1,0:T(8,128)(2,1)S(1)}, bf16[16,5120]{1,0:T(8,128)(2,1)S(1)}, u32[]{:S(2)}, u32[]{:S(2)}) %collective-permute-start.3) | collective-permute-done | bytes 163872 | tf_op jit(solution)/shard_map/ppermute | solution.py:245
  24.4 3.3 %attend.1 = (bf16[768,128]{1,0:T(8,128)(2,1)S(1)}, bf16[768,128]{1,0:T(8,128)(2,1)S(1)}, bf16[768,1024]{1,0:T(8,128)(2,1)S(1)}, bf16[768,1024]{1,0:T(8,128)(2,1)...) custom-call(f32[768,128]{1,0:T(8,128)S(1)} %get-tuple-element.37.mas, ...), custom_call_target="tpu_custom_call" | custom-call | tf_op jit(solution)/shard_map/attend/pallas_call | solution.py:314
  27.7 0.7 %collective-permute-start.8 = (bf16[128,256]{1,0:T(8,128)(2,1)S(1)}, bf16[128,256]{1,0:T(8,128)(2,1)S(1)}, u32[]{:S(2)}, u32[]{:S(2)}) collective-permute-start(bf16[128,256]{1,0:T(8,128)(2,1)S(1)} %get-tuple-element.53), channel_id=1, source_target_pairs={{20,0},{24,4},{28,8},{21,1},{25,5},{29,9},{22,2},{26,6},{30,10},{2... | collective-permute-start | bytes 196616 | tf_op jit(solution)/shard_map/ppermute | solution.py:332
  28.3 1.3 %collective-permute-start.9 = (bf16[128,256]{1,0:T(8,128)(2,1)S(1)}, bf16[128,256]{1,0:T(8,128)(2,1)S(1)}, u32[]{:S(2)}, u32[]{:S(2)}) collective-permute-start(bf16[128,256]{1,0:T(8,128)(2,1)S(1)} %get-tuple-element.54), channel_id=1, source_target_pairs={{16,0},{20,4},{24,8},{28,12},{17,1},{21,5},{25,9},{29,13},{18,2},{... | collective-permute-start | bytes 196616 | tf_op jit(solution)/shard_map/ppermute | solution.py:332
  29.6 4.0 %collective-permute-start.10 = (bf16[128,256]{1,0:T(8,128)(2,1)S(1)}, bf16[128,256]{1,0:T(8,128)(2,1)S(1)}, u32[]{:S(2)}, u32[]{:S(2)}) collective-permute-start(bf16[128,256]{1,0:T(8,128)(2,1)S(1)} %get-tuple-element.55), channel_id=1, source_target_pairs={{12,0},{16,4},{20,8},{24,12},{28,16},{13,1},{17,5},{21,9},{25,13},... | collective-permute-start | bytes 196616 | tf_op jit(solution)/shard_map/ppermute | solution.py:332
  33.6 1.9 %collective-permute-start.11 = (bf16[128,256]{1,0:T(8,128)(2,1)S(1)}, bf16[128,256]{1,0:T(8,128)(2,1)S(1)}, u32[]{:S(2)}, u32[]{:S(2)}) collective-permute-start(bf16[128,256]{1,0:T(8,128)(2,1)S(1)} %get-tuple-element.56), channel_id=1, source_target_pairs={{8,0},{12,4},{16,8},{20,12},{24,16},{28,20},{9,1},{13,5},{17,9},{2... | collective-permute-start | bytes 196616 | tf_op jit(solution)/shard_map/ppermute | solution.py:332
  35.6 1.9 %collective-permute-start.12 = (bf16[128,256]{1,0:T(8,128)(2,1)S(1)}, bf16[128,256]{1,0:T(8,128)(2,1)S(1)}, u32[]{:S(2)}, u32[]{:S(2)}) collective-permute-start(bf16[128,256]{1,0:T(8,128)(2,1)S(1)} %get-tuple-element.57), channel_id=1, source_target_pairs={{4,0},{8,4},{12,8},{16,12},{20,16},{24,20},{28,24},{5,1},{9,5},{13... | collective-permute-start | bytes 196616 | tf_op jit(solution)/shard_map/ppermute | solution.py:332
  37.5 1.5 %outputs.1 = (bf16[128,1024]{1,0:T(8,128)(2,1)}, bf16[128,1024]{1,0:T(8,128)(2,1)}) custom-call(bf16[768,128]{1,0:T(8,128)(2,1)S(1)} %get-tuple-element.46.key_ref, bf16[768,128]{1,0:T(8,128)(2,1)S(1)} %get-tuple-element.47.value_ref, bf16[768,1024]{1,0:T(8,128)(2,1)S(1)} %get-tuple-element.48.prob_ref, bf16[768,1024]{1,0:T(8,128)(2,1)S(1)} %get-tuple-element.49.ds_ref), custom_call_target="tpu_custom_call" | custom-call | tf_op jit(solution)/shard_map/outputs/pallas_call | solution.py:322
  39.0 1.6 %collective-permute-done.11 = bf16[128,256]{1,0:T(8,128)(2,1)S(1)} collective-permute-done((bf16[128,256]{1,0:T(8,128)(2,1)S(1)}, bf16[128,256]{1,0:T(8,128)(2,1)S(1)}, u32[]{:S(2)}, u32[]{:S(2)}) %collective-permute-start.11) | collective-permute-done | bytes 65568 | tf_op jit(solution)/shard_map/ppermute | solution.py:332
  40.6 2.3 %collective-permute-done.12 = bf16[128,256]{1,0:T(8,128)(2,1)S(1)} collective-permute-done((bf16[128,256]{1,0:T(8,128)(2,1)S(1)}, bf16[128,256]{1,0:T(8,128)(2,1)S(1)}, u32[]{:S(2)}, u32[]{:S(2)}) %collective-permute-start.12) | collective-permute-done | bytes 65568 | tf_op jit(solution)/shard_map/ppermute | solution.py:332
  43.0 0.6 %fusion = (bf16[128,128]{1,0:T(8,128)(2,1)}, bf16[128,128]{1,0:T(8,128)(2,1)}) fusion(bf16[128,256]{1,0:T(8,128)(2,1)S(1)} %add_convert_fusion), kind=kLoop, calls=%fused_computation.1 | loop fusion | bytes 131072 | tf_op jit(solution)/shard_map/slice | solution.py:333
  (10 shorter events, 0.8 us)
Async XLA Ops:
  2.2 10.2 %collective-permute-start = (bf16[128,256]{1,0:T(8,128)(2,1)S(1)}, bf16[128,256]{1,0:T(8,128)(2,1)S(1)}, u32[]{:S(2)}, u32[]{:S(2)}) collective-permute-start(bf16[128,256]{1,0:T(8,128)(2,1)S(1)} %get-tuple-element.31.refs_0_), channel_id=1, source_target_pairs={{0,16},{4,20},{8,24},{12,28},{16,0},{20,4},{24,8},{28,12},{1,17},{... | collective-permute-start | bytes 196616 | tf_op jit(solution)/shard_map/ppermute | solution.py:245
  4.9 9.7 %collective-permute-start.4 = (bf16[16,2048]{1,0:T(8,128)(2,1)S(1)}, bf16[16,2048]{1,0:T(8,128)(2,1)S(1)}, u32[]{:S(2)}, u32[]{:S(2)}) collective-permute-start(bf16[16,2048]{1,0:T(8,128)(2,1)S(1)} %get-tuple-element.42), channel_id=1, source_target_pairs={{0,16},{4,20},{8,24},{12,28},{16,0},{20,4},{24,8},{28,12},{1,17},{... | collective-permute-start | bytes 196616 | tf_op jit(solution)/shard_map/ppermute | solution.py:245
  5.2 10.8 %collective-permute-start.5 = (bf16[16,2048]{1,0:T(8,128)(2,1)S(1)}, bf16[16,2048]{1,0:T(8,128)(2,1)S(1)}, u32[]{:S(2)}, u32[]{:S(2)}) collective-permute-start(bf16[16,2048]{1,0:T(8,128)(2,1)S(1)} %get-tuple-element.43), channel_id=1, source_target_pairs={{0,20},{4,16},{8,28},{12,24},{16,4},{20,0},{24,12},{28,8},{1,21},{... | collective-permute-start | bytes 196616 | tf_op jit(solution)/shard_map/ppermute | solution.py:245
  7.7 11.1 %collective-permute-start.6 = (bf16[16,2048]{1,0:T(8,128)(2,1)S(1)}, bf16[16,2048]{1,0:T(8,128)(2,1)S(1)}, u32[]{:S(2)}, u32[]{:S(2)}) collective-permute-start(bf16[16,2048]{1,0:T(8,128)(2,1)S(1)} %get-tuple-element.44), channel_id=1, source_target_pairs={{0,24},{4,28},{8,16},{12,20},{16,8},{20,12},{24,0},{28,4},{1,25},{... | collective-permute-start | bytes 196616 | tf_op jit(solution)/shard_map/ppermute | solution.py:245
  7.7 11.3 %collective-permute-start.7 = (bf16[16,2048]{1,0:T(8,128)(2,1)S(1)}, bf16[16,2048]{1,0:T(8,128)(2,1)S(1)}, u32[]{:S(2)}, u32[]{:S(2)}) collective-permute-start(bf16[16,2048]{1,0:T(8,128)(2,1)S(1)} %get-tuple-element.45), channel_id=1, source_target_pairs={{0,28},{4,24},{8,20},{12,16},{16,12},{20,8},{24,4},{28,0},{1,29},{... | collective-permute-start | bytes 196616 | tf_op jit(solution)/shard_map/ppermute | solution.py:245
  12.7 6.8 %collective-permute-start.1 = (bf16[16,5120]{1,0:T(8,128)(2,1)S(1)}, bf16[16,5120]{1,0:T(8,128)(2,1)S(1)}, u32[]{:S(2)}, u32[]{:S(2)}) collective-permute-start(bf16[16,5120]{1,0:T(8,128)(2,1)S(1)} %get-tuple-element.39), channel_id=1, source_target_pairs={{0,4},{4,0},{8,12},{12,8},{16,20},{20,16},{24,28},{28,24},{1,5},{5... | collective-permute-start | bytes 491528 | tf_op jit(solution)/shard_map/ppermute | solution.py:245
  14.6 6.8 %collective-permute-start.2 = (bf16[16,5120]{1,0:T(8,128)(2,1)S(1)}, bf16[16,5120]{1,0:T(8,128)(2,1)S(1)}, u32[]{:S(2)}, u32[]{:S(2)}) collective-permute-start(bf16[16,5120]{1,0:T(8,128)(2,1)S(1)} %get-tuple-element.40), channel_id=1, source_target_pairs={{0,8},{4,12},{8,0},{12,4},{16,24},{20,28},{24,16},{28,20},{1,9},{5... | collective-permute-start | bytes 491528 | tf_op jit(solution)/shard_map/ppermute | solution.py:245
  16.0 8.3 %collective-permute-start.3 = (bf16[16,5120]{1,0:T(8,128)(2,1)S(1)}, bf16[16,5120]{1,0:T(8,128)(2,1)S(1)}, u32[]{:S(2)}, u32[]{:S(2)}) collective-permute-start(bf16[16,5120]{1,0:T(8,128)(2,1)S(1)} %get-tuple-element.41), channel_id=1, source_target_pairs={{0,12},{4,8},{8,4},{12,0},{16,28},{20,24},{24,20},{28,16},{1,13},{... | collective-permute-start | bytes 491528 | tf_op jit(solution)/shard_map/ppermute | solution.py:245
  27.7 11.3 %collective-permute-start.8 = (bf16[128,256]{1,0:T(8,128)(2,1)S(1)}, bf16[128,256]{1,0:T(8,128)(2,1)S(1)}, u32[]{:S(2)}, u32[]{:S(2)}) collective-permute-start(bf16[128,256]{1,0:T(8,128)(2,1)S(1)} %get-tuple-element.53), channel_id=1, source_target_pairs={{20,0},{24,4},{28,8},{21,1},{25,5},{29,9},{22,2},{26,6},{30,10},{2... | collective-permute-start | bytes 196616 | tf_op jit(solution)/shard_map/ppermute | solution.py:332
  28.3 10.7 %collective-permute-start.9 = (bf16[128,256]{1,0:T(8,128)(2,1)S(1)}, bf16[128,256]{1,0:T(8,128)(2,1)S(1)}, u32[]{:S(2)}, u32[]{:S(2)}) collective-permute-start(bf16[128,256]{1,0:T(8,128)(2,1)S(1)} %get-tuple-element.54), channel_id=1, source_target_pairs={{16,0},{20,4},{24,8},{28,12},{17,1},{21,5},{25,9},{29,13},{18,2},{... | collective-permute-start | bytes 196616 | tf_op jit(solution)/shard_map/ppermute | solution.py:332
  29.6 9.4 %collective-permute-start.10 = (bf16[128,256]{1,0:T(8,128)(2,1)S(1)}, bf16[128,256]{1,0:T(8,128)(2,1)S(1)}, u32[]{:S(2)}, u32[]{:S(2)}) collective-permute-start(bf16[128,256]{1,0:T(8,128)(2,1)S(1)} %get-tuple-element.55), channel_id=1, source_target_pairs={{12,0},{16,4},{20,8},{24,12},{28,16},{13,1},{17,5},{21,9},{25,13},... | collective-permute-start | bytes 196616 | tf_op jit(solution)/shard_map/ppermute | solution.py:332
  33.6 6.9 %collective-permute-start.11 = (bf16[128,256]{1,0:T(8,128)(2,1)S(1)}, bf16[128,256]{1,0:T(8,128)(2,1)S(1)}, u32[]{:S(2)}, u32[]{:S(2)}) collective-permute-start(bf16[128,256]{1,0:T(8,128)(2,1)S(1)} %get-tuple-element.56), channel_id=1, source_target_pairs={{8,0},{12,4},{16,8},{20,12},{24,16},{28,20},{9,1},{13,5},{17,9},{2... | collective-permute-start | bytes 196616 | tf_op jit(solution)/shard_map/ppermute | solution.py:332
  35.6 7.3 %collective-permute-start.12 = (bf16[128,256]{1,0:T(8,128)(2,1)S(1)}, bf16[128,256]{1,0:T(8,128)(2,1)S(1)}, u32[]{:S(2)}, u32[]{:S(2)}) collective-permute-start(bf16[128,256]{1,0:T(8,128)(2,1)S(1)} %get-tuple-element.57), channel_id=1, source_target_pairs={{4,0},{8,4},{12,8},{16,12},{20,16},{24,20},{28,24},{5,1},{9,5},{13... | collective-permute-start | bytes 196616 | tf_op jit(solution)/shard_map/ppermute | solution.py:332

commit v9 on v8

--- a/solution.py
+++ b/solution.py
@@ -26,7 +26,7 @@
     return pos_row, jnp.sum((pos_col < pos_row).astype(jnp.int32), axis=0, keepdims=True)
 
 
-def slots_kernel(per_peer, paired, pos_hbm, len_hbm, _, place_ref, mask_ref, pos_ref, len_ref, slot_ref, sems):
+def slots_kernel(per_peer, paired, pos_hbm, len_hbm, _, place_ref, mask_ref, live_ref, pos_ref, len_ref, slot_ref, sems):
     copies = [
         pltpu.make_async_copy(pos_hbm, pos_ref, sems.at[0]),
         pltpu.make_async_copy(len_hbm, len_ref, sems.at[1]),
@@ -69,9 +69,12 @@
     q_pos = me * tok + lax.broadcasted_iota(jnp.int32, (1, tok), 1)
     q_start = jnp.zeros((1, tok), jnp.int32)
     end = jnp.int32(0)
+    earliest = jnp.int32(0)
     for doc in range(len_ref.shape[0]):
         end = end + len_ref[doc]
         q_start = jnp.where(q_pos >= end, end, q_start)
+        earliest = jnp.where(me * tok >= end, end, earliest)
+    live_ref[...] = jnp.full(live_ref.shape, me - earliest // tok + 1, jnp.int32).astype(F32)
     k_pos = (me - SPAN) * tok + lax.broadcasted_iota(jnp.int32, mask_ref.shape, 0)
     mask_ref[...] = jnp.where((k_pos >= q_start) & (k_pos <= q_pos), 0.0, NEG)
 
@@ -135,7 +138,7 @@
     out_ref[...] = dot(place_ref[SPAN * out_ref.shape[0] :, :], rows, ((1,), (0,))).astype(BF16)
 
 
-def attend_kernel(width, head, pieces, mask_ref, place_ref, *refs):
+def attend_kernel(width, head, pieces, live_ref, mask_ref, place_ref, *refs):
     near = max(1, pieces // 2)
     in_refs = refs[:near]
     refs = refs[near:]
@@ -158,16 +161,6 @@
             parts += [ref[:, first : first + 2 * head] for ref in in_refs[:near]]
         return jnp.concatenate(parts, axis=0)
 
-    keys, values = [], []
-    for block in range(SPAN + 1):
-        place = place_ref[block * tok : (block + 1) * tok, :]
-        both = dot(place, window(block), ((1,), (0,))).astype(BF16)
-        keys.append(both[:, :head])
-        values.append(both[:, head:])
-    key = jnp.concatenate(keys, axis=0)
-    value = jnp.concatenate(values, axis=0)
-    key_ref[...] = key
-    value_ref[...] = value
     def placed(first, last):
         rows = arrived(first, last)
         if pieces == near:
@@ -179,36 +172,54 @@
     queries = placed(0, width)
     grads = placed(width, base)
 
-    pairs = 4
-    window_rows = (SPAN + 1) * tok
-    mask = jnp.concatenate([mask_ref[...]] * pairs, axis=1)
-
-    key_grad = jnp.zeros((window_rows, head), F32)
-    value_grad = jnp.zeros((window_rows, head), F32)
-    for first in range(0, heads, pairs):
-        spans = [slice(h * head, (h + 1) * head) for h in range(first, first + pairs)]
-        q_two = jnp.concatenate([queries[:, s] for s in spans], axis=0)
-        g_two = jnp.concatenate([grads[:, s] for s in spans], axis=0)
-        scores = dot(key, q_two, ((1,), (1,))) + mask
-        top = jnp.max(scores, axis=0, keepdims=True)
-        weights = jnp.exp2((scores - top) * factor)
-        inverse = 1.0 / jnp.sum(weights, axis=0, keepdims=True)
-        prob = weights * inverse
-        prob_low = prob.astype(BF16)
-        grad_prob = dot(value, g_two, ((1,), (1,)))
-        delta = jnp.sum(prob * grad_prob, axis=0, keepdims=True)
-        grad_score = (prob * (grad_prob - delta)).astype(BF16)
-        value_grad += dot(prob_low, g_two, ((1,), (0,)))
-        key_grad += dot(grad_score, q_two, ((1,), (0,)))
-        prob_ref[:, first * tok : (first + pairs) * tok] = prob_low
-        ds_ref[:, first * tok : (first + pairs) * tok] = grad_score
-    key_grad = key_grad * scale
-    own_ref[:, :head] = key_grad[SPAN * tok :, :]
-    own_ref[:, head:] = value_grad[SPAN * tok :, :]
-    for offset in range(1, SPAN + 1):
-        rows = slice((SPAN - offset) * tok, (SPAN - offset + 1) * tok)
-        part_refs[offset - 1][:, :head] = key_grad[rows, :].astype(BF16)
-        part_refs[offset - 1][:, head:] = value_grad[rows, :].astype(BF16)
+    live = jnp.max(live_ref[...])
+
+    def attend(skipped):
+        dead = skipped * tok
+        for ref in (key_ref, value_ref, prob_ref, ds_ref):
+            if dead:
+                ref[:dead, :] = jnp.zeros((dead, ref.shape[1]), BF16)
+        for block in range(skipped, SPAN + 1):
+            rows = slice(block * tok, (block + 1) * tok)
+            both = dot(place_ref[rows, :], window(block), ((1,), (0,))).astype(BF16)
+            key_ref[rows, :] = both[:, :head]
+            value_ref[rows, :] = both[:, head:]
+        key = key_ref[dead:, :]
+        value = value_ref[dead:, :]
+        pairs = 4
+        mask = jnp.concatenate([mask_ref[dead:, :]] * pairs, axis=1)
+        key_grad = jnp.zeros(key.shape, F32)
+        value_grad = jnp.zeros(key.shape, F32)
+        for first in range(0, heads, pairs):
+            spans = [slice(h * head, (h + 1) * head) for h in range(first, first + pairs)]
+            q_two = jnp.concatenate([queries[:, s] for s in spans], axis=0)
+            g_two = jnp.concatenate([grads[:, s] for s in spans], axis=0)
+            scores = dot(key, q_two, ((1,), (1,))) + mask
+            top = jnp.max(scores, axis=0, keepdims=True)
+            weights = jnp.exp2((scores - top) * factor)
+            inverse = 1.0 / jnp.sum(weights, axis=0, keepdims=True)
+            prob = weights * inverse
+            prob_low = prob.astype(BF16)
+            grad_prob = dot(value, g_two, ((1,), (1,)))
+            delta = jnp.sum(prob * grad_prob, axis=0, keepdims=True)
+            grad_score = (prob * (grad_prob - delta)).astype(BF16)
+            value_grad += dot(prob_low, g_two, ((1,), (0,)))
+            key_grad += dot(grad_score, q_two, ((1,), (0,)))
+            prob_ref[dead:, first * tok : (first + pairs) * tok] = prob_low
+            ds_ref[dead:, first * tok : (first + pairs) * tok] = grad_score
+        key_grad = key_grad * scale
+        for offset, ref in enumerate((own_ref, *part_refs)):
+            block = SPAN - offset - skipped
+            if block < 0:
+                ref[...] = jnp.zeros(ref.shape, ref.dtype)
+            else:
+                rows = slice(block * tok, (block + 1) * tok)
+                ref[:, :head] = key_grad[rows, :].astype(ref.dtype)
+                ref[:, head:] = value_grad[rows, :].astype(ref.dtype)
+
+    pl.when(live <= 2)(lambda: attend(SPAN - 1))
+    pl.when((live > 2) & (live <= 4))(lambda: attend(SPAN - 3))
+    pl.when(live > 4)(lambda: attend(0))
 
 
 def output_kernel(key_ref, value_ref, prob_ref, ds_ref, attn_ref, dq_ref):
@@ -278,14 +289,15 @@
             packed[step] = swapped(packed[step], step)
     else:
         packed = [lax.all_to_all(packed[0], "dcp", split_axis=0, concat_axis=0, tiled=True)]
-    places, mask = pl.pallas_call(
+    places, mask, live = pl.pallas_call(
         functools.partial(slots_kernel, per_peer, paired),
         out_shape=[
             jax.ShapeDtypeStruct(((SPAN + 1) * tok, tok), BF16),
             jax.ShapeDtypeStruct(((SPAN + 1) * tok, tok), F32),
+            jax.ShapeDtypeStruct((8, LANES), F32),
         ],
         in_specs=[hbm, hbm, pl.BlockSpec(memory_space=pl.ANY)],
-        out_specs=[vmem] * 2,
+        out_specs=[vmem] * 3,
         scratch_shapes=[
             pltpu.VMEM((devices, tok), jnp.int32),
             pltpu.SMEM(doc_lengths.shape, jnp.int32),
@@ -314,11 +326,11 @@
     keys, values, probs, grad_scores, summed, *parts = pl.pallas_call(
         functools.partial(attend_kernel, width, head, pieces),
         out_shape=[seen, seen, square, square, jax.ShapeDtypeStruct((tok, 2 * head), F32)] + [part] * SPAN,
-        in_specs=[vmem] * (2 + len(packed)),
+        in_specs=[vmem] * (3 + len(packed)),
         out_specs=[vmem] * (5 + SPAN),
         compiler_params=params,
         name="attend",
-    )(mask, places, *packed)
+    )(live, mask, places, *packed)
     attn_out, dquery = pl.pallas_call(
         output_kernel,
         out_shape=[wide, wide],

time: 44.1 us -> 43.2 us (0.980)
  starting transfers between devices: 22.3 us -> 21.5 us
  Pallas kernels: 8.12 us -> 7.45 us
  waiting for transfers between devices: 11.7 us -> 12.2 us
    ppermute x5, starting transfers between devices: 9.79 us -> 8.91 us  [per_device(): summed = summed + lax.ppermute(parts[offset - 1], 'dcp', pairs).astype(F32)]
    pallas_call x1, Pallas kernels: 3.29 us -> 2.58 us  [per_device(): pl.pallas_call(functools.partial(attend_kernel, width, head, pieces), out...]
    ppermute x5, waiting for transfers between devices: 3.89 us -> 4.42 us  [per_device(): summed = summed + lax.ppermute(parts[offset - 1], 'dcp', pairs).astype(F32)]
  transfers between devices with their start and end apart: 13 -> 13, of which waited for: 9 -> 10; matrix products, arithmetic and copies ran while one was open for 0% -> 0% of each run, Pallas kernels for 7% -> 8%
where the time goes in v9:
time: 43.2 us; the launch traced here: 42.6 us
  starting transfers between devices  21.5 us (50%)
  waiting for transfers between devices  12.2 us (28%)
  Pallas kernels  7.45 us (17%)
  between operations  0.73 us (2%)
  local copies, waits for them, and re-layouts  0.63 us (1%)
    ppermute x8, starting transfers between devices, swapped(): return lax.ppermute(rows, 'dcp', [(d, d ^ step) for d in range(devices)])  12.6 us
    ppermute x5, starting transfers between devices, per_device(): summed = summed + lax.ppermute(parts[offset - 1], 'dcp', pairs).astype(F32)  8.91 us
    ppermute x8, waiting for transfers between devices, swapped(): return lax.ppermute(rows, 'dcp', [(d, d ^ step) for d in range(devices)])  7.81 us
    ppermute x5, waiting for transfers between devices, per_device(): summed = summed + lax.ppermute(parts[offset - 1], 'dcp', pairs).astype(F32)  4.42 us
    pallas_call x1, Pallas kernels, per_device(): pl.pallas_call(functools.partial(attend_kernel, width, head, pieces), out...  2.58 us
    pallas_call x1, Pallas kernels, per_device(): pl.pallas_call(functools.partial(pack_kernel, per_peer, paired), out_shap...  1.58 us
    pallas_call x1, Pallas kernels, per_device(): pl.pallas_call(output_kernel, out_shape=[wide, wide], in_specs=[vmem] * 4...  1.54 us
    pallas_call x1, Pallas kernels, per_device(): pl.pallas_call(functools.partial(slots_kernel, per_peer, paired), out_sha...  1.21 us
  transfers between devices with their start and end apart: 13, of which 10 were waited for; matrix products, arithmetic and copies ran while one was open for 0% of the time, Pallas kernels for 8%

profile of v9, /device:TPU:14, one launch (start us, length us, event | category | flops | bytes accessed | tf_op | source)
XLA Modules:
  0.0 42.6 jit_solution(13655233355357602463)
XLA Ops:
  0.6 1.6 %pack.1 = (bf16[128,256]{1,0:T(8,128)(2,1)S(1)}, bf16[16,2048]{1,0:T(8,128)(2,1)S(1)}, bf16[16,2048]{1,0:T(8,128)(2,1)S(1)}, bf16[16,2048]{1,0:T(8,128)(2,1)S(1)...) custom-call(s32[8,128]{1,0:T(8,128)} %bitcast.1, ...), custom_call_target="tpu_custom_call" | custom-call | tf_op jit(solution)/shard_map/pack/pallas_call | solution.py:258
  2.2 2.7 %collective-permute-start = (bf16[128,256]{1,0:T(8,128)(2,1)S(1)}, bf16[128,256]{1,0:T(8,128)(2,1)S(1)}, u32[]{:S(2)}, u32[]{:S(2)}) collective-permute-start(bf16[128,256]{1,0:T(8,128)(2,1)S(1)} %get-tuple-element.32.refs_0_), channel_id=1, source_target_pairs={{0,16},{4,20},{8,24},{12,28},{16,0},{20,4},{24,8},{28,12},{1,17},{... | collective-permute-start | bytes 196616 | tf_op jit(solution)/shard_map/ppermute | solution.py:256
  4.9 0.3 collective-permute-start.4
  5.2 2.5 %collective-permute-start.5 = (bf16[16,2048]{1,0:T(8,128)(2,1)S(1)}, bf16[16,2048]{1,0:T(8,128)(2,1)S(1)}, u32[]{:S(2)}, u32[]{:S(2)}) collective-permute-start(bf16[16,2048]{1,0:T(8,128)(2,1)S(1)} %get-tuple-element.45), channel_id=1, source_target_pairs={{0,20},{4,16},{8,28},{12,24},{16,4},{20,0},{24,12},{28,8},{1,21},{... | collective-permute-start | bytes 196616 | tf_op jit(solution)/shard_map/ppermute | solution.py:256
  7.7 3.0 %collective-permute-start.7 = (bf16[16,2048]{1,0:T(8,128)(2,1)S(1)}, bf16[16,2048]{1,0:T(8,128)(2,1)S(1)}, u32[]{:S(2)}, u32[]{:S(2)}) collective-permute-start(bf16[16,2048]{1,0:T(8,128)(2,1)S(1)} %get-tuple-element.47), channel_id=1, source_target_pairs={{0,28},{4,24},{8,20},{12,16},{16,12},{20,8},{24,4},{28,0},{1,29},{... | collective-permute-start | bytes 196616 | tf_op jit(solution)/shard_map/ppermute | solution.py:256
  10.7 1.7 %collective-permute-done.refs_1_ = bf16[128,256]{1,0:T(8,128)(2,1)S(1)} collective-permute-done((bf16[128,256]{1,0:T(8,128)(2,1)S(1)}, bf16[128,256]{1,0:T(8,128)(2,1)S(1)}, u32[]{:S(2)}, u32[]{:S(2)}) %collective-permute-start) | collective-permute-done | bytes 65568 | tf_op jit(solution)/shard_map/ppermute | solution.py:256
  12.8 1.2 %slots.1 = (bf16[768,128]{1,0:T(8,128)(2,1)S(1)}, f32[768,128]{1,0:T(8,128)S(1)}, f32[8,128]{1,0:T(8,128)S(1)}) custom-call(s32[8,128]{1,0:T(8,128)} %bitcast.2, s32[3]{0:T(128)} %len_hbm.1, bf16[16,5120]{1,0:T(8,128)(2,1)S(1)} %get-tuple-element.37._.refs_0_), custom_call_target="tpu_custom_call" | custom-call | tf_op jit(solution)/shard_map/slots/pallas_call | solution.py:292
  14.0 0.5 %collective-permute-done.4.refs_0_ = bf16[16,2048]{1,0:T(8,128)(2,1)S(1)} collective-permute-done((bf16[16,2048]{1,0:T(8,128)(2,1)S(1)}, bf16[16,2048]{1,0:T(8,128)(2,1)S(1)}, u32[]{:S(2)}, u32[]{:S(2)}) %collective-permute-start.4) | collective-permute-done | bytes 65568 | tf_op jit(solution)/shard_map/ppermute | solution.py:256
  14.6 1.2 %collective-permute-start.2 = (bf16[16,5120]{1,0:T(8,128)(2,1)S(1)}, bf16[16,5120]{1,0:T(8,128)(2,1)S(1)}, u32[]{:S(2)}, u32[]{:S(2)}) collective-permute-start(bf16[16,5120]{1,0:T(8,128)(2,1)S(1)} %get-tuple-element.42), channel_id=1, source_target_pairs={{0,8},{4,12},{8,0},{12,4},{16,24},{20,28},{24,16},{28,20},{1,9},{5... | collective-permute-start | bytes 491528 | tf_op jit(solution)/shard_map/ppermute | solution.py:256
  16.0 2.8 %collective-permute-start.3 = (bf16[16,5120]{1,0:T(8,128)(2,1)S(1)}, bf16[16,5120]{1,0:T(8,128)(2,1)S(1)}, u32[]{:S(2)}, u32[]{:S(2)}) collective-permute-start(bf16[16,5120]{1,0:T(8,128)(2,1)S(1)} %get-tuple-element.43), channel_id=1, source_target_pairs={{0,12},{4,8},{8,4},{12,0},{16,28},{20,24},{24,20},{28,16},{1,13},{... | collective-permute-start | bytes 491528 | tf_op jit(solution)/shard_map/ppermute | solution.py:256
  19.0 0.3 far.1.refs_4_
  19.6 1.8 %collective-permute-done.2.refs_2_ = bf16[16,5120]{1,0:T(8,128)(2,1)S(1)} collective-permute-done((bf16[16,5120]{1,0:T(8,128)(2,1)S(1)}, bf16[16,5120]{1,0:T(8,128)(2,1)S(1)}, u32[]{:S(2)}, u32[]{:S(2)}) %collective-permute-start.2) | collective-permute-done | bytes 163872 | tf_op jit(solution)/shard_map/ppermute | solution.py:256
  21.4 3.0 %collective-permute-done.3.refs_3_ = bf16[16,5120]{1,0:T(8,128)(2,1)S(1)} collective-permute-done((bf16[16,5120]{1,0:T(8,128)(2,1)S(1)}, bf16[16,5120]{1,0:T(8,128)(2,1)S(1)}, u32[]{:S(2)}, u32[]{:S(2)}) %collective-permute-start.3) | collective-permute-done | bytes 163872 | tf_op jit(solution)/shard_map/ppermute | solution.py:256
  24.4 2.6 %attend.1 = (bf16[768,128]{1,0:T(8,128)(2,1)S(1)}, bf16[768,128]{1,0:T(8,128)(2,1)S(1)}, bf16[768,1024]{1,0:T(8,128)(2,1)S(1)}, bf16[768,1024]{1,0:T(8,128)(2,1)...) custom-call(f32[8,128]{1,0:T(8,128)S(1)} %get-tuple-element.38.live_, ...), custom_call_target="tpu_custom_call" | custom-call | tf_op jit(solution)/shard_map/attend/pallas_call | solution.py:326
  27.0 0.7 %collective-permute-start.8 = (bf16[128,256]{1,0:T(8,128)(2,1)S(1)}, bf16[128,256]{1,0:T(8,128)(2,1)S(1)}, u32[]{:S(2)}, u32[]{:S(2)}) collective-permute-start(bf16[128,256]{1,0:T(8,128)(2,1)S(1)} %get-tuple-element.55), channel_id=1, source_target_pairs={{20,0},{24,4},{28,8},{21,1},{25,5},{29,9},{22,2},{26,6},{30,10},{2... | collective-permute-start | bytes 196616 | tf_op jit(solution)/shard_map/ppermute | solution.py:344
  27.6 1.3 %collective-permute-start.9 = (bf16[128,256]{1,0:T(8,128)(2,1)S(1)}, bf16[128,256]{1,0:T(8,128)(2,1)S(1)}, u32[]{:S(2)}, u32[]{:S(2)}) collective-permute-start(bf16[128,256]{1,0:T(8,128)(2,1)S(1)} %get-tuple-element.56), channel_id=1, source_target_pairs={{16,0},{20,4},{24,8},{28,12},{17,1},{21,5},{25,9},{29,13},{18,2},{... | collective-permute-start | bytes 196616 | tf_op jit(solution)/shard_map/ppermute | solution.py:344
  28.9 3.1 %collective-permute-start.10 = (bf16[128,256]{1,0:T(8,128)(2,1)S(1)}, bf16[128,256]{1,0:T(8,128)(2,1)S(1)}, u32[]{:S(2)}, u32[]{:S(2)}) collective-permute-start(bf16[128,256]{1,0:T(8,128)(2,1)S(1)} %get-tuple-element.57), channel_id=1, source_target_pairs={{12,0},{16,4},{20,8},{24,12},{28,16},{13,1},{17,5},{21,9},{25,13},... | collective-permute-start | bytes 196616 | tf_op jit(solution)/shard_map/ppermute | solution.py:344
  32.1 1.9 %collective-permute-start.11 = (bf16[128,256]{1,0:T(8,128)(2,1)S(1)}, bf16[128,256]{1,0:T(8,128)(2,1)S(1)}, u32[]{:S(2)}, u32[]{:S(2)}) collective-permute-start(bf16[128,256]{1,0:T(8,128)(2,1)S(1)} %get-tuple-element.58), channel_id=1, source_target_pairs={{8,0},{12,4},{16,8},{20,12},{24,16},{28,20},{9,1},{13,5},{17,9},{2... | collective-permute-start | bytes 196616 | tf_op jit(solution)/shard_map/ppermute | solution.py:344
  34.0 1.9 %collective-permute-start.12 = (bf16[128,256]{1,0:T(8,128)(2,1)S(1)}, bf16[128,256]{1,0:T(8,128)(2,1)S(1)}, u32[]{:S(2)}, u32[]{:S(2)}) collective-permute-start(bf16[128,256]{1,0:T(8,128)(2,1)S(1)} %get-tuple-element.59), channel_id=1, source_target_pairs={{4,0},{8,4},{12,8},{16,12},{20,16},{24,20},{28,24},{5,1},{9,5},{13... | collective-permute-start | bytes 196616 | tf_op jit(solution)/shard_map/ppermute | solution.py:344
  35.9 1.5 %outputs.1 = (bf16[128,1024]{1,0:T(8,128)(2,1)}, bf16[128,1024]{1,0:T(8,128)(2,1)}) custom-call(bf16[768,128]{1,0:T(8,128)(2,1)S(1)} %get-tuple-element.48.key_ref, bf16[768,128]{1,0:T(8,128)(2,1)S(1)} %get-tuple-element.49.value_ref, bf16[768,1024]{1,0:T(8,128)(2,1)S(1)} %get-tuple-element.50.prob_ref, bf16[768,1024]{1,0:T(8,128)(2,1)S(1)} %get-tuple-element.51.ds_ref), custom_call_target="tpu_custom_call" | custom-call | tf_op jit(solution)/shard_map/outputs/pallas_call | solution.py:334
  37.5 0.7 %collective-permute-done.10 = bf16[128,256]{1,0:T(8,128)(2,1)S(1)} collective-permute-done((bf16[128,256]{1,0:T(8,128)(2,1)S(1)}, bf16[128,256]{1,0:T(8,128)(2,1)S(1)}, u32[]{:S(2)}, u32[]{:S(2)}) %collective-permute-start.10) | collective-permute-done | bytes 65568 | tf_op jit(solution)/shard_map/ppermute | solution.py:344
  38.2 2.0 %collective-permute-done.11 = bf16[128,256]{1,0:T(8,128)(2,1)S(1)} collective-permute-done((bf16[128,256]{1,0:T(8,128)(2,1)S(1)}, bf16[128,256]{1,0:T(8,128)(2,1)S(1)}, u32[]{:S(2)}, u32[]{:S(2)}) %collective-permute-start.11) | collective-permute-done | bytes 65568 | tf_op jit(solution)/shard_map/ppermute | solution.py:344
  40.2 1.7 %collective-permute-done.12 = bf16[128,256]{1,0:T(8,128)(2,1)S(1)} collective-permute-done((bf16[128,256]{1,0:T(8,128)(2,1)S(1)}, bf16[128,256]{1,0:T(8,128)(2,1)S(1)}, u32[]{:S(2)}, u32[]{:S(2)}) %collective-permute-start.12) | collective-permute-done | bytes 65568 | tf_op jit(solution)/shard_map/ppermute | solution.py:344
  41.9 0.6 %fusion = (bf16[128,128]{1,0:T(8,128)(2,1)}, bf16[128,128]{1,0:T(8,128)(2,1)}) fusion(bf16[128,256]{1,0:T(8,128)(2,1)S(1)} %add_convert_fusion), kind=kLoop, calls=%fused_computation.1 | loop fusion | bytes 131072 | tf_op jit(solution)/shard_map/slice | solution.py:345
  (10 shorter events, 1.1 us)
Async XLA Ops:
  2.2 10.2 %collective-permute-start = (bf16[128,256]{1,0:T(8,128)(2,1)S(1)}, bf16[128,256]{1,0:T(8,128)(2,1)S(1)}, u32[]{:S(2)}, u32[]{:S(2)}) collective-permute-start(bf16[128,256]{1,0:T(8,128)(2,1)S(1)} %get-tuple-element.32.refs_0_), channel_id=1, source_target_pairs={{0,16},{4,20},{8,24},{12,28},{16,0},{20,4},{24,8},{28,12},{1,17},{... | collective-permute-start | bytes 196616 | tf_op jit(solution)/shard_map/ppermute | solution.py:256
  4.9 9.7 %collective-permute-start.4 = (bf16[16,2048]{1,0:T(8,128)(2,1)S(1)}, bf16[16,2048]{1,0:T(8,128)(2,1)S(1)}, u32[]{:S(2)}, u32[]{:S(2)}) collective-permute-start(bf16[16,2048]{1,0:T(8,128)(2,1)S(1)} %get-tuple-element.44), channel_id=1, source_target_pairs={{0,16},{4,20},{8,24},{12,28},{16,0},{20,4},{24,8},{28,12},{1,17},{... | collective-permute-start | bytes 196616 | tf_op jit(solution)/shard_map/ppermute | solution.py:256
  5.2 10.8 %collective-permute-start.5 = (bf16[16,2048]{1,0:T(8,128)(2,1)S(1)}, bf16[16,2048]{1,0:T(8,128)(2,1)S(1)}, u32[]{:S(2)}, u32[]{:S(2)}) collective-permute-start(bf16[16,2048]{1,0:T(8,128)(2,1)S(1)} %get-tuple-element.45), channel_id=1, source_target_pairs={{0,20},{4,16},{8,28},{12,24},{16,4},{20,0},{24,12},{28,8},{1,21},{... | collective-permute-start | bytes 196616 | tf_op jit(solution)/shard_map/ppermute | solution.py:256
  7.7 11.1 %collective-permute-start.6 = (bf16[16,2048]{1,0:T(8,128)(2,1)S(1)}, bf16[16,2048]{1,0:T(8,128)(2,1)S(1)}, u32[]{:S(2)}, u32[]{:S(2)}) collective-permute-start(bf16[16,2048]{1,0:T(8,128)(2,1)S(1)} %get-tuple-element.46), channel_id=1, source_target_pairs={{0,24},{4,28},{8,16},{12,20},{16,8},{20,12},{24,0},{28,4},{1,25},{... | collective-permute-start | bytes 196616 | tf_op jit(solution)/shard_map/ppermute | solution.py:256
  7.7 11.3 %collective-permute-start.7 = (bf16[16,2048]{1,0:T(8,128)(2,1)S(1)}, bf16[16,2048]{1,0:T(8,128)(2,1)S(1)}, u32[]{:S(2)}, u32[]{:S(2)}) collective-permute-start(bf16[16,2048]{1,0:T(8,128)(2,1)S(1)} %get-tuple-element.47), channel_id=1, source_target_pairs={{0,28},{4,24},{8,20},{12,16},{16,12},{20,8},{24,4},{28,0},{1,29},{... | collective-permute-start | bytes 196616 | tf_op jit(solution)/shard_map/ppermute | solution.py:256
  12.7 6.8 %collective-permute-start.1 = (bf16[16,5120]{1,0:T(8,128)(2,1)S(1)}, bf16[16,5120]{1,0:T(8,128)(2,1)S(1)}, u32[]{:S(2)}, u32[]{:S(2)}) collective-permute-start(bf16[16,5120]{1,0:T(8,128)(2,1)S(1)} %get-tuple-element.41), channel_id=1, source_target_pairs={{0,4},{4,0},{8,12},{12,8},{16,20},{20,16},{24,28},{28,24},{1,5},{5... | collective-permute-start | bytes 491528 | tf_op jit(solution)/shard_map/ppermute | solution.py:256
  14.6 6.8 %collective-permute-start.2 = (bf16[16,5120]{1,0:T(8,128)(2,1)S(1)}, bf16[16,5120]{1,0:T(8,128)(2,1)S(1)}, u32[]{:S(2)}, u32[]{:S(2)}) collective-permute-start(bf16[16,5120]{1,0:T(8,128)(2,1)S(1)} %get-tuple-element.42), channel_id=1, source_target_pairs={{0,8},{4,12},{8,0},{12,4},{16,24},{20,28},{24,16},{28,20},{1,9},{5... | collective-permute-start | bytes 491528 | tf_op jit(solution)/shard_map/ppermute | solution.py:256
  16.0 8.3 %collective-permute-start.3 = (bf16[16,5120]{1,0:T(8,128)(2,1)S(1)}, bf16[16,5120]{1,0:T(8,128)(2,1)S(1)}, u32[]{:S(2)}, u32[]{:S(2)}) collective-permute-start(bf16[16,5120]{1,0:T(8,128)(2,1)S(1)} %get-tuple-element.43), channel_id=1, source_target_pairs={{0,12},{4,8},{8,4},{12,0},{16,28},{20,24},{24,20},{28,16},{1,13},{... | collective-permute-start | bytes 491528 | tf_op jit(solution)/shard_map/ppermute | solution.py:256
  27.0 10.5 %collective-permute-start.8 = (bf16[128,256]{1,0:T(8,128)(2,1)S(1)}, bf16[128,256]{1,0:T(8,128)(2,1)S(1)}, u32[]{:S(2)}, u32[]{:S(2)}) collective-permute-start(bf16[128,256]{1,0:T(8,128)(2,1)S(1)} %get-tuple-element.55), channel_id=1, source_target_pairs={{20,0},{24,4},{28,8},{21,1},{25,5},{29,9},{22,2},{26,6},{30,10},{2... | collective-permute-start | bytes 196616 | tf_op jit(solution)/shard_map/ppermute | solution.py:344
  27.6 9.8 %collective-permute-start.9 = (bf16[128,256]{1,0:T(8,128)(2,1)S(1)}, bf16[128,256]{1,0:T(8,128)(2,1)S(1)}, u32[]{:S(2)}, u32[]{:S(2)}) collective-permute-start(bf16[128,256]{1,0:T(8,128)(2,1)S(1)} %get-tuple-element.56), channel_id=1, source_target_pairs={{16,0},{20,4},{24,8},{28,12},{17,1},{21,5},{25,9},{29,13},{18,2},{... | collective-permute-start | bytes 196616 | tf_op jit(solution)/shard_map/ppermute | solution.py:344
  28.9 9.2 %collective-permute-start.10 = (bf16[128,256]{1,0:T(8,128)(2,1)S(1)}, bf16[128,256]{1,0:T(8,128)(2,1)S(1)}, u32[]{:S(2)}, u32[]{:S(2)}) collective-permute-start(bf16[128,256]{1,0:T(8,128)(2,1)S(1)} %get-tuple-element.57), channel_id=1, source_target_pairs={{12,0},{16,4},{20,8},{24,12},{28,16},{13,1},{17,5},{21,9},{25,13},... | collective-permute-start | bytes 196616 | tf_op jit(solution)/shard_map/ppermute | solution.py:344
  32.1 8.1 %collective-permute-start.11 = (bf16[128,256]{1,0:T(8,128)(2,1)S(1)}, bf16[128,256]{1,0:T(8,128)(2,1)S(1)}, u32[]{:S(2)}, u32[]{:S(2)}) collective-permute-start(bf16[128,256]{1,0:T(8,128)(2,1)S(1)} %get-tuple-element.58), channel_id=1, source_target_pairs={{8,0},{12,4},{16,8},{20,12},{24,16},{28,20},{9,1},{13,5},{17,9},{2... | collective-permute-start | bytes 196616 | tf_op jit(solution)/shard_map/ppermute | solution.py:344
  34.0 7.9 %collective-permute-start.12 = (bf16[128,256]{1,0:T(8,128)(2,1)S(1)}, bf16[128,256]{1,0:T(8,128)(2,1)S(1)}, u32[]{:S(2)}, u32[]{:S(2)}) collective-permute-start(bf16[128,256]{1,0:T(8,128)(2,1)S(1)} %get-tuple-element.59), channel_id=1, source_target_pairs={{4,0},{8,4},{12,8},{16,12},{20,16},{24,20},{28,24},{5,1},{9,5},{13... | collective-permute-start | bytes 196616 | tf_op jit(solution)/shard_map/ppermute | solution.py:344

commit v10 on v9

--- a/solution.py
+++ b/solution.py
@@ -217,9 +217,9 @@
                 ref[:, :head] = key_grad[rows, :].astype(ref.dtype)
                 ref[:, head:] = value_grad[rows, :].astype(ref.dtype)
 
-    pl.when(live <= 2)(lambda: attend(SPAN - 1))
-    pl.when((live > 2) & (live <= 4))(lambda: attend(SPAN - 3))
-    pl.when(live > 4)(lambda: attend(0))
+    pl.when(live > SPAN)(lambda: attend(0))
+    for skipped in range(1, SPAN + 1):
+        pl.when(live == SPAN + 1 - skipped)(functools.partial(attend, skipped))
 
 
 def output_kernel(key_ref, value_ref, prob_ref, ds_ref, attn_ref, dq_ref):

time: 43.2 us -> 42.9 us (level)
  Pallas kernels: 7.45 us -> 6.31 us
  starting transfers between devices: 21.5 us -> 22.4 us
    pallas_call x1, Pallas kernels: 2.58 us -> 1.44 us  [per_device(): pl.pallas_call(functools.partial(attend_kernel, width, head, pieces), out...]
    ppermute x5, starting transfers between devices: 8.91 us -> 9.79 us  [per_device(): summed = summed + lax.ppermute(parts[offset - 1], 'dcp', pairs).astype(F32)]
where the time goes in v10:
time: 42.9 us; the launch traced here: 42.5 us
  starting transfers between devices  22.4 us (52%)
  waiting for transfers between devices  12.4 us (29%)
  Pallas kernels  6.31 us (15%)
  between operations  0.73 us (2%)
  local copies, waits for them, and re-layouts  0.63 us (1%)
    ppermute x8, starting transfers between devices, swapped(): return lax.ppermute(rows, 'dcp', [(d, d ^ step) for d in range(devices)])  12.6 us
    ppermute x5, starting transfers between devices, per_device(): summed = summed + lax.ppermute(parts[offset - 1], 'dcp', pairs).astype(F32)  9.79 us
    ppermute x8, waiting for transfers between devices, swapped(): return lax.ppermute(rows, 'dcp', [(d, d ^ step) for d in range(devices)])  7.79 us
    ppermute x5, waiting for transfers between devices, per_device(): summed = summed + lax.ppermute(parts[offset - 1], 'dcp', pairs).astype(F32)  4.64 us
    pallas_call x1, Pallas kernels, per_device(): pl.pallas_call(functools.partial(pack_kernel, per_peer, paired), out_shap...  1.58 us
    pallas_call x1, Pallas kernels, per_device(): pl.pallas_call(output_kernel, out_shape=[wide, wide], in_specs=[vmem] * 4...  1.54 us
    pallas_call x1, Pallas kernels, per_device(): pl.pallas_call(functools.partial(attend_kernel, width, head, pieces), out...  1.44 us
    pallas_call x1, Pallas kernels, per_device(): pl.pallas_call(functools.partial(slots_kernel, per_peer, paired), out_sha...  1.21 us
  transfers between devices with their start and end apart: 13, of which 10 were waited for; matrix products, arithmetic and copies ran while one was open for 0% of the time, Pallas kernels for 8%

profile of v10, /device:TPU:14, one launch (start us, length us, event | category | flops | bytes accessed | tf_op | source)
XLA Modules:
  0.0 42.5 jit_solution(2573346541514966911)
XLA Ops:
  0.6 1.6 %pack.1 = (bf16[128,256]{1,0:T(8,128)(2,1)S(1)}, bf16[16,2048]{1,0:T(8,128)(2,1)S(1)}, bf16[16,2048]{1,0:T(8,128)(2,1)S(1)}, bf16[16,2048]{1,0:T(8,128)(2,1)S(1)...) custom-call(s32[8,128]{1,0:T(8,128)} %bitcast.1, ...), custom_call_target="tpu_custom_call" | custom-call | tf_op jit(solution)/shard_map/pack/pallas_call | solution.py:258
  2.2 2.7 %collective-permute-start = (bf16[128,256]{1,0:T(8,128)(2,1)S(1)}, bf16[128,256]{1,0:T(8,128)(2,1)S(1)}, u32[]{:S(2)}, u32[]{:S(2)}) collective-permute-start(bf16[128,256]{1,0:T(8,128)(2,1)S(1)} %get-tuple-element.32.refs_0_), channel_id=1, source_target_pairs={{0,16},{4,20},{8,24},{12,28},{16,0},{20,4},{24,8},{28,12},{1,17},{... | collective-permute-start | bytes 196616 | tf_op jit(solution)/shard_map/ppermute | solution.py:256
  4.9 0.3 collective-permute-start.4
  5.2 2.5 %collective-permute-start.5 = (bf16[16,2048]{1,0:T(8,128)(2,1)S(1)}, bf16[16,2048]{1,0:T(8,128)(2,1)S(1)}, u32[]{:S(2)}, u32[]{:S(2)}) collective-permute-start(bf16[16,2048]{1,0:T(8,128)(2,1)S(1)} %get-tuple-element.45), channel_id=1, source_target_pairs={{0,20},{4,16},{8,28},{12,24},{16,4},{20,0},{24,12},{28,8},{1,21},{... | collective-permute-start | bytes 196616 | tf_op jit(solution)/shard_map/ppermute | solution.py:256
  7.7 3.0 %collective-permute-start.7 = (bf16[16,2048]{1,0:T(8,128)(2,1)S(1)}, bf16[16,2048]{1,0:T(8,128)(2,1)S(1)}, u32[]{:S(2)}, u32[]{:S(2)}) collective-permute-start(bf16[16,2048]{1,0:T(8,128)(2,1)S(1)} %get-tuple-element.47), channel_id=1, source_target_pairs={{0,28},{4,24},{8,20},{12,16},{16,12},{20,8},{24,4},{28,0},{1,29},{... | collective-permute-start | bytes 196616 | tf_op jit(solution)/shard_map/ppermute | solution.py:256
  10.7 1.7 %collective-permute-done.refs_1_ = bf16[128,256]{1,0:T(8,128)(2,1)S(1)} collective-permute-done((bf16[128,256]{1,0:T(8,128)(2,1)S(1)}, bf16[128,256]{1,0:T(8,128)(2,1)S(1)}, u32[]{:S(2)}, u32[]{:S(2)}) %collective-permute-start) | collective-permute-done | bytes 65568 | tf_op jit(solution)/shard_map/ppermute | solution.py:256
  12.8 1.2 %slots.1 = (bf16[768,128]{1,0:T(8,128)(2,1)S(1)}, f32[768,128]{1,0:T(8,128)S(1)}, f32[8,128]{1,0:T(8,128)S(1)}) custom-call(s32[8,128]{1,0:T(8,128)} %bitcast.2, s32[3]{0:T(128)} %len_hbm.1, bf16[16,5120]{1,0:T(8,128)(2,1)S(1)} %get-tuple-element.37._.refs_0_), custom_call_target="tpu_custom_call" | custom-call | tf_op jit(solution)/shard_map/slots/pallas_call | solution.py:292
  14.0 0.5 %collective-permute-done.4.refs_0_ = bf16[16,2048]{1,0:T(8,128)(2,1)S(1)} collective-permute-done((bf16[16,2048]{1,0:T(8,128)(2,1)S(1)}, bf16[16,2048]{1,0:T(8,128)(2,1)S(1)}, u32[]{:S(2)}, u32[]{:S(2)}) %collective-permute-start.4) | collective-permute-done | bytes 65568 | tf_op jit(solution)/shard_map/ppermute | solution.py:256
  14.6 1.2 %collective-permute-start.2 = (bf16[16,5120]{1,0:T(8,128)(2,1)S(1)}, bf16[16,5120]{1,0:T(8,128)(2,1)S(1)}, u32[]{:S(2)}, u32[]{:S(2)}) collective-permute-start(bf16[16,5120]{1,0:T(8,128)(2,1)S(1)} %get-tuple-element.42), channel_id=1, source_target_pairs={{0,8},{4,12},{8,0},{12,4},{16,24},{20,28},{24,16},{28,20},{1,9},{5... | collective-permute-start | bytes 491528 | tf_op jit(solution)/shard_map/ppermute | solution.py:256
  16.0 2.8 %collective-permute-start.3 = (bf16[16,5120]{1,0:T(8,128)(2,1)S(1)}, bf16[16,5120]{1,0:T(8,128)(2,1)S(1)}, u32[]{:S(2)}, u32[]{:S(2)}) collective-permute-start(bf16[16,5120]{1,0:T(8,128)(2,1)S(1)} %get-tuple-element.43), channel_id=1, source_target_pairs={{0,12},{4,8},{8,4},{12,0},{16,28},{20,24},{24,20},{28,16},{1,13},{... | collective-permute-start | bytes 491528 | tf_op jit(solution)/shard_map/ppermute | solution.py:256
  19.0 0.3 far.1.refs_4_
  19.3 0.3 collective-permute-done.1.refs_1_
  19.6 1.8 %collective-permute-done.2.refs_2_ = bf16[16,5120]{1,0:T(8,128)(2,1)S(1)} collective-permute-done((bf16[16,5120]{1,0:T(8,128)(2,1)S(1)}, bf16[16,5120]{1,0:T(8,128)(2,1)S(1)}, u32[]{:S(2)}, u32[]{:S(2)}) %collective-permute-start.2) | collective-permute-done | bytes 163872 | tf_op jit(solution)/shard_map/ppermute | solution.py:256
  21.4 3.0 %collective-permute-done.3.refs_3_ = bf16[16,5120]{1,0:T(8,128)(2,1)S(1)} collective-permute-done((bf16[16,5120]{1,0:T(8,128)(2,1)S(1)}, bf16[16,5120]{1,0:T(8,128)(2,1)S(1)}, u32[]{:S(2)}, u32[]{:S(2)}) %collective-permute-start.3) | collective-permute-done | bytes 163872 | tf_op jit(solution)/shard_map/ppermute | solution.py:256
  24.4 1.4 %attend.1 = (bf16[768,128]{1,0:T(8,128)(2,1)S(1)}, bf16[768,128]{1,0:T(8,128)(2,1)S(1)}, bf16[768,1024]{1,0:T(8,128)(2,1)S(1)}, bf16[768,1024]{1,0:T(8,128)(2,1)...) custom-call(f32[8,128]{1,0:T(8,128)S(1)} %get-tuple-element.38.live_, ...), custom_call_target="tpu_custom_call" | custom-call | tf_op jit(solution)/shard_map/attend/pallas_call | solution.py:326
  25.8 0.7 %collective-permute-start.8 = (bf16[128,256]{1,0:T(8,128)(2,1)S(1)}, bf16[128,256]{1,0:T(8,128)(2,1)S(1)}, u32[]{:S(2)}, u32[]{:S(2)}) collective-permute-start(bf16[128,256]{1,0:T(8,128)(2,1)S(1)} %get-tuple-element.55), channel_id=1, source_target_pairs={{20,0},{24,4},{28,8},{21,1},{25,5},{29,9},{22,2},{26,6},{30,10},{2... | collective-permute-start | bytes 196616 | tf_op jit(solution)/shard_map/ppermute | solution.py:344
  26.5 1.3 %collective-permute-start.9 = (bf16[128,256]{1,0:T(8,128)(2,1)S(1)}, bf16[128,256]{1,0:T(8,128)(2,1)S(1)}, u32[]{:S(2)}, u32[]{:S(2)}) collective-permute-start(bf16[128,256]{1,0:T(8,128)(2,1)S(1)} %get-tuple-element.56), channel_id=1, source_target_pairs={{16,0},{20,4},{24,8},{28,12},{17,1},{21,5},{25,9},{29,13},{18,2},{... | collective-permute-start | bytes 196616 | tf_op jit(solution)/shard_map/ppermute | solution.py:344
  27.8 4.0 %collective-permute-start.10 = (bf16[128,256]{1,0:T(8,128)(2,1)S(1)}, bf16[128,256]{1,0:T(8,128)(2,1)S(1)}, u32[]{:S(2)}, u32[]{:S(2)}) collective-permute-start(bf16[128,256]{1,0:T(8,128)(2,1)S(1)} %get-tuple-element.57), channel_id=1, source_target_pairs={{12,0},{16,4},{20,8},{24,12},{28,16},{13,1},{17,5},{21,9},{25,13},... | collective-permute-start | bytes 196616 | tf_op jit(solution)/shard_map/ppermute | solution.py:344
  31.8 1.9 %collective-permute-start.11 = (bf16[128,256]{1,0:T(8,128)(2,1)S(1)}, bf16[128,256]{1,0:T(8,128)(2,1)S(1)}, u32[]{:S(2)}, u32[]{:S(2)}) collective-permute-start(bf16[128,256]{1,0:T(8,128)(2,1)S(1)} %get-tuple-element.58), channel_id=1, source_target_pairs={{8,0},{12,4},{16,8},{20,12},{24,16},{28,20},{9,1},{13,5},{17,9},{2... | collective-permute-start | bytes 196616 | tf_op jit(solution)/shard_map/ppermute | solution.py:344
  33.7 1.9 %collective-permute-start.12 = (bf16[128,256]{1,0:T(8,128)(2,1)S(1)}, bf16[128,256]{1,0:T(8,128)(2,1)S(1)}, u32[]{:S(2)}, u32[]{:S(2)}) collective-permute-start(bf16[128,256]{1,0:T(8,128)(2,1)S(1)} %get-tuple-element.59), channel_id=1, source_target_pairs={{4,0},{8,4},{12,8},{16,12},{20,16},{24,20},{28,24},{5,1},{9,5},{13... | collective-permute-start | bytes 196616 | tf_op jit(solution)/shard_map/ppermute | solution.py:344
  35.7 1.5 %outputs.1 = (bf16[128,1024]{1,0:T(8,128)(2,1)}, bf16[128,1024]{1,0:T(8,128)(2,1)}) custom-call(bf16[768,128]{1,0:T(8,128)(2,1)S(1)} %get-tuple-element.48.key_ref, bf16[768,128]{1,0:T(8,128)(2,1)S(1)} %get-tuple-element.49.value_ref, bf16[768,1024]{1,0:T(8,128)(2,1)S(1)} %get-tuple-element.50.prob_ref, bf16[768,1024]{1,0:T(8,128)(2,1)S(1)} %get-tuple-element.51.ds_ref), custom_call_target="tpu_custom_call" | custom-call | tf_op jit(solution)/shard_map/outputs/pallas_call | solution.py:334
  37.5 1.3 %collective-permute-done.11 = bf16[128,256]{1,0:T(8,128)(2,1)S(1)} collective-permute-done((bf16[128,256]{1,0:T(8,128)(2,1)S(1)}, bf16[128,256]{1,0:T(8,128)(2,1)S(1)}, u32[]{:S(2)}, u32[]{:S(2)}) %collective-permute-start.11) | collective-permute-done | bytes 65568 | tf_op jit(solution)/shard_map/ppermute | solution.py:344
  38.7 3.1 %collective-permute-done.12 = bf16[128,256]{1,0:T(8,128)(2,1)S(1)} collective-permute-done((bf16[128,256]{1,0:T(8,128)(2,1)S(1)}, bf16[128,256]{1,0:T(8,128)(2,1)S(1)}, u32[]{:S(2)}, u32[]{:S(2)}) %collective-permute-start.12) | collective-permute-done | bytes 65568 | tf_op jit(solution)/shard_map/ppermute | solution.py:344
  41.9 0.6 %fusion = (bf16[128,128]{1,0:T(8,128)(2,1)}, bf16[128,128]{1,0:T(8,128)(2,1)}) fusion(bf16[128,256]{1,0:T(8,128)(2,1)S(1)} %add_convert_fusion), kind=kLoop, calls=%fused_computation.1 | loop fusion | bytes 131072 | tf_op jit(solution)/shard_map/slice | solution.py:345
  (10 shorter events, 1.1 us)
Async XLA Ops:
  2.2 10.2 %collective-permute-start = (bf16[128,256]{1,0:T(8,128)(2,1)S(1)}, bf16[128,256]{1,0:T(8,128)(2,1)S(1)}, u32[]{:S(2)}, u32[]{:S(2)}) collective-permute-start(bf16[128,256]{1,0:T(8,128)(2,1)S(1)} %get-tuple-element.32.refs_0_), channel_id=1, source_target_pairs={{0,16},{4,20},{8,24},{12,28},{16,0},{20,4},{24,8},{28,12},{1,17},{... | collective-permute-start | bytes 196616 | tf_op jit(solution)/shard_map/ppermute | solution.py:256
  4.9 9.7 %collective-permute-start.4 = (bf16[16,2048]{1,0:T(8,128)(2,1)S(1)}, bf16[16,2048]{1,0:T(8,128)(2,1)S(1)}, u32[]{:S(2)}, u32[]{:S(2)}) collective-permute-start(bf16[16,2048]{1,0:T(8,128)(2,1)S(1)} %get-tuple-element.44), channel_id=1, source_target_pairs={{0,16},{4,20},{8,24},{12,28},{16,0},{20,4},{24,8},{28,12},{1,17},{... | collective-permute-start | bytes 196616 | tf_op jit(solution)/shard_map/ppermute | solution.py:256
  5.2 10.8 %collective-permute-start.5 = (bf16[16,2048]{1,0:T(8,128)(2,1)S(1)}, bf16[16,2048]{1,0:T(8,128)(2,1)S(1)}, u32[]{:S(2)}, u32[]{:S(2)}) collective-permute-start(bf16[16,2048]{1,0:T(8,128)(2,1)S(1)} %get-tuple-element.45), channel_id=1, source_target_pairs={{0,20},{4,16},{8,28},{12,24},{16,4},{20,0},{24,12},{28,8},{1,21},{... | collective-permute-start | bytes 196616 | tf_op jit(solution)/shard_map/ppermute | solution.py:256
  7.7 11.1 %collective-permute-start.6 = (bf16[16,2048]{1,0:T(8,128)(2,1)S(1)}, bf16[16,2048]{1,0:T(8,128)(2,1)S(1)}, u32[]{:S(2)}, u32[]{:S(2)}) collective-permute-start(bf16[16,2048]{1,0:T(8,128)(2,1)S(1)} %get-tuple-element.46), channel_id=1, source_target_pairs={{0,24},{4,28},{8,16},{12,20},{16,8},{20,12},{24,0},{28,4},{1,25},{... | collective-permute-start | bytes 196616 | tf_op jit(solution)/shard_map/ppermute | solution.py:256
  7.7 11.3 %collective-permute-start.7 = (bf16[16,2048]{1,0:T(8,128)(2,1)S(1)}, bf16[16,2048]{1,0:T(8,128)(2,1)S(1)}, u32[]{:S(2)}, u32[]{:S(2)}) collective-permute-start(bf16[16,2048]{1,0:T(8,128)(2,1)S(1)} %get-tuple-element.47), channel_id=1, source_target_pairs={{0,28},{4,24},{8,20},{12,16},{16,12},{20,8},{24,4},{28,0},{1,29},{... | collective-permute-start | bytes 196616 | tf_op jit(solution)/shard_map/ppermute | solution.py:256
  12.7 6.9 %collective-permute-start.1 = (bf16[16,5120]{1,0:T(8,128)(2,1)S(1)}, bf16[16,5120]{1,0:T(8,128)(2,1)S(1)}, u32[]{:S(2)}, u32[]{:S(2)}) collective-permute-start(bf16[16,5120]{1,0:T(8,128)(2,1)S(1)} %get-tuple-element.41), channel_id=1, source_target_pairs={{0,4},{4,0},{8,12},{12,8},{16,20},{20,16},{24,28},{28,24},{1,5},{5... | collective-permute-start | bytes 491528 | tf_op jit(solution)/shard_map/ppermute | solution.py:256
  14.6 6.8 %collective-permute-start.2 = (bf16[16,5120]{1,0:T(8,128)(2,1)S(1)}, bf16[16,5120]{1,0:T(8,128)(2,1)S(1)}, u32[]{:S(2)}, u32[]{:S(2)}) collective-permute-start(bf16[16,5120]{1,0:T(8,128)(2,1)S(1)} %get-tuple-element.42), channel_id=1, source_target_pairs={{0,8},{4,12},{8,0},{12,4},{16,24},{20,28},{24,16},{28,20},{1,9},{5... | collective-permute-start | bytes 491528 | tf_op jit(solution)/shard_map/ppermute | solution.py:256
  16.0 8.3 %collective-permute-start.3 = (bf16[16,5120]{1,0:T(8,128)(2,1)S(1)}, bf16[16,5120]{1,0:T(8,128)(2,1)S(1)}, u32[]{:S(2)}, u32[]{:S(2)}) collective-permute-start(bf16[16,5120]{1,0:T(8,128)(2,1)S(1)} %get-tuple-element.43), channel_id=1, source_target_pairs={{0,12},{4,8},{8,4},{12,0},{16,28},{20,24},{24,20},{28,16},{1,13},{... | collective-permute-start | bytes 491528 | tf_op jit(solution)/shard_map/ppermute | solution.py:256
  25.8 11.4 %collective-permute-start.8 = (bf16[128,256]{1,0:T(8,128)(2,1)S(1)}, bf16[128,256]{1,0:T(8,128)(2,1)S(1)}, u32[]{:S(2)}, u32[]{:S(2)}) collective-permute-start(bf16[128,256]{1,0:T(8,128)(2,1)S(1)} %get-tuple-element.55), channel_id=1, source_target_pairs={{20,0},{24,4},{28,8},{21,1},{25,5},{29,9},{22,2},{26,6},{30,10},{2... | collective-permute-start | bytes 196616 | tf_op jit(solution)/shard_map/ppermute | solution.py:344
  26.5 10.7 %collective-permute-start.9 = (bf16[128,256]{1,0:T(8,128)(2,1)S(1)}, bf16[128,256]{1,0:T(8,128)(2,1)S(1)}, u32[]{:S(2)}, u32[]{:S(2)}) collective-permute-start(bf16[128,256]{1,0:T(8,128)(2,1)S(1)} %get-tuple-element.56), channel_id=1, source_target_pairs={{16,0},{20,4},{24,8},{28,12},{17,1},{21,5},{25,9},{29,13},{18,2},{... | collective-permute-start | bytes 196616 | tf_op jit(solution)/shard_map/ppermute | solution.py:344
  27.8 9.7 %collective-permute-start.10 = (bf16[128,256]{1,0:T(8,128)(2,1)S(1)}, bf16[128,256]{1,0:T(8,128)(2,1)S(1)}, u32[]{:S(2)}, u32[]{:S(2)}) collective-permute-start(bf16[128,256]{1,0:T(8,128)(2,1)S(1)} %get-tuple-element.57), channel_id=1, source_target_pairs={{12,0},{16,4},{20,8},{24,12},{28,16},{13,1},{17,5},{21,9},{25,13},... | collective-permute-start | bytes 196616 | tf_op jit(solution)/shard_map/ppermute | solution.py:344
  31.8 6.9 %collective-permute-start.11 = (bf16[128,256]{1,0:T(8,128)(2,1)S(1)}, bf16[128,256]{1,0:T(8,128)(2,1)S(1)}, u32[]{:S(2)}, u32[]{:S(2)}) collective-permute-start(bf16[128,256]{1,0:T(8,128)(2,1)S(1)} %get-tuple-element.58), channel_id=1, source_target_pairs={{8,0},{12,4},{16,8},{20,12},{24,16},{28,20},{9,1},{13,5},{17,9},{2... | collective-permute-start | bytes 196616 | tf_op jit(solution)/shard_map/ppermute | solution.py:344
  33.7 8.1 %collective-permute-start.12 = (bf16[128,256]{1,0:T(8,128)(2,1)S(1)}, bf16[128,256]{1,0:T(8,128)(2,1)S(1)}, u32[]{:S(2)}, u32[]{:S(2)}) collective-permute-start(bf16[128,256]{1,0:T(8,128)(2,1)S(1)} %get-tuple-element.59), channel_id=1, source_target_pairs={{4,0},{8,4},{12,8},{16,12},{20,16},{24,20},{28,24},{5,1},{9,5},{13... | collective-permute-start | bytes 196616 | tf_op jit(solution)/shard_map/ppermute | solution.py:344

commit v11 on v10

--- a/solution.py
+++ b/solution.py
@@ -138,6 +138,13 @@
     out_ref[...] = dot(place_ref[SPAN * out_ref.shape[0] :, :], rows, ((1,), (0,))).astype(BF16)
 
 
+def for_live(live_ref, body):
+    live = jnp.max(live_ref[...])
+    pl.when(live > SPAN)(lambda: body(0))
+    for skipped in range(1, SPAN + 1):
+        pl.when(live == SPAN + 1 - skipped)(functools.partial(body, skipped))
+
+
 def attend_kernel(width, head, pieces, live_ref, mask_ref, place_ref, *refs):
     near = max(1, pieces // 2)
     in_refs = refs[:near]
@@ -172,13 +179,8 @@
     queries = placed(0, width)
     grads = placed(width, base)
 
-    live = jnp.max(live_ref[...])
-
     def attend(skipped):
         dead = skipped * tok
-        for ref in (key_ref, value_ref, prob_ref, ds_ref):
-            if dead:
-                ref[:dead, :] = jnp.zeros((dead, ref.shape[1]), BF16)
         for block in range(skipped, SPAN + 1):
             rows = slice(block * tok, (block + 1) * tok)
             both = dot(place_ref[rows, :], window(block), ((1,), (0,))).astype(BF16)
@@ -217,24 +219,27 @@
                 ref[:, :head] = key_grad[rows, :].astype(ref.dtype)
                 ref[:, head:] = value_grad[rows, :].astype(ref.dtype)
 
-    pl.when(live > SPAN)(lambda: attend(0))
-    for skipped in range(1, SPAN + 1):
-        pl.when(live == SPAN + 1 - skipped)(functools.partial(attend, skipped))
-
-
-def output_kernel(key_ref, value_ref, prob_ref, ds_ref, attn_ref, dq_ref):
+    for_live(live_ref, attend)
+
+
+def output_kernel(live_ref, key_ref, value_ref, prob_ref, ds_ref, attn_ref, dq_ref):
     tok, width = attn_ref.shape
     head = key_ref.shape[1]
     scale = 1.0 / math.sqrt(head)
     pairs = 4
-    for first in range(0, width // head, pairs):
-        cols = slice(first * tok, (first + pairs) * tok)
-        out_t = dot(value_ref[...], prob_ref[:, cols], ((0,), (0,)))
-        dq_t = dot(key_ref[...], ds_ref[:, cols], ((0,), (0,))) * scale
-        for i in range(pairs):
-            s = slice((first + i) * head, (first + i + 1) * head)
-            attn_ref[:, s] = jnp.transpose(out_t[:, i * tok : (i + 1) * tok]).astype(BF16)
-            dq_ref[:, s] = jnp.transpose(dq_t[:, i * tok : (i + 1) * tok]).astype(BF16)
+
+    def outputs(skipped):
+        dead = skipped * tok
+        for first in range(0, width // head, pairs):
+            cols = slice(first * tok, (first + pairs) * tok)
+            out_t = dot(value_ref[dead:, :], prob_ref[dead:, cols], ((0,), (0,)))
+            dq_t = dot(key_ref[dead:, :], ds_ref[dead:, cols], ((0,), (0,))) * scale
+            for i in range(pairs):
+                s = slice((first + i) * head, (first + i + 1) * head)
+                attn_ref[:, s] = jnp.transpose(out_t[:, i * tok : (i + 1) * tok]).astype(BF16)
+                dq_ref[:, s] = jnp.transpose(dq_t[:, i * tok : (i + 1) * tok]).astype(BF16)
+
+    for_live(live_ref, outputs)
 
 
 def per_device(query, key, value, grad_out, loader_pos, doc_lengths):
@@ -334,11 +339,11 @@
     attn_out, dquery = pl.pallas_call(
         output_kernel,
         out_shape=[wide, wide],
-        in_specs=[vmem] * 4,
+        in_specs=[vmem] * 5,
         out_specs=[vmem] * 2,
         compiler_params=params,
         name="outputs",
-    )(keys, values, probs, grad_scores)
+    )(live, keys, values, probs, grad_scores)
     for offset in range(SPAN, 0, -1):
         pairs = [(source, source - offset) for source in range(offset, devices)]
         summed = summed + lax.ppermute(parts[offset - 1], "dcp", pairs).astype(F32)

time: 42.9 us -> 43.2 us (level)
  starting transfers between devices: 22.4 us -> 21.4 us
  Pallas kernels: 6.31 us -> 7.08 us
    ppermute x5, starting transfers between devices: 9.79 us -> 8.84 us  [per_device(): summed = summed + lax.ppermute(parts[offset - 1], 'dcp', pairs).astype(F32)]
    pallas_call x1, Pallas kernels: 1.44 us -> 2.25 us  [per_device(): pl.pallas_call(functools.partial(attend_kernel, width, head, pieces), out...]
where the time goes in v11:
time: 43.2 us; the launch traced here: 42.5 us
  starting transfers between devices  21.4 us (50%)
  waiting for transfers between devices  12.6 us (29%)
  Pallas kernels  7.08 us (16%)
  between operations  0.73 us (2%)
  local copies, waits for them, and re-layouts  0.63 us (1%)
    ppermute x8, starting transfers between devices, swapped(): return lax.ppermute(rows, 'dcp', [(d, d ^ step) for d in range(devices)])  12.6 us
    ppermute x5, starting transfers between devices, per_device(): summed = summed + lax.ppermute(parts[offset - 1], 'dcp', pairs).astype(F32)  8.84 us
    ppermute x8, waiting for transfers between devices, swapped(): return lax.ppermute(rows, 'dcp', [(d, d ^ step) for d in range(devices)])  7.79 us
    ppermute x5, waiting for transfers between devices, per_device(): summed = summed + lax.ppermute(parts[offset - 1], 'dcp', pairs).astype(F32)  4.79 us
    pallas_call x1, Pallas kernels, per_device(): pl.pallas_call(functools.partial(attend_kernel, width, head, pieces), out...  2.25 us
    pallas_call x1, Pallas kernels, per_device(): pl.pallas_call(functools.partial(pack_kernel, per_peer, paired), out_shap...  1.58 us
    pallas_call x1, Pallas kernels, per_device(): pl.pallas_call(output_kernel, out_shape=[wide, wide], in_specs=[vmem] * 5...  1.5 us
    pallas_call x1, Pallas kernels, per_device(): pl.pallas_call(functools.partial(slots_kernel, per_peer, paired), out_sha...  1.21 us
  transfers between devices with their start and end apart: 13, of which 10 were waited for; matrix products, arithmetic and copies ran while one was open for 0% of the time, Pallas kernels for 8%

profile of v11, /device:TPU:14, one launch (start us, length us, event | category | flops | bytes accessed | tf_op | source)
XLA Modules:
  0.0 42.5 jit_solution(9675813304845960274)
XLA Ops:
  0.6 1.6 %pack.1 = (bf16[128,256]{1,0:T(8,128)(2,1)S(1)}, bf16[16,2048]{1,0:T(8,128)(2,1)S(1)}, bf16[16,2048]{1,0:T(8,128)(2,1)S(1)}, bf16[16,2048]{1,0:T(8,128)(2,1)S(1)...) custom-call(s32[8,128]{1,0:T(8,128)} %bitcast.1, ...), custom_call_target="tpu_custom_call" | custom-call | tf_op jit(solution)/shard_map/pack/pallas_call | solution.py:263
  2.2 2.7 %collective-permute-start = (bf16[128,256]{1,0:T(8,128)(2,1)S(1)}, bf16[128,256]{1,0:T(8,128)(2,1)S(1)}, u32[]{:S(2)}, u32[]{:S(2)}) collective-permute-start(bf16[128,256]{1,0:T(8,128)(2,1)S(1)} %get-tuple-element.32.refs_0_), channel_id=1, source_target_pairs={{0,16},{4,20},{8,24},{12,28},{16,0},{20,4},{24,8},{28,12},{1,17},{... | collective-permute-start | bytes 196616 | tf_op jit(solution)/shard_map/ppermute | solution.py:261
  4.9 0.3 collective-permute-start.4
  5.2 2.5 %collective-permute-start.5 = (bf16[16,2048]{1,0:T(8,128)(2,1)S(1)}, bf16[16,2048]{1,0:T(8,128)(2,1)S(1)}, u32[]{:S(2)}, u32[]{:S(2)}) collective-permute-start(bf16[16,2048]{1,0:T(8,128)(2,1)S(1)} %get-tuple-element.45), channel_id=1, source_target_pairs={{0,20},{4,16},{8,28},{12,24},{16,4},{20,0},{24,12},{28,8},{1,21},{... | collective-permute-start | bytes 196616 | tf_op jit(solution)/shard_map/ppermute | solution.py:261
  7.7 3.0 %collective-permute-start.7 = (bf16[16,2048]{1,0:T(8,128)(2,1)S(1)}, bf16[16,2048]{1,0:T(8,128)(2,1)S(1)}, u32[]{:S(2)}, u32[]{:S(2)}) collective-permute-start(bf16[16,2048]{1,0:T(8,128)(2,1)S(1)} %get-tuple-element.47), channel_id=1, source_target_pairs={{0,28},{4,24},{8,20},{12,16},{16,12},{20,8},{24,4},{28,0},{1,29},{... | collective-permute-start | bytes 196616 | tf_op jit(solution)/shard_map/ppermute | solution.py:261
  10.7 1.7 %collective-permute-done.refs_1_ = bf16[128,256]{1,0:T(8,128)(2,1)S(1)} collective-permute-done((bf16[128,256]{1,0:T(8,128)(2,1)S(1)}, bf16[128,256]{1,0:T(8,128)(2,1)S(1)}, u32[]{:S(2)}, u32[]{:S(2)}) %collective-permute-start) | collective-permute-done | bytes 65568 | tf_op jit(solution)/shard_map/ppermute | solution.py:261
  12.8 1.2 %slots.1 = (bf16[768,128]{1,0:T(8,128)(2,1)S(1)}, f32[768,128]{1,0:T(8,128)S(1)}, f32[8,128]{1,0:T(8,128)S(1)}) custom-call(s32[8,128]{1,0:T(8,128)} %bitcast.2, s32[3]{0:T(128)} %len_hbm.1, bf16[16,5120]{1,0:T(8,128)(2,1)S(1)} %get-tuple-element.37._.refs_0_), custom_call_target="tpu_custom_call" | custom-call | tf_op jit(solution)/shard_map/slots/pallas_call | solution.py:297
  14.0 0.5 %collective-permute-done.4.refs_0_ = bf16[16,2048]{1,0:T(8,128)(2,1)S(1)} collective-permute-done((bf16[16,2048]{1,0:T(8,128)(2,1)S(1)}, bf16[16,2048]{1,0:T(8,128)(2,1)S(1)}, u32[]{:S(2)}, u32[]{:S(2)}) %collective-permute-start.4) | collective-permute-done | bytes 65568 | tf_op jit(solution)/shard_map/ppermute | solution.py:261
  14.6 1.2 %collective-permute-start.2 = (bf16[16,5120]{1,0:T(8,128)(2,1)S(1)}, bf16[16,5120]{1,0:T(8,128)(2,1)S(1)}, u32[]{:S(2)}, u32[]{:S(2)}) collective-permute-start(bf16[16,5120]{1,0:T(8,128)(2,1)S(1)} %get-tuple-element.42), channel_id=1, source_target_pairs={{0,8},{4,12},{8,0},{12,4},{16,24},{20,28},{24,16},{28,20},{1,9},{5... | collective-permute-start | bytes 491528 | tf_op jit(solution)/shard_map/ppermute | solution.py:261
  16.0 2.8 %collective-permute-start.3 = (bf16[16,5120]{1,0:T(8,128)(2,1)S(1)}, bf16[16,5120]{1,0:T(8,128)(2,1)S(1)}, u32[]{:S(2)}, u32[]{:S(2)}) collective-permute-start(bf16[16,5120]{1,0:T(8,128)(2,1)S(1)} %get-tuple-element.43), channel_id=1, source_target_pairs={{0,12},{4,8},{8,4},{12,0},{16,28},{20,24},{24,20},{28,16},{1,13},{... | collective-permute-start | bytes 491528 | tf_op jit(solution)/shard_map/ppermute | solution.py:261
  19.3 0.3 collective-permute-done.1.refs_1_
  19.6 1.8 %collective-permute-done.2.refs_2_ = bf16[16,5120]{1,0:T(8,128)(2,1)S(1)} collective-permute-done((bf16[16,5120]{1,0:T(8,128)(2,1)S(1)}, bf16[16,5120]{1,0:T(8,128)(2,1)S(1)}, u32[]{:S(2)}, u32[]{:S(2)}) %collective-permute-start.2) | collective-permute-done | bytes 163872 | tf_op jit(solution)/shard_map/ppermute | solution.py:261
  21.4 3.0 %collective-permute-done.3.refs_3_ = bf16[16,5120]{1,0:T(8,128)(2,1)S(1)} collective-permute-done((bf16[16,5120]{1,0:T(8,128)(2,1)S(1)}, bf16[16,5120]{1,0:T(8,128)(2,1)S(1)}, u32[]{:S(2)}, u32[]{:S(2)}) %collective-permute-start.3) | collective-permute-done | bytes 163872 | tf_op jit(solution)/shard_map/ppermute | solution.py:261
  24.4 2.3 %attend.1 = (bf16[768,128]{1,0:T(8,128)(2,1)S(1)}, bf16[768,128]{1,0:T(8,128)(2,1)S(1)}, bf16[768,1024]{1,0:T(8,128)(2,1)S(1)}, bf16[768,1024]{1,0:T(8,128)(2,1)...) custom-call(f32[8,128]{1,0:T(8,128)S(1)} %get-tuple-element.38.live_, ...), custom_call_target="tpu_custom_call" | custom-call | tf_op jit(solution)/shard_map/attend/pallas_call | solution.py:331
  26.6 0.7 %collective-permute-start.8 = (bf16[128,256]{1,0:T(8,128)(2,1)S(1)}, bf16[128,256]{1,0:T(8,128)(2,1)S(1)}, u32[]{:S(2)}, u32[]{:S(2)}) collective-permute-start(bf16[128,256]{1,0:T(8,128)(2,1)S(1)} %get-tuple-element.55), channel_id=1, source_target_pairs={{20,0},{24,4},{28,8},{21,1},{25,5},{29,9},{22,2},{26,6},{30,10},{2... | collective-permute-start | bytes 196616 | tf_op jit(solution)/shard_map/ppermute | solution.py:349
  27.3 1.3 %collective-permute-start.9 = (bf16[128,256]{1,0:T(8,128)(2,1)S(1)}, bf16[128,256]{1,0:T(8,128)(2,1)S(1)}, u32[]{:S(2)}, u32[]{:S(2)}) collective-permute-start(bf16[128,256]{1,0:T(8,128)(2,1)S(1)} %get-tuple-element.56), channel_id=1, source_target_pairs={{16,0},{20,4},{24,8},{28,12},{17,1},{21,5},{25,9},{29,13},{18,2},{... | collective-permute-start | bytes 196616 | tf_op jit(solution)/shard_map/ppermute | solution.py:349
  28.6 3.0 %collective-permute-start.10 = (bf16[128,256]{1,0:T(8,128)(2,1)S(1)}, bf16[128,256]{1,0:T(8,128)(2,1)S(1)}, u32[]{:S(2)}, u32[]{:S(2)}) collective-permute-start(bf16[128,256]{1,0:T(8,128)(2,1)S(1)} %get-tuple-element.57), channel_id=1, source_target_pairs={{12,0},{16,4},{20,8},{24,12},{28,16},{13,1},{17,5},{21,9},{25,13},... | collective-permute-start | bytes 196616 | tf_op jit(solution)/shard_map/ppermute | solution.py:349
  31.7 1.9 %collective-permute-start.11 = (bf16[128,256]{1,0:T(8,128)(2,1)S(1)}, bf16[128,256]{1,0:T(8,128)(2,1)S(1)}, u32[]{:S(2)}, u32[]{:S(2)}) collective-permute-start(bf16[128,256]{1,0:T(8,128)(2,1)S(1)} %get-tuple-element.58), channel_id=1, source_target_pairs={{8,0},{12,4},{16,8},{20,12},{24,16},{28,20},{9,1},{13,5},{17,9},{2... | collective-permute-start | bytes 196616 | tf_op jit(solution)/shard_map/ppermute | solution.py:349
  33.6 1.9 %collective-permute-start.12 = (bf16[128,256]{1,0:T(8,128)(2,1)S(1)}, bf16[128,256]{1,0:T(8,128)(2,1)S(1)}, u32[]{:S(2)}, u32[]{:S(2)}) collective-permute-start(bf16[128,256]{1,0:T(8,128)(2,1)S(1)} %get-tuple-element.59), channel_id=1, source_target_pairs={{4,0},{8,4},{12,8},{16,12},{20,16},{24,20},{28,24},{5,1},{9,5},{13... | collective-permute-start | bytes 196616 | tf_op jit(solution)/shard_map/ppermute | solution.py:349
  35.5 1.5 %outputs.1 = (bf16[128,1024]{1,0:T(8,128)(2,1)}, bf16[128,1024]{1,0:T(8,128)(2,1)}) custom-call(f32[8,128]{1,0:T(8,128)S(1)} %get-tuple-element.38.live_ref, bf16[768,128]{1,0:T(8,128)(2,1)S(1)} %get-tuple-element.48.key_ref, bf16[768,128]{1,0:T(8,128)(2,1)S(1)} %get-tuple-element.49.value_ref, bf16[768,1024]{1,0:T(8,128)(2,1)S(1)} %get-tuple-element.50.prob_ref, ...), custom_call_target="tpu_custom_call" | custom-call | tf_op jit(solution)/shard_map/outputs/pallas_call | solution.py:339
  37.0 1.4 %collective-permute-done.10 = bf16[128,256]{1,0:T(8,128)(2,1)S(1)} collective-permute-done((bf16[128,256]{1,0:T(8,128)(2,1)S(1)}, bf16[128,256]{1,0:T(8,128)(2,1)S(1)}, u32[]{:S(2)}, u32[]{:S(2)}) %collective-permute-start.10) | collective-permute-done | bytes 65568 | tf_op jit(solution)/shard_map/ppermute | solution.py:349
  38.4 1.1 %collective-permute-done.11 = bf16[128,256]{1,0:T(8,128)(2,1)S(1)} collective-permute-done((bf16[128,256]{1,0:T(8,128)(2,1)S(1)}, bf16[128,256]{1,0:T(8,128)(2,1)S(1)}, u32[]{:S(2)}, u32[]{:S(2)}) %collective-permute-start.11) | collective-permute-done | bytes 65568 | tf_op jit(solution)/shard_map/ppermute | solution.py:349
  39.6 2.3 %collective-permute-done.12 = bf16[128,256]{1,0:T(8,128)(2,1)S(1)} collective-permute-done((bf16[128,256]{1,0:T(8,128)(2,1)S(1)}, bf16[128,256]{1,0:T(8,128)(2,1)S(1)}, u32[]{:S(2)}, u32[]{:S(2)}) %collective-permute-start.12) | collective-permute-done | bytes 65568 | tf_op jit(solution)/shard_map/ppermute | solution.py:349
  41.9 0.6 %fusion = (bf16[128,128]{1,0:T(8,128)(2,1)}, bf16[128,128]{1,0:T(8,128)(2,1)}) fusion(bf16[128,256]{1,0:T(8,128)(2,1)S(1)} %add_convert_fusion), kind=kLoop, calls=%fused_computation.1 | loop fusion | bytes 131072 | tf_op jit(solution)/shard_map/slice | solution.py:350
  (10 shorter events, 1.1 us)
Async XLA Ops:
  2.2 10.2 %collective-permute-start = (bf16[128,256]{1,0:T(8,128)(2,1)S(1)}, bf16[128,256]{1,0:T(8,128)(2,1)S(1)}, u32[]{:S(2)}, u32[]{:S(2)}) collective-permute-start(bf16[128,256]{1,0:T(8,128)(2,1)S(1)} %get-tuple-element.32.refs_0_), channel_id=1, source_target_pairs={{0,16},{4,20},{8,24},{12,28},{16,0},{20,4},{24,8},{28,12},{1,17},{... | collective-permute-start | bytes 196616 | tf_op jit(solution)/shard_map/ppermute | solution.py:261
  4.9 9.7 %collective-permute-start.4 = (bf16[16,2048]{1,0:T(8,128)(2,1)S(1)}, bf16[16,2048]{1,0:T(8,128)(2,1)S(1)}, u32[]{:S(2)}, u32[]{:S(2)}) collective-permute-start(bf16[16,2048]{1,0:T(8,128)(2,1)S(1)} %get-tuple-element.44), channel_id=1, source_target_pairs={{0,16},{4,20},{8,24},{12,28},{16,0},{20,4},{24,8},{28,12},{1,17},{... | collective-permute-start | bytes 196616 | tf_op jit(solution)/shard_map/ppermute | solution.py:261
  5.2 10.8 %collective-permute-start.5 = (bf16[16,2048]{1,0:T(8,128)(2,1)S(1)}, bf16[16,2048]{1,0:T(8,128)(2,1)S(1)}, u32[]{:S(2)}, u32[]{:S(2)}) collective-permute-start(bf16[16,2048]{1,0:T(8,128)(2,1)S(1)} %get-tuple-element.45), channel_id=1, source_target_pairs={{0,20},{4,16},{8,28},{12,24},{16,4},{20,0},{24,12},{28,8},{1,21},{... | collective-permute-start | bytes 196616 | tf_op jit(solution)/shard_map/ppermute | solution.py:261
  7.7 11.1 %collective-permute-start.6 = (bf16[16,2048]{1,0:T(8,128)(2,1)S(1)}, bf16[16,2048]{1,0:T(8,128)(2,1)S(1)}, u32[]{:S(2)}, u32[]{:S(2)}) collective-permute-start(bf16[16,2048]{1,0:T(8,128)(2,1)S(1)} %get-tuple-element.46), channel_id=1, source_target_pairs={{0,24},{4,28},{8,16},{12,20},{16,8},{20,12},{24,0},{28,4},{1,25},{... | collective-permute-start | bytes 196616 | tf_op jit(solution)/shard_map/ppermute | solution.py:261
  7.7 11.3 %collective-permute-start.7 = (bf16[16,2048]{1,0:T(8,128)(2,1)S(1)}, bf16[16,2048]{1,0:T(8,128)(2,1)S(1)}, u32[]{:S(2)}, u32[]{:S(2)}) collective-permute-start(bf16[16,2048]{1,0:T(8,128)(2,1)S(1)} %get-tuple-element.47), channel_id=1, source_target_pairs={{0,28},{4,24},{8,20},{12,16},{16,12},{20,8},{24,4},{28,0},{1,29},{... | collective-permute-start | bytes 196616 | tf_op jit(solution)/shard_map/ppermute | solution.py:261
  12.7 6.9 %collective-permute-start.1 = (bf16[16,5120]{1,0:T(8,128)(2,1)S(1)}, bf16[16,5120]{1,0:T(8,128)(2,1)S(1)}, u32[]{:S(2)}, u32[]{:S(2)}) collective-permute-start(bf16[16,5120]{1,0:T(8,128)(2,1)S(1)} %get-tuple-element.41), channel_id=1, source_target_pairs={{0,4},{4,0},{8,12},{12,8},{16,20},{20,16},{24,28},{28,24},{1,5},{5... | collective-permute-start | bytes 491528 | tf_op jit(solution)/shard_map/ppermute | solution.py:261
  14.6 6.8 %collective-permute-start.2 = (bf16[16,5120]{1,0:T(8,128)(2,1)S(1)}, bf16[16,5120]{1,0:T(8,128)(2,1)S(1)}, u32[]{:S(2)}, u32[]{:S(2)}) collective-permute-start(bf16[16,5120]{1,0:T(8,128)(2,1)S(1)} %get-tuple-element.42), channel_id=1, source_target_pairs={{0,8},{4,12},{8,0},{12,4},{16,24},{20,28},{24,16},{28,20},{1,9},{5... | collective-permute-start | bytes 491528 | tf_op jit(solution)/shard_map/ppermute | solution.py:261
  16.0 8.3 %collective-permute-start.3 = (bf16[16,5120]{1,0:T(8,128)(2,1)S(1)}, bf16[16,5120]{1,0:T(8,128)(2,1)S(1)}, u32[]{:S(2)}, u32[]{:S(2)}) collective-permute-start(bf16[16,5120]{1,0:T(8,128)(2,1)S(1)} %get-tuple-element.43), channel_id=1, source_target_pairs={{0,12},{4,8},{8,4},{12,0},{16,28},{20,24},{24,20},{28,16},{1,13},{... | collective-permute-start | bytes 491528 | tf_op jit(solution)/shard_map/ppermute | solution.py:261
  26.6 10.4 %collective-permute-start.8 = (bf16[128,256]{1,0:T(8,128)(2,1)S(1)}, bf16[128,256]{1,0:T(8,128)(2,1)S(1)}, u32[]{:S(2)}, u32[]{:S(2)}) collective-permute-start(bf16[128,256]{1,0:T(8,128)(2,1)S(1)} %get-tuple-element.55), channel_id=1, source_target_pairs={{20,0},{24,4},{28,8},{21,1},{25,5},{29,9},{22,2},{26,6},{30,10},{2... | collective-permute-start | bytes 196616 | tf_op jit(solution)/shard_map/ppermute | solution.py:349
  27.3 9.7 %collective-permute-start.9 = (bf16[128,256]{1,0:T(8,128)(2,1)S(1)}, bf16[128,256]{1,0:T(8,128)(2,1)S(1)}, u32[]{:S(2)}, u32[]{:S(2)}) collective-permute-start(bf16[128,256]{1,0:T(8,128)(2,1)S(1)} %get-tuple-element.56), channel_id=1, source_target_pairs={{16,0},{20,4},{24,8},{28,12},{17,1},{21,5},{25,9},{29,13},{18,2},{... | collective-permute-start | bytes 196616 | tf_op jit(solution)/shard_map/ppermute | solution.py:349
  28.6 9.8 %collective-permute-start.10 = (bf16[128,256]{1,0:T(8,128)(2,1)S(1)}, bf16[128,256]{1,0:T(8,128)(2,1)S(1)}, u32[]{:S(2)}, u32[]{:S(2)}) collective-permute-start(bf16[128,256]{1,0:T(8,128)(2,1)S(1)} %get-tuple-element.57), channel_id=1, source_target_pairs={{12,0},{16,4},{20,8},{24,12},{28,16},{13,1},{17,5},{21,9},{25,13},... | collective-permute-start | bytes 196616 | tf_op jit(solution)/shard_map/ppermute | solution.py:349
  31.7 7.9 %collective-permute-start.11 = (bf16[128,256]{1,0:T(8,128)(2,1)S(1)}, bf16[128,256]{1,0:T(8,128)(2,1)S(1)}, u32[]{:S(2)}, u32[]{:S(2)}) collective-permute-start(bf16[128,256]{1,0:T(8,128)(2,1)S(1)} %get-tuple-element.58), channel_id=1, source_target_pairs={{8,0},{12,4},{16,8},{20,12},{24,16},{28,20},{9,1},{13,5},{17,9},{2... | collective-permute-start | bytes 196616 | tf_op jit(solution)/shard_map/ppermute | solution.py:349
  33.6 8.2 %collective-permute-start.12 = (bf16[128,256]{1,0:T(8,128)(2,1)S(1)}, bf16[128,256]{1,0:T(8,128)(2,1)S(1)}, u32[]{:S(2)}, u32[]{:S(2)}) collective-permute-start(bf16[128,256]{1,0:T(8,128)(2,1)S(1)} %get-tuple-element.59), channel_id=1, source_target_pairs={{4,0},{8,4},{12,8},{16,12},{20,16},{24,20},{28,24},{5,1},{9,5},{13... | collective-permute-start | bytes 196616 | tf_op jit(solution)/shard_map/ppermute | solution.py:349

commit v12 on v11

--- a/solution.py
+++ b/solution.py
@@ -278,22 +278,6 @@
         name="pack",
     )(positions, sides[1], sides[2], sides[0], sides[3])
     held = [ordered, swapped(ordered, near)] if paired else [ordered]
-    for step in range(near, pieces if paired else 0):
-        packed[step] = swapped(packed[step], step)
-    cols = base + 2 * head * (SPAN + 1) * len(held)
-    packed[:near] = pl.pallas_call(
-        functools.partial(near_kernel, per_peer, paired, len(held)),
-        out_shape=[jax.ShapeDtypeStruct((tok // pieces, cols), BF16)] * near,
-        in_specs=[vmem] * (len(held) + near),
-        out_specs=[vmem] * near,
-        compiler_params=params,
-        name="near",
-    )(*held, *packed[:near])
-    if paired:
-        for step in range(1, near):
-            packed[step] = swapped(packed[step], step)
-    else:
-        packed = [lax.all_to_all(packed[0], "dcp", split_axis=0, concat_axis=0, tiled=True)]
     places, mask, live = pl.pallas_call(
         functools.partial(slots_kernel, per_peer, paired),
         out_shape=[
@@ -312,6 +296,23 @@
         compiler_params=params,
         name="slots",
     )(positions, lengths, packed[0])
+    places, *packed[near + 1 :] = lax.optimization_barrier((places, *packed[near + 1 :]))
+    for step in range(near, pieces if paired else 0):
+        packed[step] = swapped(packed[step], step)
+    cols = base + 2 * head * (SPAN + 1) * len(held)
+    packed[:near] = pl.pallas_call(
+        functools.partial(near_kernel, per_peer, paired, len(held)),
+        out_shape=[jax.ShapeDtypeStruct((tok // pieces, cols), BF16)] * near,
+        in_specs=[vmem] * (len(held) + near),
+        out_specs=[vmem] * near,
+        compiler_params=params,
+        name="near",
+    )(*held, *packed[:near])
+    if paired:
+        for step in range(1, near):
+            packed[step] = swapped(packed[step], step)
+    else:
+        packed = [lax.all_to_all(packed[0], "dcp", split_axis=0, concat_axis=0, tiled=True)]
     wide = jax.ShapeDtypeStruct((tok, width), BF16)
     if paired:
         far = pl.pallas_call(

time: 43.2 us -> 43 us (level); the launches traced: 42.5 us -> 43 us
  waiting for transfers between devices: 12.6 us -> 14.9 us
  Pallas kernels: 7.08 us -> 6.04 us
  starting transfers between devices: 21.4 us -> 20.6 us
    ppermute x8, waiting for transfers between devices: 7.79 us -> 9.41 us  [swapped(): return lax.ppermute(rows, 'dcp', [(d, d ^ step) for d in range(devices)])]
    pallas_call x1, Pallas kernels: 2.25 us -> 1.32 us  [per_device(): pl.pallas_call(functools.partial(attend_kernel, width, head, pieces), out...]
    ppermute x8, starting transfers between devices: 12.6 us -> 11.7 us  [swapped(): return lax.ppermute(rows, 'dcp', [(d, d ^ step) for d in range(devices)])]
    ppermute x5, waiting for transfers between devices: 4.79 us -> 5.51 us  [per_device(): summed = summed + lax.ppermute(parts[offset - 1], 'dcp', pairs).astype(F32)]
  transfers between devices with their start and end apart: 13 -> 13, of which waited for: 10 -> 7; matrix products, arithmetic and copies ran while one was open for 0% -> 0% of each run, Pallas kernels for 8% -> 7%
where the time goes in v12:
time: 43 us
  starting transfers between devices  20.6 us (48%)
  waiting for transfers between devices  14.9 us (35%)
  Pallas kernels  6.04 us (14%)
  between operations  0.74 us (2%)
  local copies, waits for them, and re-layouts  0.63 us (1%)
    ppermute x8, starting transfers between devices, swapped(): return lax.ppermute(rows, 'dcp', [(d, d ^ step) for d in range(devices)])  11.7 us
    ppermute x8, waiting for transfers between devices, swapped(): return lax.ppermute(rows, 'dcp', [(d, d ^ step) for d in range(devices)])  9.41 us
    ppermute x5, starting transfers between devices, per_device(): summed = summed + lax.ppermute(parts[offset - 1], 'dcp', pairs).astype(F32)  8.98 us
    ppermute x5, waiting for transfers between devices, per_device(): summed = summed + lax.ppermute(parts[offset - 1], 'dcp', pairs).astype(F32)  5.51 us
    pallas_call x1, Pallas kernels, per_device(): pl.pallas_call(functools.partial(pack_kernel, per_peer, paired), out_shap...  1.58 us
    pallas_call x1, Pallas kernels, per_device(): pl.pallas_call(output_kernel, out_shape=[wide, wide], in_specs=[vmem] * 5...  1.39 us
    pallas_call x1, Pallas kernels, per_device(): pl.pallas_call(functools.partial(attend_kernel, width, head, pieces), out...  1.32 us
    pallas_call x1, Pallas kernels, per_device(): pl.pallas_call(functools.partial(slots_kernel, per_peer, paired), out_sha...  1.2 us
  transfers between devices with their start and end apart: 13, of which 7 were waited for; matrix products, arithmetic and copies ran while one was open for 0% of the time, Pallas kernels for 7%

profile of v12, /device:TPU:14, one launch (start us, length us, event | category | flops | bytes accessed | tf_op | source)
XLA Modules:
  0.0 43.0 jit_solution(14883950498163299791)
XLA Ops:
  0.6 1.6 %pack.1 = (bf16[128,256]{1,0:T(8,128)(2,1)S(1)}, bf16[16,2048]{1,0:T(8,128)(2,1)S(1)}, bf16[16,2048]{1,0:T(8,128)(2,1)S(1)}, bf16[16,2048]{1,0:T(8,128)(2,1)S(1)...) custom-call(s32[8,128]{1,0:T(8,128)} %bitcast.1, ...), custom_call_target="tpu_custom_call" | custom-call | tf_op jit(solution)/shard_map/pack/pallas_call | solution.py:263
  2.2 2.7 %collective-permute-start.4 = (bf16[16,2048]{1,0:T(8,128)(2,1)S(1)}, bf16[16,2048]{1,0:T(8,128)(2,1)S(1)}, u32[]{:S(2)}, u32[]{:S(2)}) collective-permute-start(bf16[16,2048]{1,0:T(8,128)(2,1)S(1)} %get-tuple-element.52), channel_id=1, source_target_pairs={{0,16},{4,20},{8,24},{12,28},{16,0},{20,4},{24,8},{28,12},{1,17},{... | collective-permute-start | bytes 196616 | tf_op jit(solution)/shard_map/ppermute | solution.py:261
  4.9 0.3 collective-permute-start
  5.2 1.2 %slots.1 = (bf16[768,128]{1,0:T(8,128)(2,1)S(1)}, f32[768,128]{1,0:T(8,128)S(1)}, f32[8,128]{1,0:T(8,128)S(1)}) custom-call(s32[8,128]{1,0:T(8,128)} %bitcast.2, s32[3]{0:T(128)} %len_hbm.1, bf16[16,2048]{1,0:T(8,128)(2,1)S(1)} %get-tuple-element.36._.refs_2_), custom_call_target="tpu_custom_call" | custom-call | tf_op jit(solution)/shard_map/slots/pallas_call | solution.py:281
  6.4 2.6 %collective-permute-start.5 = (bf16[16,2048]{1,0:T(8,128)(2,1)S(1)}, bf16[16,2048]{1,0:T(8,128)(2,1)S(1)}, u32[]{:S(2)}, u32[]{:S(2)}) collective-permute-start(bf16[16,2048]{1,0:T(8,128)(2,1)S(1)} %get-tuple-element.53), channel_id=1, source_target_pairs={{0,20},{4,16},{8,28},{12,24},{16,4},{20,0},{24,12},{28,8},{1,21},{... | collective-permute-start | bytes 196616 | tf_op jit(solution)/shard_map/ppermute | solution.py:261
  9.0 3.0 %collective-permute-start.7 = (bf16[16,2048]{1,0:T(8,128)(2,1)S(1)}, bf16[16,2048]{1,0:T(8,128)(2,1)S(1)}, u32[]{:S(2)}, u32[]{:S(2)}) collective-permute-start(bf16[16,2048]{1,0:T(8,128)(2,1)S(1)} %get-tuple-element.55), channel_id=1, source_target_pairs={{0,28},{4,24},{8,20},{12,16},{16,12},{20,8},{24,4},{28,0},{1,29},{... | collective-permute-start | bytes 196616 | tf_op jit(solution)/shard_map/ppermute | solution.py:261
  12.0 1.9 %collective-permute-done.refs_1_ = bf16[128,256]{1,0:T(8,128)(2,1)S(1)} collective-permute-done((bf16[128,256]{1,0:T(8,128)(2,1)S(1)}, bf16[128,256]{1,0:T(8,128)(2,1)S(1)}, u32[]{:S(2)}, u32[]{:S(2)}) %collective-permute-start) | collective-permute-done | bytes 65568 | tf_op jit(solution)/shard_map/ppermute | solution.py:261
  14.3 0.8 %collective-permute-start.2 = (bf16[16,5120]{1,0:T(8,128)(2,1)S(1)}, bf16[16,5120]{1,0:T(8,128)(2,1)S(1)}, u32[]{:S(2)}, u32[]{:S(2)}) collective-permute-start(bf16[16,5120]{1,0:T(8,128)(2,1)S(1)} %get-tuple-element.50), channel_id=1, source_target_pairs={{0,8},{4,12},{8,0},{12,4},{16,24},{20,28},{24,16},{28,20},{1,9},{5... | collective-permute-start | bytes 491528 | tf_op jit(solution)/shard_map/ppermute | solution.py:261
  15.1 0.9 %collective-permute-done.5.refs_1_ = bf16[16,2048]{1,0:T(8,128)(2,1)S(1)} collective-permute-done((bf16[16,2048]{1,0:T(8,128)(2,1)S(1)}, bf16[16,2048]{1,0:T(8,128)(2,1)S(1)}, u32[]{:S(2)}, u32[]{:S(2)}) %collective-permute-start.5) | collective-permute-done | bytes 65568 | tf_op jit(solution)/shard_map/ppermute | solution.py:261
  16.0 2.2 %collective-permute-start.3 = (bf16[16,5120]{1,0:T(8,128)(2,1)S(1)}, bf16[16,5120]{1,0:T(8,128)(2,1)S(1)}, u32[]{:S(2)}, u32[]{:S(2)}) collective-permute-start(bf16[16,5120]{1,0:T(8,128)(2,1)S(1)} %get-tuple-element.51), channel_id=1, source_target_pairs={{0,12},{4,8},{8,4},{12,0},{16,28},{20,24},{24,20},{28,16},{1,13},{... | collective-permute-start | bytes 491528 | tf_op jit(solution)/shard_map/ppermute | solution.py:261
  18.2 0.8 %collective-permute-done.7.refs_3_ = bf16[16,2048]{1,0:T(8,128)(2,1)S(1)} collective-permute-done((bf16[16,2048]{1,0:T(8,128)(2,1)S(1)}, bf16[16,2048]{1,0:T(8,128)(2,1)S(1)}, u32[]{:S(2)}, u32[]{:S(2)}) %collective-permute-start.7) | collective-permute-done | bytes 65568 | tf_op jit(solution)/shard_map/ppermute | solution.py:261
  19.0 0.3 far.1.refs_4_
  19.3 5.8 %collective-permute-done.1.refs_1_ = bf16[16,5120]{1,0:T(8,128)(2,1)S(1)} collective-permute-done((bf16[16,5120]{1,0:T(8,128)(2,1)S(1)}, bf16[16,5120]{1,0:T(8,128)(2,1)S(1)}, u32[]{:S(2)}, u32[]{:S(2)}) %collective-permute-start.1) | collective-permute-done | bytes 163872 | tf_op jit(solution)/shard_map/ppermute | solution.py:261
  25.1 1.3 %attend.1 = (bf16[768,128]{1,0:T(8,128)(2,1)S(1)}, bf16[768,128]{1,0:T(8,128)(2,1)S(1)}, bf16[768,1024]{1,0:T(8,128)(2,1)S(1)}, bf16[768,1024]{1,0:T(8,128)(2,1)...) custom-call(f32[8,128]{1,0:T(8,128)S(1)} %get-tuple-element.37.live_, ...), custom_call_target="tpu_custom_call" | custom-call | tf_op jit(solution)/shard_map/attend/pallas_call | solution.py:332
  26.4 0.7 %collective-permute-start.8 = (bf16[128,256]{1,0:T(8,128)(2,1)S(1)}, bf16[128,256]{1,0:T(8,128)(2,1)S(1)}, u32[]{:S(2)}, u32[]{:S(2)}) collective-permute-start(bf16[128,256]{1,0:T(8,128)(2,1)S(1)} %get-tuple-element.63), channel_id=1, source_target_pairs={{20,0},{24,4},{28,8},{21,1},{25,5},{29,9},{22,2},{26,6},{30,10},{2... | collective-permute-start | bytes 196616 | tf_op jit(solution)/shard_map/ppermute | solution.py:350
  27.1 1.3 %collective-permute-start.9 = (bf16[128,256]{1,0:T(8,128)(2,1)S(1)}, bf16[128,256]{1,0:T(8,128)(2,1)S(1)}, u32[]{:S(2)}, u32[]{:S(2)}) collective-permute-start(bf16[128,256]{1,0:T(8,128)(2,1)S(1)} %get-tuple-element.64), channel_id=1, source_target_pairs={{16,0},{20,4},{24,8},{28,12},{17,1},{21,5},{25,9},{29,13},{18,2},{... | collective-permute-start | bytes 196616 | tf_op jit(solution)/shard_map/ppermute | solution.py:350
  28.4 3.2 %collective-permute-start.10 = (bf16[128,256]{1,0:T(8,128)(2,1)S(1)}, bf16[128,256]{1,0:T(8,128)(2,1)S(1)}, u32[]{:S(2)}, u32[]{:S(2)}) collective-permute-start(bf16[128,256]{1,0:T(8,128)(2,1)S(1)} %get-tuple-element.65), channel_id=1, source_target_pairs={{12,0},{16,4},{20,8},{24,12},{28,16},{13,1},{17,5},{21,9},{25,13},... | collective-permute-start | bytes 196616 | tf_op jit(solution)/shard_map/ppermute | solution.py:350
  31.6 1.9 %collective-permute-start.11 = (bf16[128,256]{1,0:T(8,128)(2,1)S(1)}, bf16[128,256]{1,0:T(8,128)(2,1)S(1)}, u32[]{:S(2)}, u32[]{:S(2)}) collective-permute-start(bf16[128,256]{1,0:T(8,128)(2,1)S(1)} %get-tuple-element.66), channel_id=1, source_target_pairs={{8,0},{12,4},{16,8},{20,12},{24,16},{28,20},{9,1},{13,5},{17,9},{2... | collective-permute-start | bytes 196616 | tf_op jit(solution)/shard_map/ppermute | solution.py:350
  33.5 1.9 %collective-permute-start.12 = (bf16[128,256]{1,0:T(8,128)(2,1)S(1)}, bf16[128,256]{1,0:T(8,128)(2,1)S(1)}, u32[]{:S(2)}, u32[]{:S(2)}) collective-permute-start(bf16[128,256]{1,0:T(8,128)(2,1)S(1)} %get-tuple-element.67), channel_id=1, source_target_pairs={{4,0},{8,4},{12,8},{16,12},{20,16},{24,20},{28,24},{5,1},{9,5},{13... | collective-permute-start | bytes 196616 | tf_op jit(solution)/shard_map/ppermute | solution.py:350
  35.4 1.4 %outputs.1 = (bf16[128,1024]{1,0:T(8,128)(2,1)}, bf16[128,1024]{1,0:T(8,128)(2,1)}) custom-call(f32[8,128]{1,0:T(8,128)S(1)} %get-tuple-element.37.live_ref, bf16[768,128]{1,0:T(8,128)(2,1)S(1)} %get-tuple-element.56.key_ref, bf16[768,128]{1,0:T(8,128)(2,1)S(1)} %get-tuple-element.57.value_ref, bf16[768,1024]{1,0:T(8,128)(2,1)S(1)} %get-tuple-element.58.prob_ref, ...), custom_call_target="tpu_custom_call" | custom-call | tf_op jit(solution)/shard_map/outputs/pallas_call | solution.py:340
  36.8 0.9 %collective-permute-done.10 = bf16[128,256]{1,0:T(8,128)(2,1)S(1)} collective-permute-done((bf16[128,256]{1,0:T(8,128)(2,1)S(1)}, bf16[128,256]{1,0:T(8,128)(2,1)S(1)}, u32[]{:S(2)}, u32[]{:S(2)}) %collective-permute-start.10) | collective-permute-done | bytes 65568 | tf_op jit(solution)/shard_map/ppermute | solution.py:350
  37.7 1.7 %collective-permute-done.11 = bf16[128,256]{1,0:T(8,128)(2,1)S(1)} collective-permute-done((bf16[128,256]{1,0:T(8,128)(2,1)S(1)}, bf16[128,256]{1,0:T(8,128)(2,1)S(1)}, u32[]{:S(2)}, u32[]{:S(2)}) %collective-permute-start.11) | collective-permute-done | bytes 65568 | tf_op jit(solution)/shard_map/ppermute | solution.py:350
  39.4 2.9 %collective-permute-done.12 = bf16[128,256]{1,0:T(8,128)(2,1)S(1)} collective-permute-done((bf16[128,256]{1,0:T(8,128)(2,1)S(1)}, bf16[128,256]{1,0:T(8,128)(2,1)S(1)}, u32[]{:S(2)}, u32[]{:S(2)}) %collective-permute-start.12) | collective-permute-done | bytes 65568 | tf_op jit(solution)/shard_map/ppermute | solution.py:350
  42.4 0.6 %fusion = (bf16[128,128]{1,0:T(8,128)(2,1)}, bf16[128,128]{1,0:T(8,128)(2,1)}) fusion(bf16[128,256]{1,0:T(8,128)(2,1)S(1)} %add_convert_fusion), kind=kLoop, calls=%fused_computation.1 | loop fusion | bytes 131072 | tf_op jit(solution)/shard_map/slice | solution.py:351
  (10 shorter events, 0.4 us)
Async XLA Ops:
  2.2 12.1 %collective-permute-start.4 = (bf16[16,2048]{1,0:T(8,128)(2,1)S(1)}, bf16[16,2048]{1,0:T(8,128)(2,1)S(1)}, u32[]{:S(2)}, u32[]{:S(2)}) collective-permute-start(bf16[16,2048]{1,0:T(8,128)(2,1)S(1)} %get-tuple-element.52), channel_id=1, source_target_pairs={{0,16},{4,20},{8,24},{12,28},{16,0},{20,4},{24,8},{28,12},{1,17},{... | collective-permute-start | bytes 196616 | tf_op jit(solution)/shard_map/ppermute | solution.py:261
  4.9 9.1 %collective-permute-start = (bf16[128,256]{1,0:T(8,128)(2,1)S(1)}, bf16[128,256]{1,0:T(8,128)(2,1)S(1)}, u32[]{:S(2)}, u32[]{:S(2)}) collective-permute-start(bf16[128,256]{1,0:T(8,128)(2,1)S(1)} %get-tuple-element.44.refs_0_), channel_id=1, source_target_pairs={{0,16},{4,20},{8,24},{12,28},{16,0},{20,4},{24,8},{28,12},{1,17},{... | collective-permute-start | bytes 196616 | tf_op jit(solution)/shard_map/ppermute | solution.py:261
  6.4 9.6 %collective-permute-start.5 = (bf16[16,2048]{1,0:T(8,128)(2,1)S(1)}, bf16[16,2048]{1,0:T(8,128)(2,1)S(1)}, u32[]{:S(2)}, u32[]{:S(2)}) collective-permute-start(bf16[16,2048]{1,0:T(8,128)(2,1)S(1)} %get-tuple-element.53), channel_id=1, source_target_pairs={{0,20},{4,16},{8,28},{12,24},{16,4},{20,0},{24,12},{28,8},{1,21},{... | collective-permute-start | bytes 196616 | tf_op jit(solution)/shard_map/ppermute | solution.py:261
  9.0 9.2 %collective-permute-start.6 = (bf16[16,2048]{1,0:T(8,128)(2,1)S(1)}, bf16[16,2048]{1,0:T(8,128)(2,1)S(1)}, u32[]{:S(2)}, u32[]{:S(2)}) collective-permute-start(bf16[16,2048]{1,0:T(8,128)(2,1)S(1)} %get-tuple-element.54), channel_id=1, source_target_pairs={{0,24},{4,28},{8,16},{12,20},{16,8},{20,12},{24,0},{28,4},{1,25},{... | collective-permute-start | bytes 196616 | tf_op jit(solution)/shard_map/ppermute | solution.py:261
  9.0 10.0 %collective-permute-start.7 = (bf16[16,2048]{1,0:T(8,128)(2,1)S(1)}, bf16[16,2048]{1,0:T(8,128)(2,1)S(1)}, u32[]{:S(2)}, u32[]{:S(2)}) collective-permute-start(bf16[16,2048]{1,0:T(8,128)(2,1)S(1)} %get-tuple-element.55), channel_id=1, source_target_pairs={{0,28},{4,24},{8,20},{12,16},{16,12},{20,8},{24,4},{28,0},{1,29},{... | collective-permute-start | bytes 196616 | tf_op jit(solution)/shard_map/ppermute | solution.py:261
  14.2 10.9 %collective-permute-start.1 = (bf16[16,5120]{1,0:T(8,128)(2,1)S(1)}, bf16[16,5120]{1,0:T(8,128)(2,1)S(1)}, u32[]{:S(2)}, u32[]{:S(2)}) collective-permute-start(bf16[16,5120]{1,0:T(8,128)(2,1)S(1)} %get-tuple-element.49), channel_id=1, source_target_pairs={{0,4},{4,0},{8,12},{12,8},{16,20},{20,16},{24,28},{28,24},{1,5},{5... | collective-permute-start | bytes 491528 | tf_op jit(solution)/shard_map/ppermute | solution.py:261
  14.3 10.8 %collective-permute-start.2 = (bf16[16,5120]{1,0:T(8,128)(2,1)S(1)}, bf16[16,5120]{1,0:T(8,128)(2,1)S(1)}, u32[]{:S(2)}, u32[]{:S(2)}) collective-permute-start(bf16[16,5120]{1,0:T(8,128)(2,1)S(1)} %get-tuple-element.50), channel_id=1, source_target_pairs={{0,8},{4,12},{8,0},{12,4},{16,24},{20,28},{24,16},{28,20},{1,9},{5... | collective-permute-start | bytes 491528 | tf_op jit(solution)/shard_map/ppermute | solution.py:261
  16.0 9.1 %collective-permute-start.3 = (bf16[16,5120]{1,0:T(8,128)(2,1)S(1)}, bf16[16,5120]{1,0:T(8,128)(2,1)S(1)}, u32[]{:S(2)}, u32[]{:S(2)}) collective-permute-start(bf16[16,5120]{1,0:T(8,128)(2,1)S(1)} %get-tuple-element.51), channel_id=1, source_target_pairs={{0,12},{4,8},{8,4},{12,0},{16,28},{20,24},{24,20},{28,16},{1,13},{... | collective-permute-start | bytes 491528 | tf_op jit(solution)/shard_map/ppermute | solution.py:261
  26.4 10.4 %collective-permute-start.8 = (bf16[128,256]{1,0:T(8,128)(2,1)S(1)}, bf16[128,256]{1,0:T(8,128)(2,1)S(1)}, u32[]{:S(2)}, u32[]{:S(2)}) collective-permute-start(bf16[128,256]{1,0:T(8,128)(2,1)S(1)} %get-tuple-element.63), channel_id=1, source_target_pairs={{20,0},{24,4},{28,8},{21,1},{25,5},{29,9},{22,2},{26,6},{30,10},{2... | collective-permute-start | bytes 196616 | tf_op jit(solution)/shard_map/ppermute | solution.py:350
  27.1 9.7 %collective-permute-start.9 = (bf16[128,256]{1,0:T(8,128)(2,1)S(1)}, bf16[128,256]{1,0:T(8,128)(2,1)S(1)}, u32[]{:S(2)}, u32[]{:S(2)}) collective-permute-start(bf16[128,256]{1,0:T(8,128)(2,1)S(1)} %get-tuple-element.64), channel_id=1, source_target_pairs={{16,0},{20,4},{24,8},{28,12},{17,1},{21,5},{25,9},{29,13},{18,2},{... | collective-permute-start | bytes 196616 | tf_op jit(solution)/shard_map/ppermute | solution.py:350
  28.4 9.3 %collective-permute-start.10 = (bf16[128,256]{1,0:T(8,128)(2,1)S(1)}, bf16[128,256]{1,0:T(8,128)(2,1)S(1)}, u32[]{:S(2)}, u32[]{:S(2)}) collective-permute-start(bf16[128,256]{1,0:T(8,128)(2,1)S(1)} %get-tuple-element.65), channel_id=1, source_target_pairs={{12,0},{16,4},{20,8},{24,12},{28,16},{13,1},{17,5},{21,9},{25,13},... | collective-permute-start | bytes 196616 | tf_op jit(solution)/shard_map/ppermute | solution.py:350
  31.6 7.9 %collective-permute-start.11 = (bf16[128,256]{1,0:T(8,128)(2,1)S(1)}, bf16[128,256]{1,0:T(8,128)(2,1)S(1)}, u32[]{:S(2)}, u32[]{:S(2)}) collective-permute-start(bf16[128,256]{1,0:T(8,128)(2,1)S(1)} %get-tuple-element.66), channel_id=1, source_target_pairs={{8,0},{12,4},{16,8},{20,12},{24,16},{28,20},{9,1},{13,5},{17,9},{2... | collective-permute-start | bytes 196616 | tf_op jit(solution)/shard_map/ppermute | solution.py:350
  33.5 8.8 %collective-permute-start.12 = (bf16[128,256]{1,0:T(8,128)(2,1)S(1)}, bf16[128,256]{1,0:T(8,128)(2,1)S(1)}, u32[]{:S(2)}, u32[]{:S(2)}) collective-permute-start(bf16[128,256]{1,0:T(8,128)(2,1)S(1)} %get-tuple-element.67), channel_id=1, source_target_pairs={{4,0},{8,4},{12,8},{16,12},{20,16},{24,20},{28,24},{5,1},{9,5},{13... | collective-permute-start | bytes 196616 | tf_op jit(solution)/shard_map/ppermute | solution.py:350

commit v13 on v11

--- a/solution.py
+++ b/solution.py
@@ -344,7 +344,7 @@
         compiler_params=params,
         name="outputs",
     )(live, keys, values, probs, grad_scores)
-    for offset in range(SPAN, 0, -1):
+    for offset in (4, 5, 3, 2, 1):
         pairs = [(source, source - offset) for source in range(offset, devices)]
         summed = summed + lax.ppermute(parts[offset - 1], "dcp", pairs).astype(F32)
     return attn_out, dquery, summed[:, :head].astype(BF16), summed[:, head:].astype(BF16)

time: 43.2 us -> 42.7 us (0.988)
  no operation moved by 1% of the time
where the time goes in v13:
time: 42.7 us; the launch traced here: 42.3 us
  starting transfers between devices  21.4 us (50%)
  waiting for transfers between devices  12.3 us (29%)
  Pallas kernels  7.08 us (17%)
  between operations  0.73 us (2%)
  local copies, waits for them, and re-layouts  0.63 us (1%)
    ppermute x8, starting transfers between devices, swapped(): return lax.ppermute(rows, 'dcp', [(d, d ^ step) for d in range(devices)])  12.6 us
    ppermute x5, starting transfers between devices, per_device(): summed = summed + lax.ppermute(parts[offset - 1], 'dcp', pairs).astype(F32)  8.84 us
    ppermute x8, waiting for transfers between devices, swapped(): return lax.ppermute(rows, 'dcp', [(d, d ^ step) for d in range(devices)])  7.79 us
    ppermute x5, waiting for transfers between devices, per_device(): summed = summed + lax.ppermute(parts[offset - 1], 'dcp', pairs).astype(F32)  4.54 us
    pallas_call x1, Pallas kernels, per_device(): pl.pallas_call(functools.partial(attend_kernel, width, head, pieces), out...  2.25 us
    pallas_call x1, Pallas kernels, per_device(): pl.pallas_call(functools.partial(pack_kernel, per_peer, paired), out_shap...  1.58 us
    pallas_call x1, Pallas kernels, per_device(): pl.pallas_call(output_kernel, out_shape=[wide, wide], in_specs=[vmem] * 5...  1.5 us
    pallas_call x1, Pallas kernels, per_device(): pl.pallas_call(functools.partial(slots_kernel, per_peer, paired), out_sha...  1.21 us
  transfers between devices with their start and end apart: 13, of which 10 were waited for; matrix products, arithmetic and copies ran while one was open for 0% of the time, Pallas kernels for 8%

profile of v13, /device:TPU:14, one launch (start us, length us, event | category | flops | bytes accessed | tf_op | source)
XLA Modules:
  0.0 42.3 jit_solution(7600726166229812793)
XLA Ops:
  0.6 1.6 %pack.1 = (bf16[128,256]{1,0:T(8,128)(2,1)S(1)}, bf16[16,2048]{1,0:T(8,128)(2,1)S(1)}, bf16[16,2048]{1,0:T(8,128)(2,1)S(1)}, bf16[16,2048]{1,0:T(8,128)(2,1)S(1)...) custom-call(s32[8,128]{1,0:T(8,128)} %bitcast.1, ...), custom_call_target="tpu_custom_call" | custom-call | tf_op jit(solution)/shard_map/pack/pallas_call | solution.py:263
  2.2 2.7 %collective-permute-start = (bf16[128,256]{1,0:T(8,128)(2,1)S(1)}, bf16[128,256]{1,0:T(8,128)(2,1)S(1)}, u32[]{:S(2)}, u32[]{:S(2)}) collective-permute-start(bf16[128,256]{1,0:T(8,128)(2,1)S(1)} %get-tuple-element.32.refs_0_), channel_id=1, source_target_pairs={{0,16},{4,20},{8,24},{12,28},{16,0},{20,4},{24,8},{28,12},{1,17},{... | collective-permute-start | bytes 196616 | tf_op jit(solution)/shard_map/ppermute | solution.py:261
  4.9 0.3 collective-permute-start.4
  5.2 2.5 %collective-permute-start.5 = (bf16[16,2048]{1,0:T(8,128)(2,1)S(1)}, bf16[16,2048]{1,0:T(8,128)(2,1)S(1)}, u32[]{:S(2)}, u32[]{:S(2)}) collective-permute-start(bf16[16,2048]{1,0:T(8,128)(2,1)S(1)} %get-tuple-element.45), channel_id=1, source_target_pairs={{0,20},{4,16},{8,28},{12,24},{16,4},{20,0},{24,12},{28,8},{1,21},{... | collective-permute-start | bytes 196616 | tf_op jit(solution)/shard_map/ppermute | solution.py:261
  7.7 3.0 %collective-permute-start.7 = (bf16[16,2048]{1,0:T(8,128)(2,1)S(1)}, bf16[16,2048]{1,0:T(8,128)(2,1)S(1)}, u32[]{:S(2)}, u32[]{:S(2)}) collective-permute-start(bf16[16,2048]{1,0:T(8,128)(2,1)S(1)} %get-tuple-element.47), channel_id=1, source_target_pairs={{0,28},{4,24},{8,20},{12,16},{16,12},{20,8},{24,4},{28,0},{1,29},{... | collective-permute-start | bytes 196616 | tf_op jit(solution)/shard_map/ppermute | solution.py:261
  10.7 1.7 %collective-permute-done.refs_1_ = bf16[128,256]{1,0:T(8,128)(2,1)S(1)} collective-permute-done((bf16[128,256]{1,0:T(8,128)(2,1)S(1)}, bf16[128,256]{1,0:T(8,128)(2,1)S(1)}, u32[]{:S(2)}, u32[]{:S(2)}) %collective-permute-start) | collective-permute-done | bytes 65568 | tf_op jit(solution)/shard_map/ppermute | solution.py:261
  12.8 1.2 %slots.1 = (bf16[768,128]{1,0:T(8,128)(2,1)S(1)}, f32[768,128]{1,0:T(8,128)S(1)}, f32[8,128]{1,0:T(8,128)S(1)}) custom-call(s32[8,128]{1,0:T(8,128)} %bitcast.2, s32[3]{0:T(128)} %len_hbm.1, bf16[16,5120]{1,0:T(8,128)(2,1)S(1)} %get-tuple-element.37._.refs_0_), custom_call_target="tpu_custom_call" | custom-call | tf_op jit(solution)/shard_map/slots/pallas_call | solution.py:297
  14.0 0.5 %collective-permute-done.4.refs_0_ = bf16[16,2048]{1,0:T(8,128)(2,1)S(1)} collective-permute-done((bf16[16,2048]{1,0:T(8,128)(2,1)S(1)}, bf16[16,2048]{1,0:T(8,128)(2,1)S(1)}, u32[]{:S(2)}, u32[]{:S(2)}) %collective-permute-start.4) | collective-permute-done | bytes 65568 | tf_op jit(solution)/shard_map/ppermute | solution.py:261
  14.6 1.2 %collective-permute-start.2 = (bf16[16,5120]{1,0:T(8,128)(2,1)S(1)}, bf16[16,5120]{1,0:T(8,128)(2,1)S(1)}, u32[]{:S(2)}, u32[]{:S(2)}) collective-permute-start(bf16[16,5120]{1,0:T(8,128)(2,1)S(1)} %get-tuple-element.42), channel_id=1, source_target_pairs={{0,8},{4,12},{8,0},{12,4},{16,24},{20,28},{24,16},{28,20},{1,9},{5... | collective-permute-start | bytes 491528 | tf_op jit(solution)/shard_map/ppermute | solution.py:261
  16.0 2.8 %collective-permute-start.3 = (bf16[16,5120]{1,0:T(8,128)(2,1)S(1)}, bf16[16,5120]{1,0:T(8,128)(2,1)S(1)}, u32[]{:S(2)}, u32[]{:S(2)}) collective-permute-start(bf16[16,5120]{1,0:T(8,128)(2,1)S(1)} %get-tuple-element.43), channel_id=1, source_target_pairs={{0,12},{4,8},{8,4},{12,0},{16,28},{20,24},{24,20},{28,16},{1,13},{... | collective-permute-start | bytes 491528 | tf_op jit(solution)/shard_map/ppermute | solution.py:261
  19.3 0.3 collective-permute-done.1.refs_1_
  19.6 1.8 %collective-permute-done.2.refs_2_ = bf16[16,5120]{1,0:T(8,128)(2,1)S(1)} collective-permute-done((bf16[16,5120]{1,0:T(8,128)(2,1)S(1)}, bf16[16,5120]{1,0:T(8,128)(2,1)S(1)}, u32[]{:S(2)}, u32[]{:S(2)}) %collective-permute-start.2) | collective-permute-done | bytes 163872 | tf_op jit(solution)/shard_map/ppermute | solution.py:261
  21.4 3.0 %collective-permute-done.3.refs_3_ = bf16[16,5120]{1,0:T(8,128)(2,1)S(1)} collective-permute-done((bf16[16,5120]{1,0:T(8,128)(2,1)S(1)}, bf16[16,5120]{1,0:T(8,128)(2,1)S(1)}, u32[]{:S(2)}, u32[]{:S(2)}) %collective-permute-start.3) | collective-permute-done | bytes 163872 | tf_op jit(solution)/shard_map/ppermute | solution.py:261
  24.4 2.3 %attend.1 = (bf16[768,128]{1,0:T(8,128)(2,1)S(1)}, bf16[768,128]{1,0:T(8,128)(2,1)S(1)}, bf16[768,1024]{1,0:T(8,128)(2,1)S(1)}, bf16[768,1024]{1,0:T(8,128)(2,1)...) custom-call(f32[8,128]{1,0:T(8,128)S(1)} %get-tuple-element.38.live_, ...), custom_call_target="tpu_custom_call" | custom-call | tf_op jit(solution)/shard_map/attend/pallas_call | solution.py:331
  26.6 1.3 %collective-permute-start.8 = (bf16[128,256]{1,0:T(8,128)(2,1)S(1)}, bf16[128,256]{1,0:T(8,128)(2,1)S(1)}, u32[]{:S(2)}, u32[]{:S(2)}) collective-permute-start(bf16[128,256]{1,0:T(8,128)(2,1)S(1)} %get-tuple-element.55), channel_id=1, source_target_pairs={{16,0},{20,4},{24,8},{28,12},{17,1},{21,5},{25,9},{29,13},{18,2},{... | collective-permute-start | bytes 196616 | tf_op jit(solution)/shard_map/ppermute | solution.py:349
  27.9 0.7 %collective-permute-start.9 = (bf16[128,256]{1,0:T(8,128)(2,1)S(1)}, bf16[128,256]{1,0:T(8,128)(2,1)S(1)}, u32[]{:S(2)}, u32[]{:S(2)}) collective-permute-start(bf16[128,256]{1,0:T(8,128)(2,1)S(1)} %get-tuple-element.56), channel_id=1, source_target_pairs={{20,0},{24,4},{28,8},{21,1},{25,5},{29,9},{22,2},{26,6},{30,10},{2... | collective-permute-start | bytes 196616 | tf_op jit(solution)/shard_map/ppermute | solution.py:349
  28.6 3.0 %collective-permute-start.10 = (bf16[128,256]{1,0:T(8,128)(2,1)S(1)}, bf16[128,256]{1,0:T(8,128)(2,1)S(1)}, u32[]{:S(2)}, u32[]{:S(2)}) collective-permute-start(bf16[128,256]{1,0:T(8,128)(2,1)S(1)} %get-tuple-element.57), channel_id=1, source_target_pairs={{12,0},{16,4},{20,8},{24,12},{28,16},{13,1},{17,5},{21,9},{25,13},... | collective-permute-start | bytes 196616 | tf_op jit(solution)/shard_map/ppermute | solution.py:349
  31.7 1.9 %collective-permute-start.11 = (bf16[128,256]{1,0:T(8,128)(2,1)S(1)}, bf16[128,256]{1,0:T(8,128)(2,1)S(1)}, u32[]{:S(2)}, u32[]{:S(2)}) collective-permute-start(bf16[128,256]{1,0:T(8,128)(2,1)S(1)} %get-tuple-element.58), channel_id=1, source_target_pairs={{8,0},{12,4},{16,8},{20,12},{24,16},{28,20},{9,1},{13,5},{17,9},{2... | collective-permute-start | bytes 196616 | tf_op jit(solution)/shard_map/ppermute | solution.py:349
  33.6 1.9 %collective-permute-start.12 = (bf16[128,256]{1,0:T(8,128)(2,1)S(1)}, bf16[128,256]{1,0:T(8,128)(2,1)S(1)}, u32[]{:S(2)}, u32[]{:S(2)}) collective-permute-start(bf16[128,256]{1,0:T(8,128)(2,1)S(1)} %get-tuple-element.59), channel_id=1, source_target_pairs={{4,0},{8,4},{12,8},{16,12},{20,16},{24,20},{28,24},{5,1},{9,5},{13... | collective-permute-start | bytes 196616 | tf_op jit(solution)/shard_map/ppermute | solution.py:349
  35.5 1.5 %outputs.1 = (bf16[128,1024]{1,0:T(8,128)(2,1)}, bf16[128,1024]{1,0:T(8,128)(2,1)}) custom-call(f32[8,128]{1,0:T(8,128)S(1)} %get-tuple-element.38.live_ref, bf16[768,128]{1,0:T(8,128)(2,1)S(1)} %get-tuple-element.48.key_ref, bf16[768,128]{1,0:T(8,128)(2,1)S(1)} %get-tuple-element.49.value_ref, bf16[768,1024]{1,0:T(8,128)(2,1)S(1)} %get-tuple-element.50.prob_ref, ...), custom_call_target="tpu_custom_call" | custom-call | tf_op jit(solution)/shard_map/outputs/pallas_call | solution.py:339
  37.0 1.4 %collective-permute-done.10 = bf16[128,256]{1,0:T(8,128)(2,1)S(1)} collective-permute-done((bf16[128,256]{1,0:T(8,128)(2,1)S(1)}, bf16[128,256]{1,0:T(8,128)(2,1)S(1)}, u32[]{:S(2)}, u32[]{:S(2)}) %collective-permute-start.10) | collective-permute-done | bytes 65568 | tf_op jit(solution)/shard_map/ppermute | solution.py:349
  38.4 1.1 %collective-permute-done.11 = bf16[128,256]{1,0:T(8,128)(2,1)S(1)} collective-permute-done((bf16[128,256]{1,0:T(8,128)(2,1)S(1)}, bf16[128,256]{1,0:T(8,128)(2,1)S(1)}, u32[]{:S(2)}, u32[]{:S(2)}) %collective-permute-start.11) | collective-permute-done | bytes 65568 | tf_op jit(solution)/shard_map/ppermute | solution.py:349
  39.6 2.0 %collective-permute-done.12 = bf16[128,256]{1,0:T(8,128)(2,1)S(1)} collective-permute-done((bf16[128,256]{1,0:T(8,128)(2,1)S(1)}, bf16[128,256]{1,0:T(8,128)(2,1)S(1)}, u32[]{:S(2)}, u32[]{:S(2)}) %collective-permute-start.12) | collective-permute-done | bytes 65568 | tf_op jit(solution)/shard_map/ppermute | solution.py:349
  41.6 0.6 %fusion = (bf16[128,128]{1,0:T(8,128)(2,1)}, bf16[128,128]{1,0:T(8,128)(2,1)}) fusion(bf16[128,256]{1,0:T(8,128)(2,1)S(1)} %add_convert_fusion), kind=kLoop, calls=%fused_computation.1 | loop fusion | bytes 131072 | tf_op jit(solution)/shard_map/slice | solution.py:350
  (10 shorter events, 1.1 us)
Async XLA Ops:
  2.2 10.2 %collective-permute-start = (bf16[128,256]{1,0:T(8,128)(2,1)S(1)}, bf16[128,256]{1,0:T(8,128)(2,1)S(1)}, u32[]{:S(2)}, u32[]{:S(2)}) collective-permute-start(bf16[128,256]{1,0:T(8,128)(2,1)S(1)} %get-tuple-element.32.refs_0_), channel_id=1, source_target_pairs={{0,16},{4,20},{8,24},{12,28},{16,0},{20,4},{24,8},{28,12},{1,17},{... | collective-permute-start | bytes 196616 | tf_op jit(solution)/shard_map/ppermute | solution.py:261
  4.9 9.7 %collective-permute-start.4 = (bf16[16,2048]{1,0:T(8,128)(2,1)S(1)}, bf16[16,2048]{1,0:T(8,128)(2,1)S(1)}, u32[]{:S(2)}, u32[]{:S(2)}) collective-permute-start(bf16[16,2048]{1,0:T(8,128)(2,1)S(1)} %get-tuple-element.44), channel_id=1, source_target_pairs={{0,16},{4,20},{8,24},{12,28},{16,0},{20,4},{24,8},{28,12},{1,17},{... | collective-permute-start | bytes 196616 | tf_op jit(solution)/shard_map/ppermute | solution.py:261
  5.2 10.8 %collective-permute-start.5 = (bf16[16,2048]{1,0:T(8,128)(2,1)S(1)}, bf16[16,2048]{1,0:T(8,128)(2,1)S(1)}, u32[]{:S(2)}, u32[]{:S(2)}) collective-permute-start(bf16[16,2048]{1,0:T(8,128)(2,1)S(1)} %get-tuple-element.45), channel_id=1, source_target_pairs={{0,20},{4,16},{8,28},{12,24},{16,4},{20,0},{24,12},{28,8},{1,21},{... | collective-permute-start | bytes 196616 | tf_op jit(solution)/shard_map/ppermute | solution.py:261
  7.7 11.1 %collective-permute-start.6 = (bf16[16,2048]{1,0:T(8,128)(2,1)S(1)}, bf16[16,2048]{1,0:T(8,128)(2,1)S(1)}, u32[]{:S(2)}, u32[]{:S(2)}) collective-permute-start(bf16[16,2048]{1,0:T(8,128)(2,1)S(1)} %get-tuple-element.46), channel_id=1, source_target_pairs={{0,24},{4,28},{8,16},{12,20},{16,8},{20,12},{24,0},{28,4},{1,25},{... | collective-permute-start | bytes 196616 | tf_op jit(solution)/shard_map/ppermute | solution.py:261
  7.7 11.3 %collective-permute-start.7 = (bf16[16,2048]{1,0:T(8,128)(2,1)S(1)}, bf16[16,2048]{1,0:T(8,128)(2,1)S(1)}, u32[]{:S(2)}, u32[]{:S(2)}) collective-permute-start(bf16[16,2048]{1,0:T(8,128)(2,1)S(1)} %get-tuple-element.47), channel_id=1, source_target_pairs={{0,28},{4,24},{8,20},{12,16},{16,12},{20,8},{24,4},{28,0},{1,29},{... | collective-permute-start | bytes 196616 | tf_op jit(solution)/shard_map/ppermute | solution.py:261
  12.7 6.9 %collective-permute-start.1 = (bf16[16,5120]{1,0:T(8,128)(2,1)S(1)}, bf16[16,5120]{1,0:T(8,128)(2,1)S(1)}, u32[]{:S(2)}, u32[]{:S(2)}) collective-permute-start(bf16[16,5120]{1,0:T(8,128)(2,1)S(1)} %get-tuple-element.41), channel_id=1, source_target_pairs={{0,4},{4,0},{8,12},{12,8},{16,20},{20,16},{24,28},{28,24},{1,5},{5... | collective-permute-start | bytes 491528 | tf_op jit(solution)/shard_map/ppermute | solution.py:261
  14.6 6.8 %collective-permute-start.2 = (bf16[16,5120]{1,0:T(8,128)(2,1)S(1)}, bf16[16,5120]{1,0:T(8,128)(2,1)S(1)}, u32[]{:S(2)}, u32[]{:S(2)}) collective-permute-start(bf16[16,5120]{1,0:T(8,128)(2,1)S(1)} %get-tuple-element.42), channel_id=1, source_target_pairs={{0,8},{4,12},{8,0},{12,4},{16,24},{20,28},{24,16},{28,20},{1,9},{5... | collective-permute-start | bytes 491528 | tf_op jit(solution)/shard_map/ppermute | solution.py:261
  16.0 8.3 %collective-permute-start.3 = (bf16[16,5120]{1,0:T(8,128)(2,1)S(1)}, bf16[16,5120]{1,0:T(8,128)(2,1)S(1)}, u32[]{:S(2)}, u32[]{:S(2)}) collective-permute-start(bf16[16,5120]{1,0:T(8,128)(2,1)S(1)} %get-tuple-element.43), channel_id=1, source_target_pairs={{0,12},{4,8},{8,4},{12,0},{16,28},{20,24},{24,20},{28,16},{1,13},{... | collective-permute-start | bytes 491528 | tf_op jit(solution)/shard_map/ppermute | solution.py:261
  26.6 10.4 %collective-permute-start.8 = (bf16[128,256]{1,0:T(8,128)(2,1)S(1)}, bf16[128,256]{1,0:T(8,128)(2,1)S(1)}, u32[]{:S(2)}, u32[]{:S(2)}) collective-permute-start(bf16[128,256]{1,0:T(8,128)(2,1)S(1)} %get-tuple-element.55), channel_id=1, source_target_pairs={{16,0},{20,4},{24,8},{28,12},{17,1},{21,5},{25,9},{29,13},{18,2},{... | collective-permute-start | bytes 196616 | tf_op jit(solution)/shard_map/ppermute | solution.py:349
  27.9 9.1 %collective-permute-start.9 = (bf16[128,256]{1,0:T(8,128)(2,1)S(1)}, bf16[128,256]{1,0:T(8,128)(2,1)S(1)}, u32[]{:S(2)}, u32[]{:S(2)}) collective-permute-start(bf16[128,256]{1,0:T(8,128)(2,1)S(1)} %get-tuple-element.56), channel_id=1, source_target_pairs={{20,0},{24,4},{28,8},{21,1},{25,5},{29,9},{22,2},{26,6},{30,10},{2... | collective-permute-start | bytes 196616 | tf_op jit(solution)/shard_map/ppermute | solution.py:349
  28.6 9.8 %collective-permute-start.10 = (bf16[128,256]{1,0:T(8,128)(2,1)S(1)}, bf16[128,256]{1,0:T(8,128)(2,1)S(1)}, u32[]{:S(2)}, u32[]{:S(2)}) collective-permute-start(bf16[128,256]{1,0:T(8,128)(2,1)S(1)} %get-tuple-element.57), channel_id=1, source_target_pairs={{12,0},{16,4},{20,8},{24,12},{28,16},{13,1},{17,5},{21,9},{25,13},... | collective-permute-start | bytes 196616 | tf_op jit(solution)/shard_map/ppermute | solution.py:349
  31.7 7.9 %collective-permute-start.11 = (bf16[128,256]{1,0:T(8,128)(2,1)S(1)}, bf16[128,256]{1,0:T(8,128)(2,1)S(1)}, u32[]{:S(2)}, u32[]{:S(2)}) collective-permute-start(bf16[128,256]{1,0:T(8,128)(2,1)S(1)} %get-tuple-element.58), channel_id=1, source_target_pairs={{8,0},{12,4},{16,8},{20,12},{24,16},{28,20},{9,1},{13,5},{17,9},{2... | collective-permute-start | bytes 196616 | tf_op jit(solution)/shard_map/ppermute | solution.py:349
  33.6 8.0 %collective-permute-start.12 = (bf16[128,256]{1,0:T(8,128)(2,1)S(1)}, bf16[128,256]{1,0:T(8,128)(2,1)S(1)}, u32[]{:S(2)}, u32[]{:S(2)}) collective-permute-start(bf16[128,256]{1,0:T(8,128)(2,1)S(1)} %get-tuple-element.59), channel_id=1, source_target_pairs={{4,0},{8,4},{12,8},{16,12},{20,16},{24,20},{28,24},{5,1},{9,5},{13... | collective-permute-start | bytes 196616 | tf_op jit(solution)/shard_map/ppermute | solution.py:349
